TPU v7x, 32 devices: a whole 2x2x4 slice. The times are simulated.
32 devices in a mesh: lat: 4 (over z), lon: 8 (over y, x, core).
Axes of the slice: x: 2, y: 2, z: 4, core: 2. Of those that a mesh axis runs over, the one named last changes fastest.
Arguments:
- satellite_blocks: bfloat16 [4096, 16, 128], P(('lat', 'lon')), may hold values from -6 to 6
- slot_source: int32 [32, 32, 4], P(('lat', 'lon')), may hold values from 0 to 127
- slot_weight: bfloat16 [32, 32, 4, 8, 128], P(('lat', 'lon')), may hold values from -2 to 2
- slot_target: int32 [32, 32, 4], P(('lat', 'lon')), may hold values from 0 to 63
- tile_counts: int32 [32, 32], P(('lat', 'lon')), may hold values from 0 to 4, as said below
- gate_input_weight: bfloat16 [128, 144], replicated, may hold values from -0.5 to 0.5
- gate_state_weight: bfloat16 [128, 288], replicated, may hold values from -0.375 to 0.375
- gate_bias: float32 [128], replicated, may hold values from -4 to 4
- hidden_init: bfloat16 [32, 128, 2048], P(None, 'lat', 'lon'), may hold values from -1 to 1
- cell_init: bfloat16 [32, 128, 2048], P(None, 'lat', 'lon'), may hold values from -6 to 6
Outputs:
- hidden_out: bfloat16 [32, 128, 2048], P(None, 'lat', 'lon')
- cell_out: bfloat16 [32, 128, 2048], P(None, 'lat', 'lon')
Inputs may be any that keep to these rules, and one draw needn't show every extreme that they name: slot_source[p, q, s] names one of the 128 blocks held by source device p. slot_target[q, p, s] is the cell block of tile q fed by slot s from device p. Only slots s < tile_counts[q, p] carry data from device p to tile q; at least one tile receives 4 blocks from every source device.
All inputs are finite; a program needn't handle non-finite values.
Results may differ from a plain program's by a relative error of at most 0.0069.
Values may be sent and summed in bfloat16 or wider, within the bound.
No kernel may reach another device: no remote copies, remote signals or barrier semaphores. Data moves between devices by JAX's collectives and lax.ppermute only.
A program may use at most 128 MiB of HBM per device.

v0:
```python
import functools

import jax
import jax.numpy as jnp
from jax import lax
from jax.experimental import pallas as pl
from jax.experimental.pallas import tpu as pltpu
from jax.sharding import PartitionSpec as P

STEPS = 3
PAD = 4
LANES = 128
STRIP = 3 * LANES
BF = jnp.bfloat16
F32 = jnp.float32


def lane_of(shape):
    return lax.broadcasted_iota(jnp.int32, shape, len(shape) - 1)


def whole(count):
    return [pl.BlockSpec(memory_space=pltpu.VMEM)] * count


def scalars(count):
    return [pl.BlockSpec(memory_space=pltpu.SMEM)] * count


def call(kernel, outs, ins, scalar_count, scratch, name, flops, args):
    nbytes = sum(a.size * a.dtype.itemsize for a in list(args) + list(outs))
    return pl.pallas_call(
        kernel,
        out_shape=tuple(outs),
        in_specs=scalars(scalar_count) + whole(ins),
        out_specs=tuple(whole(len(outs))),
        scratch_shapes=scratch,
        compiler_params=pltpu.CompilerParams(vmem_limit_bytes=40 * 2**20),
        cost_estimate=pl.CostEstimate(flops=flops, bytes_accessed=nbytes, transcendentals=0),
        name=name,
    )(*args)


def edge_tiles(row_of, row_count, channels):
    lane = lane_of((channels, LANES))
    tiles = [jnp.zeros((channels, LANES), BF) for _ in range(STRIP // LANES)]
    for y in range(row_count):
        row = row_of(y)
        both = jnp.where(lane < 64, row[:, :LANES], row[:, -LANES:])
        r = y + PAD
        place = r % 16
        turned = pltpu.roll(both, (8 * place + 4) % LANES, axis=1)
        tiles[r // 16] = jnp.where(lane // 8 == place, turned, tiles[r // 16])
    return tiles


def gather_kernel(source_ref, blocks_ref, weight_ref, out_ref):
    slots, band, width = weight_ref.shape
    channels = blocks_ref.shape[1]
    offset = lax.broadcasted_iota(jnp.int32, (band, width), 0) - band // 2
    spot = lane_of((band, width)) + offset
    inside = (spot >= 0) & (spot < width)

    def one(slot, carry):
        block = blocks_ref[source_ref[slot]]
        factor = jnp.where(inside, weight_ref[slot].astype(F32), 0.0)
        total = jnp.zeros((channels, width), F32)
        for k in range(band):
            moved = block if k == band // 2 else pltpu.roll(block, (band // 2 - k) % width, axis=1)
            total = total + factor[k : k + 1, :] * moved.astype(F32)
        out_ref[slot] = total.astype(BF)
        return carry

    lax.fori_loop(0, slots, one, 0, unroll=8)


def prepare_kernel(hidden_ref, cell_ref, rows_ref, edge_ref):
    units = hidden_ref.shape[0]
    row_count = hidden_ref.shape[1]
    rows_ref[:, :units, :] = jnp.swapaxes(hidden_ref[...], 0, 1)
    rows_ref[:, units:, :] = jnp.swapaxes(cell_ref[...], 0, 1)
    tiles = edge_tiles(lambda y: rows_ref[y], row_count, 2 * units)
    for t, tile in enumerate(tiles):
        edge_ref[:, t * LANES : (t + 1) * LANES] = tile


def strips_kernel(rows_ref, edge_ref, left_ref, right_ref, strip_ref, up_ref, down_ref):
    channels = edge_ref.shape[0]
    near = lane_of((channels, STRIP)) % 8 < 4
    left = jnp.where(near, left_ref[...], edge_ref[...])
    right = jnp.where(near, edge_ref[...], right_ref[...])
    strip_ref[:, :STRIP] = left
    strip_ref[:, STRIP:] = right
    rows = rows_ref.shape[0]
    up_ref[:3] = rows_ref[:3]
    up_ref[3, :, :LANES] = left[:, :LANES]
    up_ref[3, :, LANES:] = right[:, :LANES]
    down_ref[:3] = rows_ref[rows - 3 :]
    down_ref[3, :, :LANES] = left[:, 2 * LANES :]
    down_ref[3, :, LANES:] = right[:, 2 * LANES :]


def full_strip(strip, above, below, has_above, has_below):
    lane = lane_of(above[:, :LANES].shape)
    from_above = (lane >= 8) & (lane < 32)
    from_below = (lane >= 32) & (lane < 56)
    parts = []
    for side in range(2):
        base = side * STRIP
        theirs = above[:, side * LANES : (side + 1) * LANES] * has_above
        parts.append(jnp.where(from_above, theirs, strip[:, base : base + LANES]))
        parts.append(strip[:, base + LANES : base + 2 * LANES])
        theirs = below[:, side * LANES : (side + 1) * LANES] * has_below
        parts.append(jnp.where(from_below, theirs, strip[:, base + 2 * LANES : base + STRIP]))
    return jnp.concatenate(parts, axis=1)


def strip_taps(strip):
    width = strip.shape[1]
    taps = []
    for a in range(3):
        for e in range(3):
            shift = 8 * (a - 1) + e - 1
            taps.append(strip if shift == 0 else pltpu.roll(strip, -shift % width, axis=1))
    return jnp.concatenate(taps, axis=0)


def store_patches(strip, patch_ref, first, last):
    channels = strip.shape[0]
    near = lane_of((channels, LANES)) % 8 < 4
    for t in range(STRIP // LANES):
        left = strip[:, t * LANES : (t + 1) * LANES]
        right = strip[:, STRIP + t * LANES : STRIP + (t + 1) * LANES]
        mixed = jnp.where(near, left, right)
        for r in range(max(first, 16 * t), min(last, 16 * t + 16)):
            patch_ref[r] = pltpu.roll(mixed, -(8 * (r % 16) + 4) % LANES, axis=1)


def store_three(ref, r, row, patch):
    channels = row.shape[0]
    lane = lane_of((channels, LANES))
    head, tail = row[:, :LANES], row[:, LANES:]
    ref[r, :channels, :LANES] = pltpu.roll(jnp.where(lane == LANES - 1, patch, head), 1, axis=1)
    ref[r, :channels, LANES:] = pltpu.roll(jnp.where(lane == LANES - 1, head, tail), 1, axis=1)
    ref[r, channels : 2 * channels, :] = row
    ref[r, 2 * channels :, :LANES] = pltpu.roll(jnp.where(lane == 0, tail, head), LANES - 1, axis=1)
    ref[r, 2 * channels :, LANES:] = pltpu.roll(jnp.where(lane == 0, patch, tail), LANES - 1, axis=1)


def row_taps(ref, r):
    channels = ref.shape[1]
    return ref[pl.ds(r - 1, 3)].reshape(3 * channels, ref.shape[2])


def matmul(weights, taps):
    return jnp.dot(weights, taps, preferred_element_type=F32)


def state_kernel(
    flag_ref, rows_ref, strip_ref, above_ref, below_ref, weight_ref,
    gates_ref, strip_gates_ref, cell_strip_ref, three, patches,
):
    units = rows_ref.shape[1] // 2
    count = rows_ref.shape[0]
    has_above = flag_ref[0].astype(F32).astype(BF)
    has_below = flag_ref[1].astype(F32).astype(BF)
    strip = full_strip(strip_ref[...], above_ref[3], below_ref[3], has_above, has_below)
    cell_strip_ref[...] = strip[units:]
    strip = strip[:units]
    strip_gates_ref[...] = matmul(weight_ref[...], strip_taps(strip))
    store_patches(strip, patches, 1, count + 7)
    for i in range(3):
        store_three(three, 1 + i, above_ref[i, :units] * has_above, patches[1 + i])
        r = count + PAD + i
        store_three(three, r, below_ref[i, :units] * has_below, patches[r])

    def fill(y, carry):
        store_three(three, y + PAD, rows_ref[y, :units], patches[y + PAD])
        return carry

    lax.fori_loop(0, count, fill, 0, unroll=4)

    def one(i, carry):
        gates_ref[i] = matmul(weight_ref[...], row_taps(three, i + 2))
        return carry

    lax.fori_loop(0, count + 4, one, 0, unroll=4)


def update(gates, memory):
    units = memory.shape[0]
    ingate = 0.5 * jnp.tanh(gates[:units]) + 0.5
    forget = 0.5 * jnp.tanh(gates[units : 2 * units]) + 0.5
    outgate = 0.5 * jnp.tanh(gates[2 * units : 3 * units]) + 0.5
    memory = forget * memory + ingate * jnp.tanh(gates[3 * units :])
    return outgate * jnp.tanh(memory), memory


def window_kernel(
    flag_ref, gates_ref, strip_gates_ref, rows_ref, above_ref, below_ref, cell_strip_ref,
    forcing_ref, forcing_strip_ref, f_above_ref, f_below_ref, in_weight_ref, weight_ref, bias_ref,
    hidden_ref, cell_ref,
    f_three, f_patches, f_gates, first, second, patches, memory, h_rows, c_rows,
):
    units = rows_ref.shape[1] // 2
    count = rows_ref.shape[0]
    has_above = flag_ref[0].astype(F32)
    has_below = flag_ref[1].astype(F32)
    bf_above, bf_below = has_above.astype(BF), has_below.astype(BF)
    bias = jnp.broadcast_to(bias_ref[...], (bias_ref.shape[0], 2 * LANES))

    strip = full_strip(forcing_strip_ref[...], f_above_ref[3], f_below_ref[3], bf_above, bf_below)
    strip_forcing = matmul(in_weight_ref[...], strip_taps(strip)) + bias_ref[...]
    store_patches(strip, f_patches, 1, count + 7)
    for i in range(3):
        store_three(f_three, 1 + i, f_above_ref[i] * bf_above, f_patches[1 + i])
        r = count + PAD + i
        store_three(f_three, r, f_below_ref[i] * bf_below, f_patches[r])

    def fill(y, carry):
        store_three(f_three, y + PAD, forcing_ref[y], f_patches[y + PAD])
        return carry

    lax.fori_loop(0, count, fill, 0, unroll=4)

    row_of_lane = (lane_of((units, 2 * STRIP)) % STRIP) // 8
    keep = jnp.where(row_of_lane < PAD, has_above, 1.0)
    keep = jnp.where(row_of_lane >= PAD + count, has_below, keep)

    strip_memory = cell_strip_ref[...].astype(F32)
    strip_hidden, strip_memory = update(strip_gates_ref[...] + strip_forcing, strip_memory)
    strip_hidden = (strip_hidden * keep).astype(BF)
    store_patches(strip_hidden, patches, 2, count + 6)

    def scale_of(r):
        scale = jnp.where(r < PAD, has_above, 1.0)
        return jnp.where(r >= PAD + count, has_below, scale)

    def first_row(r, old):
        forcing_gates = matmul(in_weight_ref[...], row_taps(f_three, r)) + bias
        f_gates[r] = forcing_gates
        hidden, new = update(gates_ref[r - 2] + forcing_gates, old)
        memory[r] = new
        store_three(first, r, (hidden * scale_of(r)).astype(BF), patches[r])

    for i in range(2):
        first_row(2 + i, above_ref[1 + i, units:].astype(F32))
        first_row(count + PAD + i, below_ref[i, units:].astype(F32))

    def one(y, carry):
        first_row(y + PAD, rows_ref[y, units:].astype(F32))
        return carry

    lax.fori_loop(0, count, one, 0, unroll=2)

    strip_gates = matmul(weight_ref[...], strip_taps(strip_hidden)) + strip_forcing
    strip_hidden, strip_memory = update(strip_gates, strip_memory)
    strip_hidden = (strip_hidden * keep).astype(BF)
    store_patches(strip_hidden, patches, 3, count + 5)

    def two(i, carry):
        r = i + 3
        gates = f_gates[r] + matmul(weight_ref[...], row_taps(first, r))
        hidden, new = update(gates, memory[r])
        memory[r] = new
        store_three(second, r, (hidden * scale_of(r)).astype(BF), patches[r])
        return carry

    lax.fori_loop(0, count + 2, two, 0, unroll=2)

    def three(y, carry):
        r = y + PAD
        gates = f_gates[r] + matmul(weight_ref[...], row_taps(second, r))
        hidden, new = update(gates, memory[r])
        h_rows[y] = hidden.astype(BF)
        c_rows[y] = new.astype(BF)
        return carry

    lax.fori_loop(0, count, three, 0, unroll=2)
    hidden_ref[...] = jnp.swapaxes(h_rows[...], 0, 1)
    cell_ref[...] = jnp.swapaxes(c_rows[...], 0, 1)


def scatter_kernel(target_ref, count_ref, incoming_ref, rows_ref, edge_ref, total):
    slots, channels, width = incoming_ref.shape
    sources = count_ref.shape[0]
    cap = slots // sources
    row_count = rows_ref.shape[0]
    spare = 2 * row_count
    total[...] = jnp.zeros(total.shape, F32)

    def one(p, carry):
        live = count_ref[p]
        for s in range(cap):
            block = jnp.where(s < live, target_ref[p * cap + s], spare)
            total[block] = total[block] + incoming_ref[p * cap + s].astype(F32)
        return carry

    lax.fori_loop(0, sources, one, 0, unroll=4)
    for y in range(row_count):
        rows_ref[y, :, :width] = total[2 * y].astype(BF)
        rows_ref[y, :, width:] = total[2 * y + 1].astype(BF)
    tiles = edge_tiles(lambda y: rows_ref[y], row_count, channels)
    for t, tile in enumerate(tiles):
        edge_ref[:, t * LANES : (t + 1) * LANES] = tile


def around(count):
    return [(i, (i + 1) % count) for i in range(count)]


def back(count):
    return [((i + 1) % count, i) for i in range(count)]


def exchange_columns(edge):
    count = lax.axis_size("lon")
    from_left = lax.ppermute(edge, "lon", around(count))
    from_right = lax.ppermute(edge, "lon", back(count))
    return from_left, from_right


def exchange_rows(up, down):
    count = lax.axis_size("lat")
    from_above = lax.ppermute(down, "lat", around(count))
    from_below = lax.ppermute(up, "lat", back(count))
    return from_above, from_below


def strips_of(rows, edge, name):
    from_left, from_right = exchange_columns(edge)
    channels = edge.shape[0]
    ends = jax.ShapeDtypeStruct((4, channels, rows.shape[2]), BF)
    strip, up, down = call(
        strips_kernel,
        [jax.ShapeDtypeStruct((channels, 2 * STRIP), BF), ends, ends],
        4, 0, [], name, 1000, (rows, edge, from_left, from_right),
    )
    from_above, from_below = exchange_rows(up, down)
    return strip, from_above, from_below


def on_device(
    satellite_blocks,
    slot_source,
    slot_weight,
    slot_target,
    tile_counts,
    gate_input_weight,
    gate_state_weight,
    gate_bias,
    hidden_init,
    cell_init,
):
    _, tiles, cap, band, block = slot_weight.shape
    channels = satellite_blocks.shape[1]
    units, row_count, column_count = hidden_init.shape
    gates = gate_bias.shape[0]
    slots = tiles * cap
    half = jnp.where(jnp.arange(gates) < 3 * units, 0.5, 1.0)
    in_weight = gate_input_weight * half[:, None].astype(BF)
    state_weight = gate_state_weight * half[:, None].astype(BF)
    bias = (gate_bias * half)[:, None]
    lat = lax.axis_index("lat")
    flags = jnp.stack([lat > 0, lat < lax.axis_size("lat") - 1]).astype(jnp.int32)

    rows, edge = call(
        prepare_kernel,
        [
            jax.ShapeDtypeStruct((row_count, 2 * units, column_count), BF),
            jax.ShapeDtypeStruct((2 * units, STRIP), BF),
        ],
        2, 0, [], "prepare", 1000, (hidden_init, cell_init),
    )
    (outgoing,) = call(
        gather_kernel,
        [jax.ShapeDtypeStruct((slots, channels, block), BF)],
        2, 1, [], "gather_band", 2 * slots * channels * block * band,
        (slot_source.reshape(slots), satellite_blocks, slot_weight.reshape(slots, band, block)),
    )
    incoming = lax.all_to_all(
        outgoing.reshape(tiles, cap, channels, block), ("lat", "lon"), split_axis=0, concat_axis=0, tiled=True
    ).reshape(slots, channels, block)

    strip, above, below = strips_of(rows, edge, "state_strips")
    extended = row_count + 4
    state_gates, strip_gates, cell_strip = call(
        state_kernel,
        [
            jax.ShapeDtypeStruct((extended, gates, column_count), F32),
            jax.ShapeDtypeStruct((gates, 2 * STRIP), F32),
            jax.ShapeDtypeStruct((units, 2 * STRIP), BF),
        ],
        5, 1,
        [
            pltpu.VMEM((row_count + 8, 3 * units, column_count), BF),
            pltpu.VMEM((row_count + 8, units, LANES), BF),
        ],
        "state_gates", 2 * gates * 9 * units * extended * column_count,
        (flags, rows, strip, above, below, state_weight),
    )

    forcing, forcing_edge = call(
        scatter_kernel,
        [
            jax.ShapeDtypeStruct((row_count, channels, column_count), BF),
            jax.ShapeDtypeStruct((channels, STRIP), BF),
        ],
        1, 2,
        [pltpu.VMEM((2 * row_count + 1, channels, block), F32)],
        "scatter_add", slots * channels * block,
        (slot_target.reshape(slots), tile_counts.reshape(tiles), incoming),
    )
    forcing_strip, f_above, f_below = strips_of(forcing, forcing_edge, "forcing_strips")
    out = jax.ShapeDtypeStruct((units, row_count, column_count), BF)
    padded = row_count + 8
    return call(
        window_kernel,
        [out, out],
        13, 1,
        [
            pltpu.VMEM((padded, 3 * channels, column_count), BF),
            pltpu.VMEM((padded, channels, LANES), BF),
            pltpu.VMEM((padded, gates, column_count), F32),
            pltpu.VMEM((padded, 3 * units, column_count), BF),
            pltpu.VMEM((padded, 3 * units, column_count), BF),
            pltpu.VMEM((padded, units, LANES), BF),
            pltpu.VMEM((padded, units, column_count), F32),
            pltpu.VMEM((row_count, units, column_count), BF),
            pltpu.VMEM((row_count, units, column_count), BF),
        ],
        "window", 2 * gates * 9 * (channels + 2 * units) * row_count * column_count,
        (flags, state_gates, strip_gates, rows, above, below, cell_strip,
         forcing, forcing_strip, f_above, f_below, in_weight, state_weight, bias),
    )


def solution(mesh):
    placed = (
        P(("lat", "lon"), None, None),
        P(("lat", "lon"), None, None),
        P(("lat", "lon"), None, None, None, None),
        P(("lat", "lon"), None, None),
        P(("lat", "lon"), None),
        P(),
        P(),
        P(),
        P(None, "lat", "lon"),
        P(None, "lat", "lon"),
    )
    return jax.shard_map(
        on_device,
        mesh=mesh,
        in_specs=placed,
        out_specs=(P(None, "lat", "lon"), P(None, "lat", "lon")),
        check_vma=False,
    )
```

profile of v0, /device:TPU:0, one launch (start us, length us, event | category | flops | bytes accessed | tf_op | source)
XLA Modules:
  0.0 66.1 jit_solution(5241901960814527278)
XLA Ops:
  0.6 0.0 copy-start.6
  0.6 0.0 copy-start.5
  0.7 0.0 copy-start.4
  0.7 0.8 %copy.24 = s32[1,32,4]{2,1,0:T(8,128)S(1)} copy(s32[1,32,4]{1,2,0:T(4,128)} %param.11) | data formatting | bytes 1024 | tf_op args[1]
  1.4 0.1 reshape.31.source_ref
  1.5 0.0 copy-start
  1.6 1.0 %copy-done = bf16[128,16,128]{2,1,0:T(8,128)(2,1)S(1)} copy-done((bf16[128,16,128]{2,1,0:T(8,128)(2,1)S(1)}, bf16[128,16,128]{2,1,0:T(8,128)(2,1)}, u32[]{:S(2)}) %copy-start) | copy-done | bytes 524312
  2.6 0.0 copy-start.3
  2.6 0.9 %copy-done.3 = bf16[1,32,4,8,128]{4,3,2,1,0:T(8,128)(2,1)S(1)} copy-done((bf16[1,32,4,8,128]{4,3,2,1,0:T(8,128)(2,1)S(1)}, bf16[1,32,4,8,128]{4,3,2,1,0:T(8,128)(2,1)}, u32[]{:S(2)}) %copy-start.3) | copy-done | bytes 262168
  3.5 3.5 %gather_band.1 = bf16[128,16,128]{2,1,0:T(8,128)(2,1)} custom-call(s32[128]{0:T(128)S(1)} %reshape.31.source_ref, bf16[128,16,128]{2,1,0:T(8,128)(2,1)S(1)} %copy-done, bf16[128,8,128]{2,1,0:T(8,128)(2,1)S(1)} %bitcast.9), custom_call_target="tpu_custom_call" | custom-call | flops 4194304 | bytes 1311232 | tf_op jit(solution)/shard_map/gather_band/pallas_call | solution.py:32
  7.1 7.3 %all-to-all-start = ((bf16[32,4,16,128]{3,2,1,0:T(8,128)(2,1)}), bf16[32,4,16,128]{3,2,1,0:T(8,128)(2,1)S(1)}, u32[]{:S(2)}, u32[]{:S(2)}) async-start(bf16[32,4,16,128]{3,2,1,0:T(8,128)(2,1)} %bitcast.4), calls=%async_computation | async-start | bytes 1048576 | tf_op jit(solution)/shard_map/all_to_all | solution.py:381
  14.4 0.0 copy-start.1
  14.4 1.0 %copy-done.1 = bf16[32,32,256]{2,1,0:T(8,128)(2,1)S(1)} copy-done((bf16[32,32,256]{2,1,0:T(8,128)(2,1)S(1)}, bf16[32,32,256]{2,1,0:T(8,128)(2,1)}, u32[]{:S(2)}) %copy-start.1) | copy-done | bytes 524312
  15.4 0.0 copy-start.2
  15.4 1.0 %copy-done.2 = bf16[32,32,256]{2,1,0:T(8,128)(2,1)S(1)} copy-done((bf16[32,32,256]{2,1,0:T(8,128)(2,1)S(1)}, bf16[32,32,256]{2,1,0:T(8,128)(2,1)}, u32[]{:S(2)}) %copy-start.2) | copy-done | bytes 524312
  16.5 0.4 prepare.1
  16.9 2.5 %collective-permute-start.1 = (bf16[64,384]{1,0:T(8,128)(2,1)S(1)}, bf16[64,384]{1,0:T(8,128)(2,1)S(1)}, u32[]{:S(2)}, u32[]{:S(2)}) collective-permute-start(bf16[64,384]{1,0:T(8,128)(2,1)S(1)} %get-tuple-element.16.edge_ref), channel_id=1, source_target_pairs={{1,0},{2,1},{3,2},{4,3},{5,4},{6,5},{7,6},{0,7},{9,8},{10,9},{11,1... | collective-permute-start | bytes 147464 | tf_op jit(solution)/shard_map/ppermute | solution.py:319
  19.4 0.0 collective-permute-start
  19.4 0.9 %copy.25 = bf16[128,144]{1,0:T(8,128)(2,1)S(1)} copy(bf16[128,144]{0,1:T(8,128)(2,1)} %param.15) | data formatting | bytes 73728 | tf_op args[5]
  20.3 1.0 %copy.22 = bf16[128,288]{1,0:T(8,128)(2,1)S(1)} copy(bf16[128,288]{0,1:T(8,128)(2,1)} %param.16) | data formatting | bytes 147456 | tf_op args[6]
  21.3 0.1 broadcast_multiply_fusion.weight_ref
  21.4 0.1 broadcast_multiply_fusion.1.in_weight_ref
  21.5 0.1 collective-permute-done.1.right_ref
  21.6 2.4 %collective-permute-done.left_ref = bf16[64,384]{1,0:T(8,128)(2,1)S(1)} collective-permute-done((bf16[64,384]{1,0:T(8,128)(2,1)S(1)}, bf16[64,384]{1,0:T(8,128)(2,1)S(1)}, u32[]{:S(2)}, u32[]{:S(2)}) %collective-permute-start) | collective-permute-done | bytes 49184 | tf_op jit(solution)/shard_map/ppermute | solution.py:318
  24.0 1.9 %collective-permute-start.2 = (bf16[4,64,256]{2,1,0:T(8,128)(2,1)S(1)}, bf16[4,64,256]{2,1,0:T(8,128)(2,1)S(1)}, u32[]{:S(2)}, u32[]{:S(2)}) collective-permute-start(bf16[4,64,256]{2,1,0:T(8,128)(2,1)S(1)} %get-tuple-element.18), channel_id=1, source_target_pairs={{0,8},{8,16},{16,24},{24,0},{1,9},{9,17},{17,25},{25,1},{2,10},{10... | collective-permute-start | bytes 393224 | tf_op jit(solution)/shard_map/ppermute | solution.py:325
  25.9 2.0 %collective-permute-start.3 = (bf16[4,64,256]{2,1,0:T(8,128)(2,1)S(1)}, bf16[4,64,256]{2,1,0:T(8,128)(2,1)S(1)}, u32[]{:S(2)}, u32[]{:S(2)}) collective-permute-start(bf16[4,64,256]{2,1,0:T(8,128)(2,1)S(1)} %get-tuple-element.19), channel_id=1, source_target_pairs={{8,0},{16,8},{24,16},{0,24},{9,1},{17,9},{25,17},{1,25},{10,2},{18... | collective-permute-start | bytes 393224 | tf_op jit(solution)/shard_map/ppermute | solution.py:326
  27.9 0.0 copy-done.6
  27.9 0.0 copy-done.5
  27.9 0.1 copy.23
  28.0 0.1 reshape.29.target_ref
  28.1 4.6 %all-to-all-done = bf16[32,4,16,128]{3,2,1,0:T(8,128)(2,1)S(1)} async-done(((bf16[32,4,16,128]{3,2,1,0:T(8,128)(2,1)}), bf16[32,4,16,128]{3,2,1,0:T(8,128)(2,1)S(1)}, u32[]{:S(2)}, u32[]{:S(2)}) %all-to-all-start) | async-done | bytes 524320 | tf_op jit(solution)/shard_map/all_to_all | solution.py:381
  32.8 0.0 copy-done.4
  32.8 1.3 %scatter_add.1 = (bf16[32,16,256]{2,1,0:T(8,128)(2,1)S(1)}, bf16[16,384]{1,0:T(8,128)(2,1)S(1)}) custom-call(s32[128]{0:T(128)S(1)} %reshape.29.target_ref, s32[32]{0:T(128)S(1)} %bitcast.10, bf16[128,16,128]{2,1,0:T(8,128)(2,1)S(1)} %bitcast.8), custom_call_target="tpu_custom_call" | custom-call | flops 262144 | bytes 799360 | tf_op jit(solution)/shard_map/scatter_add/pallas_call | solution.py:32
  34.1 1.5 %collective-permute-start.5 = (bf16[16,384]{1,0:T(8,128)(2,1)S(1)}, bf16[16,384]{1,0:T(8,128)(2,1)S(1)}, u32[]{:S(2)}, u32[]{:S(2)}) collective-permute-start(bf16[16,384]{1,0:T(8,128)(2,1)S(1)} %get-tuple-element.24.edge_ref), channel_id=1, source_target_pairs={{1,0},{2,1},{3,2},{4,3},{5,4},{6,5},{7,6},{0,7},{9,8},{10,9},{11,1... | collective-permute-start | bytes 36872 | tf_op jit(solution)/shard_map/ppermute | solution.py:319
  35.6 0.0 collective-permute-start.4
  35.6 0.1 add_convert_fusion.flag_ref
  35.7 0.1 copy.27.bias_ref
  35.8 1.2 %collective-permute-done.5.right_ref = bf16[16,384]{1,0:T(8,128)(2,1)S(1)} collective-permute-done((bf16[16,384]{1,0:T(8,128)(2,1)S(1)}, bf16[16,384]{1,0:T(8,128)(2,1)S(1)}, u32[]{:S(2)}, u32[]{:S(2)}) %collective-permute-start.5) | collective-permute-done | bytes 12320 | tf_op jit(solution)/shard_map/ppermute | solution.py:319
  37.0 2.6 %collective-permute-done.4.left_ref = bf16[16,384]{1,0:T(8,128)(2,1)S(1)} collective-permute-done((bf16[16,384]{1,0:T(8,128)(2,1)S(1)}, bf16[16,384]{1,0:T(8,128)(2,1)S(1)}, u32[]{:S(2)}, u32[]{:S(2)}) %collective-permute-start.4) | collective-permute-done | bytes 12320 | tf_op jit(solution)/shard_map/ppermute | solution.py:318
  39.6 0.1 collective-permute-start.6
  39.7 3.8 %collective-permute-start.7 = (bf16[4,16,256]{2,1,0:T(8,128)(2,1)S(1)}, bf16[4,16,256]{2,1,0:T(8,128)(2,1)S(1)}, u32[]{:S(2)}, u32[]{:S(2)}) collective-permute-start(bf16[4,16,256]{2,1,0:T(8,128)(2,1)S(1)} %get-tuple-element.27), channel_id=1, source_target_pairs={{8,0},{16,8},{24,16},{0,24},{9,1},{17,9},{25,17},{1,25},{10,2},{18... | collective-permute-start | bytes 98312 | tf_op jit(solution)/shard_map/ppermute | solution.py:326
  43.5 0.0 collective-permute-done.2.above_ref
  43.5 0.0 collective-permute-done.3.below_ref
  43.5 4.5 %state_gates.1 = (f32[36,128,256]{2,1,0:T(8,128)S(1)}, f32[128,768]{1,0:T(8,128)S(1)}, bf16[32,768]{1,0:T(8,128)(2,1)S(1)}) custom-call(s32[2]{0:T(128)S(1)} %add_convert_fusion.flag_ref, bf16[32,64,256]{2,1,0:T(8,128)(2,1)S(1)} %get-tuple-element.15.rows_ref, bf16[64,768]{1,0:T(8,128)(2,1)S(1)} %get-tuple-element.17.strip_ref, ...), custom_call_target="tpu_custom_call" | custom-call | flops 679477248 | bytes 6643720 | tf_op jit(solution)/shard_map/state_gates/pallas_call | solution.py:32
  48.0 0.0 collective-permute-done.6.f_above_ref
  48.0 0.0 collective-permute-done.7.f_below_ref
  48.0 18.1 %window.1 = (bf16[32,32,256]{2,1,0:T(8,128)(2,1)}, bf16[32,32,256]{2,1,0:T(8,128)(2,1)}) custom-call(s32[2]{0:T(128)S(1)} %add_convert_fusion.flag_ref, f32[36,128,256]{2,1,0:T(8,128)S(1)} %get-tuple-element.20.gates_ref, f32[128,768]{1,0:T(8,128)S(1)} %get-tuple-element.21.strip_gates_ref, bf16[32,64,256]{2,1,0:T(8,128)(2,1)S(1)} %get-tuple-element.15.rows_ref, ...), custom_call_target="tpu_custom_call" | custom-call | flops 1509949440 | bytes 7983624 | tf_op jit(solution)/shard_map/window/pallas_call | solution.py:32
  (4 shorter events, 0.1 us)
Async XLA Ops:
  0.6 27.3 %copy-start.6 = (f32[128]{0:T(128)S(1)}, f32[128]{0:T(128)}, u32[]{:S(2)}) copy-start(f32[128]{0:T(128)} %param.17) | copy-start | bytes 1540
  0.6 27.3 %copy-start.5 = (s32[1,32,4]{1,2,0:T(4,128)S(1)}, s32[1,32,4]{1,2,0:T(4,128)}, u32[]{:S(2)}) copy-start(s32[1,32,4]{1,2,0:T(4,128)} %param.13) | copy-start | bytes 1540
  0.7 32.1 %copy-start.4 = (s32[1,32]{1,0:T(1,128)S(1)}, s32[1,32]{1,0:T(1,128)}, u32[]{:S(2)}) copy-start(s32[1,32]{1,0:T(1,128)} %param.14) | copy-start | bytes 388
  1.5 1.0 %copy-start = (bf16[128,16,128]{2,1,0:T(8,128)(2,1)S(1)}, bf16[128,16,128]{2,1,0:T(8,128)(2,1)}, u32[]{:S(2)}) copy-start(bf16[128,16,128]{2,1,0:T(8,128)(2,1)} %blocks_ref.1) | copy-start | bytes 1572868
  2.6 0.9 %copy-start.3 = (bf16[1,32,4,8,128]{4,3,2,1,0:T(8,128)(2,1)S(1)}, bf16[1,32,4,8,128]{4,3,2,1,0:T(8,128)(2,1)}, u32[]{:S(2)}) copy-start(bf16[1,32,4,8,128]{4,3,2,1,0:T(8,128)(2,1)} %param.12) | copy-start | bytes 786436
  7.1 25.7 %all-to-all-start = ((bf16[32,4,16,128]{3,2,1,0:T(8,128)(2,1)}), bf16[32,4,16,128]{3,2,1,0:T(8,128)(2,1)S(1)}, u32[]{:S(2)}, u32[]{:S(2)}) async-start(bf16[32,4,16,128]{3,2,1,0:T(8,128)(2,1)} %bitcast.4), calls=%async_computation | async-start | bytes 1048576 | tf_op jit(solution)/shard_map/all_to_all | solution.py:381
  14.4 1.0 %copy-start.1 = (bf16[32,32,256]{2,1,0:T(8,128)(2,1)S(1)}, bf16[32,32,256]{2,1,0:T(8,128)(2,1)}, u32[]{:S(2)}) copy-start(bf16[32,32,256]{2,1,0:T(8,128)(2,1)} %hidden_ref.1) | copy-start | bytes 1572868
  15.4 1.0 %copy-start.2 = (bf16[32,32,256]{2,1,0:T(8,128)(2,1)S(1)}, bf16[32,32,256]{2,1,0:T(8,128)(2,1)}, u32[]{:S(2)}) copy-start(bf16[32,32,256]{2,1,0:T(8,128)(2,1)} %cell_ref.1) | copy-start | bytes 1572868
  16.9 4.6 %collective-permute-start.1 = (bf16[64,384]{1,0:T(8,128)(2,1)S(1)}, bf16[64,384]{1,0:T(8,128)(2,1)S(1)}, u32[]{:S(2)}, u32[]{:S(2)}) collective-permute-start(bf16[64,384]{1,0:T(8,128)(2,1)S(1)} %get-tuple-element.16.edge_ref), channel_id=1, source_target_pairs={{1,0},{2,1},{3,2},{4,3},{5,4},{6,5},{7,6},{0,7},{9,8},{10,9},{11,1... | collective-permute-start | bytes 147464 | tf_op jit(solution)/shard_map/ppermute | solution.py:319
  19.4 4.6 %collective-permute-start = (bf16[64,384]{1,0:T(8,128)(2,1)S(1)}, bf16[64,384]{1,0:T(8,128)(2,1)S(1)}, u32[]{:S(2)}, u32[]{:S(2)}) collective-permute-start(bf16[64,384]{1,0:T(8,128)(2,1)S(1)} %get-tuple-element.16.edge_ref), channel_id=1, source_target_pairs={{0,1},{1,2},{2,3},{3,4},{4,5},{5,6},{6,7},{7,0},{8,9},{9,10},{10,1... | collective-permute-start | bytes 147464 | tf_op jit(solution)/shard_map/ppermute | solution.py:318
  24.0 19.5 %collective-permute-start.2 = (bf16[4,64,256]{2,1,0:T(8,128)(2,1)S(1)}, bf16[4,64,256]{2,1,0:T(8,128)(2,1)S(1)}, u32[]{:S(2)}, u32[]{:S(2)}) collective-permute-start(bf16[4,64,256]{2,1,0:T(8,128)(2,1)S(1)} %get-tuple-element.18), channel_id=1, source_target_pairs={{0,8},{8,16},{16,24},{24,0},{1,9},{9,17},{17,25},{25,1},{2,10},{10... | collective-permute-start | bytes 393224 | tf_op jit(solution)/shard_map/ppermute | solution.py:325
  25.9 17.6 %collective-permute-start.3 = (bf16[4,64,256]{2,1,0:T(8,128)(2,1)S(1)}, bf16[4,64,256]{2,1,0:T(8,128)(2,1)S(1)}, u32[]{:S(2)}, u32[]{:S(2)}) collective-permute-start(bf16[4,64,256]{2,1,0:T(8,128)(2,1)S(1)} %get-tuple-element.19), channel_id=1, source_target_pairs={{8,0},{16,8},{24,16},{0,24},{9,1},{17,9},{25,17},{1,25},{10,2},{18... | collective-permute-start | bytes 393224 | tf_op jit(solution)/shard_map/ppermute | solution.py:326
  34.1 2.9 %collective-permute-start.5 = (bf16[16,384]{1,0:T(8,128)(2,1)S(1)}, bf16[16,384]{1,0:T(8,128)(2,1)S(1)}, u32[]{:S(2)}, u32[]{:S(2)}) collective-permute-start(bf16[16,384]{1,0:T(8,128)(2,1)S(1)} %get-tuple-element.24.edge_ref), channel_id=1, source_target_pairs={{1,0},{2,1},{3,2},{4,3},{5,4},{6,5},{7,6},{0,7},{9,8},{10,9},{11,1... | collective-permute-start | bytes 36872 | tf_op jit(solution)/shard_map/ppermute | solution.py:319
  35.6 4.0 %collective-permute-start.4 = (bf16[16,384]{1,0:T(8,128)(2,1)S(1)}, bf16[16,384]{1,0:T(8,128)(2,1)S(1)}, u32[]{:S(2)}, u32[]{:S(2)}) collective-permute-start(bf16[16,384]{1,0:T(8,128)(2,1)S(1)} %get-tuple-element.24.edge_ref), channel_id=1, source_target_pairs={{0,1},{1,2},{2,3},{3,4},{4,5},{5,6},{6,7},{7,0},{8,9},{9,10},{10,1... | collective-permute-start | bytes 36872 | tf_op jit(solution)/shard_map/ppermute | solution.py:318
  39.6 8.4 %collective-permute-start.6 = (bf16[4,16,256]{2,1,0:T(8,128)(2,1)S(1)}, bf16[4,16,256]{2,1,0:T(8,128)(2,1)S(1)}, u32[]{:S(2)}, u32[]{:S(2)}) collective-permute-start(bf16[4,16,256]{2,1,0:T(8,128)(2,1)S(1)} %get-tuple-element.26), channel_id=1, source_target_pairs={{0,8},{8,16},{16,24},{24,0},{1,9},{9,17},{17,25},{25,1},{2,10},{10... | collective-permute-start | bytes 98312 | tf_op jit(solution)/shard_map/ppermute | solution.py:325
  39.7 8.3 %collective-permute-start.7 = (bf16[4,16,256]{2,1,0:T(8,128)(2,1)S(1)}, bf16[4,16,256]{2,1,0:T(8,128)(2,1)S(1)}, u32[]{:S(2)}, u32[]{:S(2)}) collective-permute-start(bf16[4,16,256]{2,1,0:T(8,128)(2,1)S(1)} %get-tuple-element.27), channel_id=1, source_target_pairs={{8,0},{16,8},{24,16},{0,24},{9,1},{17,9},{25,17},{1,25},{10,2},{18... | collective-permute-start | bytes 98312 | tf_op jit(solution)/shard_map/ppermute | solution.py:326
where the time goes:
time: 66.6 us; the launch traced here: 66.1 us
  Pallas kernels  27.9 us (42%)
  starting transfers between devices  19 us (29%)
  waiting for transfers between devices  11 us (17%)
  local copies, waits for them, and re-layouts  7.13 us (11%)
  between operations  0.79 us (1%)
    pallas_call x7, Pallas kernels, call(): pl.pallas_call(kernel, out_shape=tuple(outs), in_specs=scalars(scalar_cou...  27.9 us
    all_to_all x1, starting transfers between devices, on_device(): lax.all_to_all(outgoing.reshape(tiles, cap, channels, block), ('lat', 'lo...  7.3 us
    unnamed x18, local copies, waits for them, and re-layouts  6.81 us
    ppermute x2, starting transfers between devices, exchange_rows(): from_below = lax.ppermute(up, 'lat', back(count))  5.82 us
    ppermute x2, waiting for transfers between devices, exchange_columns(): from_left = lax.ppermute(edge, 'lon', around(count))  5.06 us
    all_to_all x1, waiting for transfers between devices, on_device(): lax.all_to_all(outgoing.reshape(tiles, cap, channels, block), ('lat', 'lo...  4.65 us
    ppermute x2, starting transfers between devices, exchange_columns(): from_right = lax.ppermute(edge, 'lon', back(count))  3.94 us
    ppermute x2, starting transfers between devices, exchange_rows(): from_above = lax.ppermute(down, 'lat', around(count))  1.93 us
  transfers between devices with their start and end apart: 9, of which 5 were waited for; matrix products, arithmetic and copies ran while one was open for 4% of the time, Pallas kernels for 10%

commit v1 on v0

--- a/solution.py
+++ b/solution.py
@@ -11,6 +11,7 @@
 PAD = 4
 LANES = 128
 STRIP = 3 * LANES
+BATCH = 2
 BF = jnp.bfloat16
 F32 = jnp.float32
 
@@ -61,7 +62,7 @@
     spot = lane_of((band, width)) + offset
     inside = (spot >= 0) & (spot < width)
 
-    def one(slot, carry):
+    for slot in range(slots):
         block = blocks_ref[source_ref[slot]]
         factor = jnp.where(inside, weight_ref[slot].astype(F32), 0.0)
         total = jnp.zeros((channels, width), F32)
@@ -69,9 +70,6 @@
             moved = block if k == band // 2 else pltpu.roll(block, (band // 2 - k) % width, axis=1)
             total = total + factor[k : k + 1, :] * moved.astype(F32)
         out_ref[slot] = total.astype(BF)
-        return carry
-
-    lax.fori_loop(0, slots, one, 0, unroll=8)
 
 
 def prepare_kernel(hidden_ref, cell_ref, rows_ref, edge_ref):
@@ -174,17 +172,10 @@
         r = count + PAD + i
         store_three(three, r, below_ref[i, :units] * has_below, patches[r])
 
-    def fill(y, carry):
+    for y in range(count):
         store_three(three, y + PAD, rows_ref[y, :units], patches[y + PAD])
-        return carry
-
-    lax.fori_loop(0, count, fill, 0, unroll=4)
-
-    def one(i, carry):
+    for i in range(count + 4):
         gates_ref[i] = matmul(weight_ref[...], row_taps(three, i + 2))
-        return carry
-
-    lax.fori_loop(0, count + 4, one, 0, unroll=4)
 
 
 def update(gates, memory):
@@ -217,11 +208,8 @@
         r = count + PAD + i
         store_three(f_three, r, f_below_ref[i] * bf_below, f_patches[r])
 
-    def fill(y, carry):
+    for y in range(count):
         store_three(f_three, y + PAD, forcing_ref[y], f_patches[y + PAD])
-        return carry
-
-    lax.fori_loop(0, count, fill, 0, unroll=4)
 
     row_of_lane = (lane_of((units, 2 * STRIP)) % STRIP) // 8
     keep = jnp.where(row_of_lane < PAD, has_above, 1.0)
@@ -232,51 +220,56 @@
     strip_hidden = (strip_hidden * keep).astype(BF)
     store_patches(strip_hidden, patches, 2, count + 6)
 
-    def scale_of(r):
-        scale = jnp.where(r < PAD, has_above, 1.0)
-        return jnp.where(r >= PAD + count, has_below, scale)
-
-    def first_row(r, old):
-        forcing_gates = matmul(in_weight_ref[...], row_taps(f_three, r)) + bias
-        f_gates[r] = forcing_gates
-        hidden, new = update(gates_ref[r - 2] + forcing_gates, old)
-        memory[r] = new
-        store_three(first, r, (hidden * scale_of(r)).astype(BF), patches[r])
-
-    for i in range(2):
-        first_row(2 + i, above_ref[1 + i, units:].astype(F32))
-        first_row(count + PAD + i, below_ref[i, units:].astype(F32))
-
-    def one(y, carry):
-        first_row(y + PAD, rows_ref[y, units:].astype(F32))
-        return carry
-
-    lax.fori_loop(0, count, one, 0, unroll=2)
+    def kept(hidden, r):
+        if r < PAD:
+            hidden = hidden * has_above
+        elif r >= PAD + count:
+            hidden = hidden * has_below
+        return hidden.astype(BF)
+
+    def run(first_r, total, batch, body):
+        for start in range(first_r, first_r + total, batch):
+            body(range(start, min(start + batch, first_r + total)))
+
+    def first_rows(group, olds):
+        sums = [matmul(in_weight_ref[...], row_taps(f_three, r)) + bias for r in group]
+        states = [update(gates_ref[r - 2] + s, old) for r, s, old in zip(group, sums, olds)]
+        marks = [patches[r] for r in group]
+        for r, s, (hidden, new), mark in zip(group, sums, states, marks):
+            f_gates[r] = s
+            memory[r] = new
+            store_three(first, r, kept(hidden, r), mark)
+
+    first_rows(
+        [2, 3, count + PAD, count + PAD + 1],
+        [ref[i, units:].astype(F32) for ref, i in ((above_ref, 1), (above_ref, 2), (below_ref, 0), (below_ref, 1))],
+    )
+    run(PAD, count, BATCH, lambda group: first_rows(group, [rows_ref[r - PAD, units:].astype(F32) for r in group]))
 
     strip_gates = matmul(weight_ref[...], strip_taps(strip_hidden)) + strip_forcing
     strip_hidden, strip_memory = update(strip_gates, strip_memory)
     strip_hidden = (strip_hidden * keep).astype(BF)
     store_patches(strip_hidden, patches, 3, count + 5)
 
-    def two(i, carry):
-        r = i + 3
-        gates = f_gates[r] + matmul(weight_ref[...], row_taps(first, r))
-        hidden, new = update(gates, memory[r])
-        memory[r] = new
-        store_three(second, r, (hidden * scale_of(r)).astype(BF), patches[r])
-        return carry
-
-    lax.fori_loop(0, count + 2, two, 0, unroll=2)
-
-    def three(y, carry):
-        r = y + PAD
-        gates = f_gates[r] + matmul(weight_ref[...], row_taps(second, r))
-        hidden, new = update(gates, memory[r])
-        h_rows[y] = hidden.astype(BF)
-        c_rows[y] = new.astype(BF)
-        return carry
-
-    lax.fori_loop(0, count, three, 0, unroll=2)
+    def later(source, group):
+        sums = [f_gates[r] + matmul(weight_ref[...], row_taps(source, r)) for r in group]
+        return [update(s, memory[r]) for r, s in zip(group, sums)]
+
+    def second_rows(group):
+        states = later(first, group)
+        marks = [patches[r] for r in group]
+        for r, (hidden, new), mark in zip(group, states, marks):
+            memory[r] = new
+            store_three(second, r, kept(hidden, r), mark)
+
+    run(PAD - 1, count + 2, BATCH, second_rows)
+
+    def third_rows(group):
+        for r, (hidden, new) in zip(group, later(second, group)):
+            h_rows[r - PAD] = hidden.astype(BF)
+            c_rows[r - PAD] = new.astype(BF)
+
+    run(PAD, count, BATCH, third_rows)
     hidden_ref[...] = jnp.swapaxes(h_rows[...], 0, 1)
     cell_ref[...] = jnp.swapaxes(c_rows[...], 0, 1)
 
@@ -289,14 +282,11 @@
     spare = 2 * row_count
     total[...] = jnp.zeros(total.shape, F32)
 
-    def one(p, carry):
+    for p in range(sources):
         live = count_ref[p]
         for s in range(cap):
             block = jnp.where(s < live, target_ref[p * cap + s], spare)
             total[block] = total[block] + incoming_ref[p * cap + s].astype(F32)
-        return carry
-
-    lax.fori_loop(0, sources, one, 0, unroll=4)
     for y in range(row_count):
         rows_ref[y, :, :width] = total[2 * y].astype(BF)
         rows_ref[y, :, width:] = total[2 * y + 1].astype(BF)

time: 66.6 us -> 52.8 us (0.79)
  Pallas kernels: 27.9 us -> 14.1 us
    pallas_call x7, Pallas kernels: 27.9 us -> 14.1 us  [call(): pl.pallas_call(kernel, out_shape=tuple(outs), in_specs=scalars(scalar_cou...]
  transfers between devices with their start and end apart: 9 -> 9, of which waited for: 5 -> 5; matrix products, arithmetic and copies ran while one was open for 4% -> 5% of each run, Pallas kernels for 10% -> 9%
where the time goes in v1:
time: 52.8 us; the launch traced here: 52.3 us
  starting transfers between devices  19 us (36%)
  Pallas kernels  14.1 us (27%)
  waiting for transfers between devices  11 us (21%)
  local copies, waits for them, and re-layouts  7.13 us (14%)
  between operations  0.78 us (1%)
    pallas_call x7, Pallas kernels, call(): pl.pallas_call(kernel, out_shape=tuple(outs), in_specs=scalars(scalar_cou...  14.1 us
    all_to_all x1, starting transfers between devices, on_device(): lax.all_to_all(outgoing.reshape(tiles, cap, channels, block), ('lat', 'lo...  7.29 us
    unnamed x18, local copies, waits for them, and re-layouts  6.81 us
    ppermute x2, starting transfers between devices, exchange_rows(): from_below = lax.ppermute(up, 'lat', back(count))  5.82 us
    ppermute x2, waiting for transfers between devices, exchange_columns(): from_left = lax.ppermute(edge, 'lon', around(count))  5.06 us
    all_to_all x1, waiting for transfers between devices, on_device(): lax.all_to_all(outgoing.reshape(tiles, cap, channels, block), ('lat', 'lo...  4.65 us
    ppermute x2, starting transfers between devices, exchange_columns(): from_right = lax.ppermute(edge, 'lon', back(count))  3.93 us
    ppermute x2, starting transfers between devices, exchange_rows(): from_above = lax.ppermute(down, 'lat', around(count))  1.93 us
  transfers between devices with their start and end apart: 9, of which 5 were waited for; matrix products, arithmetic and copies ran while one was open for 5% of the time, Pallas kernels for 9%

profile of v1, /device:TPU:0, one launch (start us, length us, event | category | flops | bytes accessed | tf_op | source)
XLA Modules:
  0.0 52.3 jit_solution(16426723573017411296)
XLA Ops:
  0.6 0.0 copy-start.6
  0.6 0.0 copy-start.5
  0.7 0.0 copy-start.4
  0.7 0.8 %copy.24 = s32[1,32,4]{2,1,0:T(8,128)S(1)} copy(s32[1,32,4]{1,2,0:T(4,128)} %param.11) | data formatting | bytes 1024 | tf_op args[1]
  1.4 0.1 reshape.31.source_ref
  1.5 0.0 copy-start
  1.6 1.0 %copy-done = bf16[128,16,128]{2,1,0:T(8,128)(2,1)S(1)} copy-done((bf16[128,16,128]{2,1,0:T(8,128)(2,1)S(1)}, bf16[128,16,128]{2,1,0:T(8,128)(2,1)}, u32[]{:S(2)}) %copy-start) | copy-done | bytes 524312
  2.6 0.0 copy-start.3
  2.6 0.9 %copy-done.3 = bf16[1,32,4,8,128]{4,3,2,1,0:T(8,128)(2,1)S(1)} copy-done((bf16[1,32,4,8,128]{4,3,2,1,0:T(8,128)(2,1)S(1)}, bf16[1,32,4,8,128]{4,3,2,1,0:T(8,128)(2,1)}, u32[]{:S(2)}) %copy-start.3) | copy-done | bytes 262168
  3.5 2.4 %gather_band.1 = bf16[128,16,128]{2,1,0:T(8,128)(2,1)} custom-call(s32[128]{0:T(128)S(1)} %reshape.31.source_ref, bf16[128,16,128]{2,1,0:T(8,128)(2,1)S(1)} %copy-done, bf16[128,8,128]{2,1,0:T(8,128)(2,1)S(1)} %bitcast.9), custom_call_target="tpu_custom_call" | custom-call | flops 4194304 | bytes 1311232 | tf_op jit(solution)/shard_map/gather_band/pallas_call | solution.py:33
  6.0 7.3 %all-to-all-start = ((bf16[32,4,16,128]{3,2,1,0:T(8,128)(2,1)}), bf16[32,4,16,128]{3,2,1,0:T(8,128)(2,1)S(1)}, u32[]{:S(2)}, u32[]{:S(2)}) async-start(bf16[32,4,16,128]{3,2,1,0:T(8,128)(2,1)} %bitcast.4), calls=%async_computation | async-start | bytes 1048576 | tf_op jit(solution)/shard_map/all_to_all | solution.py:371
  13.3 0.0 copy-start.1
  13.3 1.0 %copy-done.1 = bf16[32,32,256]{2,1,0:T(8,128)(2,1)S(1)} copy-done((bf16[32,32,256]{2,1,0:T(8,128)(2,1)S(1)}, bf16[32,32,256]{2,1,0:T(8,128)(2,1)}, u32[]{:S(2)}) %copy-start.1) | copy-done | bytes 524312
  14.3 0.0 copy-start.2
  14.3 1.0 %copy-done.2 = bf16[32,32,256]{2,1,0:T(8,128)(2,1)S(1)} copy-done((bf16[32,32,256]{2,1,0:T(8,128)(2,1)S(1)}, bf16[32,32,256]{2,1,0:T(8,128)(2,1)}, u32[]{:S(2)}) %copy-start.2) | copy-done | bytes 524312
  15.3 0.4 prepare.1
  15.8 2.5 %collective-permute-start.1 = (bf16[64,384]{1,0:T(8,128)(2,1)S(1)}, bf16[64,384]{1,0:T(8,128)(2,1)S(1)}, u32[]{:S(2)}, u32[]{:S(2)}) collective-permute-start(bf16[64,384]{1,0:T(8,128)(2,1)S(1)} %get-tuple-element.16.edge_ref), channel_id=1, source_target_pairs={{1,0},{2,1},{3,2},{4,3},{5,4},{6,5},{7,6},{0,7},{9,8},{10,9},{11,1... | collective-permute-start | bytes 147464 | tf_op jit(solution)/shard_map/ppermute | solution.py:309
  18.2 0.0 collective-permute-start
  18.2 0.9 %copy.25 = bf16[128,144]{1,0:T(8,128)(2,1)S(1)} copy(bf16[128,144]{0,1:T(8,128)(2,1)} %param.15) | data formatting | bytes 73728 | tf_op args[5]
  19.1 1.0 %copy.22 = bf16[128,288]{1,0:T(8,128)(2,1)S(1)} copy(bf16[128,288]{0,1:T(8,128)(2,1)} %param.16) | data formatting | bytes 147456 | tf_op args[6]
  20.1 0.1 broadcast_multiply_fusion.weight_ref
  20.2 0.1 broadcast_multiply_fusion.1.in_weight_ref
  20.3 0.1 collective-permute-done.1.right_ref
  20.4 2.4 %collective-permute-done.left_ref = bf16[64,384]{1,0:T(8,128)(2,1)S(1)} collective-permute-done((bf16[64,384]{1,0:T(8,128)(2,1)S(1)}, bf16[64,384]{1,0:T(8,128)(2,1)S(1)}, u32[]{:S(2)}, u32[]{:S(2)}) %collective-permute-start) | collective-permute-done | bytes 49184 | tf_op jit(solution)/shard_map/ppermute | solution.py:308
  22.9 1.9 %collective-permute-start.2 = (bf16[4,64,256]{2,1,0:T(8,128)(2,1)S(1)}, bf16[4,64,256]{2,1,0:T(8,128)(2,1)S(1)}, u32[]{:S(2)}, u32[]{:S(2)}) collective-permute-start(bf16[4,64,256]{2,1,0:T(8,128)(2,1)S(1)} %get-tuple-element.18), channel_id=1, source_target_pairs={{0,8},{8,16},{16,24},{24,0},{1,9},{9,17},{17,25},{25,1},{2,10},{10... | collective-permute-start | bytes 393224 | tf_op jit(solution)/shard_map/ppermute | solution.py:315
  24.8 2.0 %collective-permute-start.3 = (bf16[4,64,256]{2,1,0:T(8,128)(2,1)S(1)}, bf16[4,64,256]{2,1,0:T(8,128)(2,1)S(1)}, u32[]{:S(2)}, u32[]{:S(2)}) collective-permute-start(bf16[4,64,256]{2,1,0:T(8,128)(2,1)S(1)} %get-tuple-element.19), channel_id=1, source_target_pairs={{8,0},{16,8},{24,16},{0,24},{9,1},{17,9},{25,17},{1,25},{10,2},{18... | collective-permute-start | bytes 393224 | tf_op jit(solution)/shard_map/ppermute | solution.py:316
  26.8 0.0 copy-done.6
  26.8 0.0 copy-done.5
  26.8 0.1 copy.23
  26.9 0.1 reshape.29.target_ref
  27.0 4.6 %all-to-all-done = bf16[32,4,16,128]{3,2,1,0:T(8,128)(2,1)S(1)} async-done(((bf16[32,4,16,128]{3,2,1,0:T(8,128)(2,1)}), bf16[32,4,16,128]{3,2,1,0:T(8,128)(2,1)S(1)}, u32[]{:S(2)}, u32[]{:S(2)}) %all-to-all-start) | async-done | bytes 524320 | tf_op jit(solution)/shard_map/all_to_all | solution.py:371
  31.6 0.0 copy-done.4
  31.6 1.3 %scatter_add.1 = (bf16[32,16,256]{2,1,0:T(8,128)(2,1)S(1)}, bf16[16,384]{1,0:T(8,128)(2,1)S(1)}) custom-call(s32[128]{0:T(128)S(1)} %reshape.29.target_ref, s32[32]{0:T(128)S(1)} %bitcast.10, bf16[128,16,128]{2,1,0:T(8,128)(2,1)S(1)} %bitcast.8), custom_call_target="tpu_custom_call" | custom-call | flops 262144 | bytes 799360 | tf_op jit(solution)/shard_map/scatter_add/pallas_call | solution.py:33
  32.9 1.5 %collective-permute-start.5 = (bf16[16,384]{1,0:T(8,128)(2,1)S(1)}, bf16[16,384]{1,0:T(8,128)(2,1)S(1)}, u32[]{:S(2)}, u32[]{:S(2)}) collective-permute-start(bf16[16,384]{1,0:T(8,128)(2,1)S(1)} %get-tuple-element.24.edge_ref), channel_id=1, source_target_pairs={{1,0},{2,1},{3,2},{4,3},{5,4},{6,5},{7,6},{0,7},{9,8},{10,9},{11,1... | collective-permute-start | bytes 36872 | tf_op jit(solution)/shard_map/ppermute | solution.py:309
  34.4 0.0 collective-permute-start.4
  34.4 0.1 add_convert_fusion.flag_ref
  34.5 0.1 copy.27.bias_ref
  34.6 1.2 %collective-permute-done.5.right_ref = bf16[16,384]{1,0:T(8,128)(2,1)S(1)} collective-permute-done((bf16[16,384]{1,0:T(8,128)(2,1)S(1)}, bf16[16,384]{1,0:T(8,128)(2,1)S(1)}, u32[]{:S(2)}, u32[]{:S(2)}) %collective-permute-start.5) | collective-permute-done | bytes 12320 | tf_op jit(solution)/shard_map/ppermute | solution.py:309
  35.8 2.6 %collective-permute-done.4.left_ref = bf16[16,384]{1,0:T(8,128)(2,1)S(1)} collective-permute-done((bf16[16,384]{1,0:T(8,128)(2,1)S(1)}, bf16[16,384]{1,0:T(8,128)(2,1)S(1)}, u32[]{:S(2)}, u32[]{:S(2)}) %collective-permute-start.4) | collective-permute-done | bytes 12320 | tf_op jit(solution)/shard_map/ppermute | solution.py:308
  38.4 0.1 collective-permute-start.6
  38.5 3.8 %collective-permute-start.7 = (bf16[4,16,256]{2,1,0:T(8,128)(2,1)S(1)}, bf16[4,16,256]{2,1,0:T(8,128)(2,1)S(1)}, u32[]{:S(2)}, u32[]{:S(2)}) collective-permute-start(bf16[4,16,256]{2,1,0:T(8,128)(2,1)S(1)} %get-tuple-element.27), channel_id=1, source_target_pairs={{8,0},{16,8},{24,16},{0,24},{9,1},{17,9},{25,17},{1,25},{10,2},{18... | collective-permute-start | bytes 98312 | tf_op jit(solution)/shard_map/ppermute | solution.py:316
  42.3 0.0 collective-permute-done.2.above_ref
  42.3 0.0 collective-permute-done.3.below_ref
  42.3 2.8 %state_gates.1 = (f32[36,128,256]{2,1,0:T(8,128)S(1)}, f32[128,768]{1,0:T(8,128)S(1)}, bf16[32,768]{1,0:T(8,128)(2,1)S(1)}) custom-call(s32[2]{0:T(128)S(1)} %add_convert_fusion.flag_ref, bf16[32,64,256]{2,1,0:T(8,128)(2,1)S(1)} %get-tuple-element.15.rows_ref, bf16[64,768]{1,0:T(8,128)(2,1)S(1)} %get-tuple-element.17.strip_ref, ...), custom_call_target="tpu_custom_call" | custom-call | flops 679477248 | bytes 6643720 | tf_op jit(solution)/shard_map/state_gates/pallas_call | solution.py:33
  45.1 0.0 collective-permute-done.6.f_above_ref
  45.1 0.0 collective-permute-done.7.f_below_ref
  45.1 7.2 %window.1 = (bf16[32,32,256]{2,1,0:T(8,128)(2,1)}, bf16[32,32,256]{2,1,0:T(8,128)(2,1)}) custom-call(s32[2]{0:T(128)S(1)} %add_convert_fusion.flag_ref, f32[36,128,256]{2,1,0:T(8,128)S(1)} %get-tuple-element.20.gates_ref, f32[128,768]{1,0:T(8,128)S(1)} %get-tuple-element.21.strip_gates_ref, bf16[32,64,256]{2,1,0:T(8,128)(2,1)S(1)} %get-tuple-element.15.rows_ref, ...), custom_call_target="tpu_custom_call" | custom-call | flops 1509949440 | bytes 7983624 | tf_op jit(solution)/shard_map/window/pallas_call | solution.py:33
  (4 shorter events, 0.1 us)
Async XLA Ops:
  0.6 26.2 %copy-start.6 = (f32[128]{0:T(128)S(1)}, f32[128]{0:T(128)}, u32[]{:S(2)}) copy-start(f32[128]{0:T(128)} %param.17) | copy-start | bytes 1540
  0.6 26.2 %copy-start.5 = (s32[1,32,4]{1,2,0:T(4,128)S(1)}, s32[1,32,4]{1,2,0:T(4,128)}, u32[]{:S(2)}) copy-start(s32[1,32,4]{1,2,0:T(4,128)} %param.13) | copy-start | bytes 1540
  0.7 31.0 %copy-start.4 = (s32[1,32]{1,0:T(1,128)S(1)}, s32[1,32]{1,0:T(1,128)}, u32[]{:S(2)}) copy-start(s32[1,32]{1,0:T(1,128)} %param.14) | copy-start | bytes 388
  1.5 1.0 %copy-start = (bf16[128,16,128]{2,1,0:T(8,128)(2,1)S(1)}, bf16[128,16,128]{2,1,0:T(8,128)(2,1)}, u32[]{:S(2)}) copy-start(bf16[128,16,128]{2,1,0:T(8,128)(2,1)} %blocks_ref.1) | copy-start | bytes 1572868
  2.6 0.9 %copy-start.3 = (bf16[1,32,4,8,128]{4,3,2,1,0:T(8,128)(2,1)S(1)}, bf16[1,32,4,8,128]{4,3,2,1,0:T(8,128)(2,1)}, u32[]{:S(2)}) copy-start(bf16[1,32,4,8,128]{4,3,2,1,0:T(8,128)(2,1)} %param.12) | copy-start | bytes 786436
  6.0 25.7 %all-to-all-start = ((bf16[32,4,16,128]{3,2,1,0:T(8,128)(2,1)}), bf16[32,4,16,128]{3,2,1,0:T(8,128)(2,1)S(1)}, u32[]{:S(2)}, u32[]{:S(2)}) async-start(bf16[32,4,16,128]{3,2,1,0:T(8,128)(2,1)} %bitcast.4), calls=%async_computation | async-start | bytes 1048576 | tf_op jit(solution)/shard_map/all_to_all | solution.py:371
  13.3 1.0 %copy-start.1 = (bf16[32,32,256]{2,1,0:T(8,128)(2,1)S(1)}, bf16[32,32,256]{2,1,0:T(8,128)(2,1)}, u32[]{:S(2)}) copy-start(bf16[32,32,256]{2,1,0:T(8,128)(2,1)} %hidden_ref.1) | copy-start | bytes 1572868
  14.3 1.0 %copy-start.2 = (bf16[32,32,256]{2,1,0:T(8,128)(2,1)S(1)}, bf16[32,32,256]{2,1,0:T(8,128)(2,1)}, u32[]{:S(2)}) copy-start(bf16[32,32,256]{2,1,0:T(8,128)(2,1)} %cell_ref.1) | copy-start | bytes 1572868
  15.8 4.6 %collective-permute-start.1 = (bf16[64,384]{1,0:T(8,128)(2,1)S(1)}, bf16[64,384]{1,0:T(8,128)(2,1)S(1)}, u32[]{:S(2)}, u32[]{:S(2)}) collective-permute-start(bf16[64,384]{1,0:T(8,128)(2,1)S(1)} %get-tuple-element.16.edge_ref), channel_id=1, source_target_pairs={{1,0},{2,1},{3,2},{4,3},{5,4},{6,5},{7,6},{0,7},{9,8},{10,9},{11,1... | collective-permute-start | bytes 147464 | tf_op jit(solution)/shard_map/ppermute | solution.py:309
  18.2 4.6 %collective-permute-start = (bf16[64,384]{1,0:T(8,128)(2,1)S(1)}, bf16[64,384]{1,0:T(8,128)(2,1)S(1)}, u32[]{:S(2)}, u32[]{:S(2)}) collective-permute-start(bf16[64,384]{1,0:T(8,128)(2,1)S(1)} %get-tuple-element.16.edge_ref), channel_id=1, source_target_pairs={{0,1},{1,2},{2,3},{3,4},{4,5},{5,6},{6,7},{7,0},{8,9},{9,10},{10,1... | collective-permute-start | bytes 147464 | tf_op jit(solution)/shard_map/ppermute | solution.py:308
  22.9 19.4 %collective-permute-start.2 = (bf16[4,64,256]{2,1,0:T(8,128)(2,1)S(1)}, bf16[4,64,256]{2,1,0:T(8,128)(2,1)S(1)}, u32[]{:S(2)}, u32[]{:S(2)}) collective-permute-start(bf16[4,64,256]{2,1,0:T(8,128)(2,1)S(1)} %get-tuple-element.18), channel_id=1, source_target_pairs={{0,8},{8,16},{16,24},{24,0},{1,9},{9,17},{17,25},{25,1},{2,10},{10... | collective-permute-start | bytes 393224 | tf_op jit(solution)/shard_map/ppermute | solution.py:315
  24.8 17.5 %collective-permute-start.3 = (bf16[4,64,256]{2,1,0:T(8,128)(2,1)S(1)}, bf16[4,64,256]{2,1,0:T(8,128)(2,1)S(1)}, u32[]{:S(2)}, u32[]{:S(2)}) collective-permute-start(bf16[4,64,256]{2,1,0:T(8,128)(2,1)S(1)} %get-tuple-element.19), channel_id=1, source_target_pairs={{8,0},{16,8},{24,16},{0,24},{9,1},{17,9},{25,17},{1,25},{10,2},{18... | collective-permute-start | bytes 393224 | tf_op jit(solution)/shard_map/ppermute | solution.py:316
  32.9 2.9 %collective-permute-start.5 = (bf16[16,384]{1,0:T(8,128)(2,1)S(1)}, bf16[16,384]{1,0:T(8,128)(2,1)S(1)}, u32[]{:S(2)}, u32[]{:S(2)}) collective-permute-start(bf16[16,384]{1,0:T(8,128)(2,1)S(1)} %get-tuple-element.24.edge_ref), channel_id=1, source_target_pairs={{1,0},{2,1},{3,2},{4,3},{5,4},{6,5},{7,6},{0,7},{9,8},{10,9},{11,1... | collective-permute-start | bytes 36872 | tf_op jit(solution)/shard_map/ppermute | solution.py:309
  34.4 4.0 %collective-permute-start.4 = (bf16[16,384]{1,0:T(8,128)(2,1)S(1)}, bf16[16,384]{1,0:T(8,128)(2,1)S(1)}, u32[]{:S(2)}, u32[]{:S(2)}) collective-permute-start(bf16[16,384]{1,0:T(8,128)(2,1)S(1)} %get-tuple-element.24.edge_ref), channel_id=1, source_target_pairs={{0,1},{1,2},{2,3},{3,4},{4,5},{5,6},{6,7},{7,0},{8,9},{9,10},{10,1... | collective-permute-start | bytes 36872 | tf_op jit(solution)/shard_map/ppermute | solution.py:308
  38.4 6.7 %collective-permute-start.6 = (bf16[4,16,256]{2,1,0:T(8,128)(2,1)S(1)}, bf16[4,16,256]{2,1,0:T(8,128)(2,1)S(1)}, u32[]{:S(2)}, u32[]{:S(2)}) collective-permute-start(bf16[4,16,256]{2,1,0:T(8,128)(2,1)S(1)} %get-tuple-element.26), channel_id=1, source_target_pairs={{0,8},{8,16},{16,24},{24,0},{1,9},{9,17},{17,25},{25,1},{2,10},{10... | collective-permute-start | bytes 98312 | tf_op jit(solution)/shard_map/ppermute | solution.py:315
  38.5 6.6 %collective-permute-start.7 = (bf16[4,16,256]{2,1,0:T(8,128)(2,1)S(1)}, bf16[4,16,256]{2,1,0:T(8,128)(2,1)S(1)}, u32[]{:S(2)}, u32[]{:S(2)}) collective-permute-start(bf16[4,16,256]{2,1,0:T(8,128)(2,1)S(1)} %get-tuple-element.27), channel_id=1, source_target_pairs={{8,0},{16,8},{24,16},{0,24},{9,1},{17,9},{25,17},{1,25},{10,2},{18... | collective-permute-start | bytes 98312 | tf_op jit(solution)/shard_map/ppermute | solution.py:316

commit v2 on v1

v2 whole, which is shorter than its diff:
```python
import functools

import jax
import jax.numpy as jnp
from jax import lax
from jax.experimental import pallas as pl
from jax.experimental.pallas import tpu as pltpu
from jax.sharding import PartitionSpec as P

STEPS = 3
PAD = 4
LANES = 128
STRIP = 3 * LANES
BATCH = 2
BF = jnp.bfloat16
F32 = jnp.float32


def lane_of(shape):
    return lax.broadcasted_iota(jnp.int32, shape, len(shape) - 1)


def whole(count):
    return [pl.BlockSpec(memory_space=pltpu.VMEM)] * count


def scalars(count):
    return [pl.BlockSpec(memory_space=pltpu.SMEM)] * count


def call(kernel, outs, ins, scalar_count, scratch, name, flops, args):
    nbytes = sum(a.size * a.dtype.itemsize for a in list(args) + list(outs))
    return pl.pallas_call(
        kernel,
        out_shape=tuple(outs),
        in_specs=scalars(scalar_count) + whole(ins),
        out_specs=tuple(whole(len(outs))),
        scratch_shapes=scratch,
        compiler_params=pltpu.CompilerParams(vmem_limit_bytes=40 * 2**20),
        cost_estimate=pl.CostEstimate(flops=flops, bytes_accessed=nbytes, transcendentals=0),
        name=name,
    )(*args)


def edge_tiles(row_of, row_count, channels):
    lane = lane_of((channels, LANES))
    tiles = [jnp.zeros((channels, LANES), BF) for _ in range(STRIP // LANES)]
    for y in range(row_count):
        row = row_of(y)
        both = jnp.where(lane < 64, row[:, :LANES], row[:, -LANES:])
        r = y + PAD
        place = r % 16
        turned = pltpu.roll(both, (8 * place + 4) % LANES, axis=1)
        tiles[r // 16] = jnp.where(lane // 8 == place, turned, tiles[r // 16])
    return tiles


def gather_kernel(
    ring, source_ref, blocks_hbm, weight_hbm, out_hbm, blocks, weights, out, block_sem, weight_sem, out_sem
):
    cap, tiles = source_ref.shape
    band, width = weights.shape[1:]
    channels = blocks.shape[1]
    groups = tiles // ring
    share = ring * cap
    fetch = pltpu.make_async_copy(blocks_hbm, blocks, block_sem)
    fetch.start()
    parts = [
        pltpu.make_async_copy(
            weight_hbm.at[pl.ds(g * share, share)], weights.at[pl.ds(g * share, share)], weight_sem.at[g]
        )
        for g in range(groups)
    ]
    for part in parts:
        part.start()
    offset = lax.broadcasted_iota(jnp.int32, (band, width), 0) - band // 2
    spot = lane_of((band, width)) + offset
    inside = (spot >= 0) & (spot < width)
    lane = lane_of((channels, width))
    near = lane_of((channels // 2, width)) % 8 < 4
    fetch.wait()
    sends = []
    for g in range(groups):
        parts[g].wait()
        folded = []
        for j in range(ring):
            q = g * ring + j
            edges = jnp.zeros((channels, width), BF)
            for s in range(cap):
                block = blocks[source_ref[s, q]]
                factor = jnp.where(inside, weights[q * cap + s].astype(F32), 0.0)
                total = jnp.zeros((channels, width), F32)
                for k in range(band):
                    moved = block if k == band // 2 else pltpu.roll(block, (band // 2 - k) % width, axis=1)
                    total = total + factor[k : k + 1, :] * moved.astype(F32)
                rounded = total.astype(BF)
                out[q, s * channels : (s + 1) * channels, :] = rounded
                edges = jnp.where(lane // 8 == s, pltpu.roll(rounded, 8 * s + 4, axis=1), edges)
            wide = edges.astype(F32)
            folded.append(wide[: channels // 2] + pltpu.roll(wide[channels // 2 :], 8 * cap, axis=1))
        for j in range(ring):
            both = jnp.where(near, folded[j - 1], folded[(j + 1) % ring])
            out[g * ring + j, cap * channels :, :] = both.astype(BF)
        send = pltpu.make_async_copy(
            out.at[pl.ds(g * ring, ring)], out_hbm.at[pl.ds(g * ring, ring)], out_sem.at[g]
        )
        send.start()
        sends.append(send)
    for send in sends:
        send.wait()


def prepare_kernel(hidden_ref, cell_ref, mark_ref, rows_ref, edge_ref):
    units = hidden_ref.shape[0]
    row_count = hidden_ref.shape[1]
    rows_ref[:, :units, :] = jnp.swapaxes(hidden_ref[...], 0, 1)
    rows_ref[:, units:, :] = jnp.swapaxes(cell_ref[...], 0, 1)
    tiles = edge_tiles(lambda y: rows_ref[y], row_count, 2 * units)
    for t, tile in enumerate(tiles):
        edge_ref[: 2 * units, t * LANES : (t + 1) * LANES] = tile
    edge_ref[2 * units :, :LANES] = mark_ref[...]
    edge_ref[2 * units :, LANES:] = jnp.zeros((mark_ref.shape[0], STRIP - LANES), BF)


def lay_out(rows_ref, own, from_left, from_right, strip_ref, up_ref, down_ref):
    near = lane_of(own.shape) % 8 < 4
    left = jnp.where(near, from_left, own)
    right = jnp.where(near, own, from_right)
    strip_ref[:, :STRIP] = left
    strip_ref[:, STRIP:] = right
    rows = rows_ref.shape[0]
    up_ref[:3] = rows_ref[:3]
    up_ref[3, :, :LANES] = left[:, :LANES]
    up_ref[3, :, LANES:] = right[:, :LANES]
    down_ref[:3] = rows_ref[rows - 3 :]
    down_ref[3, :, :LANES] = left[:, 2 * LANES :]
    down_ref[3, :, LANES:] = right[:, 2 * LANES :]


def strips_kernel(rows_ref, edge_ref, left_ref, right_ref, strip_ref, up_ref, down_ref, mark_ref):
    channels = rows_ref.shape[1]
    lay_out(
        rows_ref, edge_ref[:channels], left_ref[:channels], right_ref[:channels], strip_ref, up_ref, down_ref
    )
    near = lane_of(mark_ref.shape) % 8 < 4
    from_left = left_ref[channels:, :LANES].astype(F32)
    mark_ref[...] = jnp.where(near, from_left, right_ref[channels:, :LANES].astype(F32))


def full_strip(strip, above, below, has_above, has_below):
    lane = lane_of(above[:, :LANES].shape)
    from_above = (lane >= 8) & (lane < 32)
    from_below = (lane >= 32) & (lane < 56)
    parts = []
    for side in range(2):
        base = side * STRIP
        theirs = above[:, side * LANES : (side + 1) * LANES] * has_above
        parts.append(jnp.where(from_above, theirs, strip[:, base : base + LANES]))
        parts.append(strip[:, base + LANES : base + 2 * LANES])
        theirs = below[:, side * LANES : (side + 1) * LANES] * has_below
        parts.append(jnp.where(from_below, theirs, strip[:, base + 2 * LANES : base + STRIP]))
    return jnp.concatenate(parts, axis=1)


def strip_taps(strip):
    width = strip.shape[1]
    taps = []
    for a in range(3):
        for e in range(3):
            shift = 8 * (a - 1) + e - 1
            taps.append(strip if shift == 0 else pltpu.roll(strip, -shift % width, axis=1))
    return jnp.concatenate(taps, axis=0)


def patches_of(strip, tiles, first, last):
    channels = strip.shape[0]
    near = lane_of((channels, LANES)) % 8 < 4
    found = {}
    for i, t in enumerate(tiles):
        left = strip[:, i * LANES : (i + 1) * LANES]
        right = strip[:, (len(tiles) + i) * LANES : (len(tiles) + i + 1) * LANES]
        mixed = jnp.where(near, left, right)
        for r in range(max(first, 16 * t), min(last, 16 * t + 16)):
            found[r] = pltpu.roll(mixed, -(8 * (r % 16) + 4) % LANES, axis=1)
    return found


def store_patches(strip, patch_ref, first, last):
    for r, patch in patches_of(strip, range(STRIP // LANES), first, last).items():
        patch_ref[r] = patch


def store_three(ref, r, row, patch):
    channels = row.shape[0]
    lane = lane_of((channels, LANES))
    head, tail = row[:, :LANES], row[:, LANES:]
    ref[r, :channels, :LANES] = pltpu.roll(jnp.where(lane == LANES - 1, patch, head), 1, axis=1)
    ref[r, :channels, LANES:] = pltpu.roll(jnp.where(lane == LANES - 1, head, tail), 1, axis=1)
    ref[r, channels : 2 * channels, :] = row
    ref[r, 2 * channels :, :LANES] = pltpu.roll(jnp.where(lane == 0, tail, head), LANES - 1, axis=1)
    ref[r, 2 * channels :, LANES:] = pltpu.roll(jnp.where(lane == 0, patch, tail), LANES - 1, axis=1)


def row_taps(ref, r):
    channels = ref.shape[1]
    return ref[pl.ds(r - 1, 3)].reshape(3 * channels, ref.shape[2])


def matmul(weights, taps):
    return jnp.dot(weights, taps, preferred_element_type=F32)


def state_kernel(
    flag_ref, rows_ref, strip_ref, above_ref, below_ref, weight_ref, bias_ref,
    gates_ref, strip_gates_ref, cell_strip_ref, wide_bias_ref, three, patches,
):
    units = rows_ref.shape[1] // 2
    count = rows_ref.shape[0]
    has_above = flag_ref[0].astype(F32).astype(BF)
    has_below = flag_ref[1].astype(F32).astype(BF)
    strip = full_strip(strip_ref[...], above_ref[3], below_ref[3], has_above, has_below)
    cell_strip_ref[...] = strip[units:]
    wide_bias_ref[...] = jnp.broadcast_to(bias_ref[...], wide_bias_ref.shape)
    strip = strip[:units]
    strip_gates_ref[...] = matmul(weight_ref[...], strip_taps(strip))
    store_patches(strip, patches, 1, count + 7)
    for i in range(3):
        store_three(three, 1 + i, above_ref[i, :units] * has_above, patches[1 + i])
        r = count + PAD + i
        store_three(three, r, below_ref[i, :units] * has_below, patches[r])

    for y in range(count):
        store_three(three, y + PAD, rows_ref[y, :units], patches[y + PAD])
    for i in range(count + 4):
        gates_ref[i] = matmul(weight_ref[...], row_taps(three, i + 2))


def update(gates, memory):
    units = memory.shape[0]
    ingate = 0.5 * jnp.tanh(gates[:units]) + 0.5
    forget = 0.5 * jnp.tanh(gates[units : 2 * units]) + 0.5
    outgate = 0.5 * jnp.tanh(gates[2 * units : 3 * units]) + 0.5
    memory = forget * memory + ingate * jnp.tanh(gates[3 * units :])
    return outgate * jnp.tanh(memory), memory


def inner_kernel(
    gates_ref, strip_gates_ref, rows_ref, cell_strip_ref, forcing_ref, forcing_strip_ref,
    in_weight_ref, weight_ref, bias_ref,
    hidden_ref, cell_ref, sums_ref, first_ref, second_ref, memory_ref,
    f_three, f_patches, f_gates, first, second, patches, memory,
):
    units = rows_ref.shape[1] // 2
    count = rows_ref.shape[0]
    bias = bias_ref[...]

    strip = forcing_strip_ref[...]
    strip_forcing = matmul(in_weight_ref[...], strip_taps(strip)) + jnp.concatenate([bias] * 3, axis=1)
    store_patches(strip, f_patches, PAD, count + PAD)
    for y in range(count):
        store_three(f_three, y + PAD, forcing_ref[y], f_patches[y + PAD])

    strip_memory = cell_strip_ref[...].astype(F32)
    strip_hidden, strip_memory = update(strip_gates_ref[...] + strip_forcing, strip_memory)
    strip_hidden = strip_hidden.astype(BF)
    store_patches(strip_hidden, patches, PAD + 1, count + PAD - 1)

    def run(margin, body):
        stop = PAD + count - margin
        for start in range(PAD + margin, stop, BATCH):
            body(range(start, min(start + BATCH, stop)))

    def first_rows(group):
        sums = [matmul(in_weight_ref[...], row_taps(f_three, r)) + bias for r in group]
        states = [
            update(gates_ref[r - 2] + s, rows_ref[r - PAD, units:].astype(F32)) for r, s in zip(group, sums)
        ]
        marks = [patches[r] for r in group]
        for r, s, (hidden, new), mark in zip(group, sums, states, marks):
            f_gates[r] = s
            memory[r] = new
            store_three(first, r, hidden.astype(BF), mark)

    run(1, first_rows)

    strip_gates = matmul(weight_ref[...], strip_taps(strip_hidden)) + strip_forcing
    strip_hidden, strip_memory = update(strip_gates, strip_memory)
    store_patches(strip_hidden.astype(BF), patches, PAD + 2, count + PAD - 2)

    def later(source, group):
        sums = [f_gates[r] + matmul(weight_ref[...], row_taps(source, r)) for r in group]
        return [update(s, memory[r]) for r, s in zip(group, sums)]

    def second_rows(group):
        states = later(first, group)
        marks = [patches[r] for r in group]
        for r, (hidden, new), mark in zip(group, states, marks):
            memory[r] = new
            store_three(second, r, hidden.astype(BF), mark)

    run(2, second_rows)

    def third_rows(group):
        for r, (hidden, new) in zip(group, later(second, group)):
            hidden_ref[r - PAD - 3] = hidden.astype(BF)
            cell_ref[r - PAD - 3] = new.astype(BF)

    run(3, third_rows)
    for i, r in enumerate(edge_rows(count, 1, 2)):
        sums_ref[i] = f_gates[r]
        first_ref[i] = first[r]
        memory_ref[i] = memory[r]
    for i, r in enumerate(edge_rows(count, 2, 2)):
        second_ref[i] = second[r]


def edge_rows(count, depth, many):
    top = [PAD + depth + i for i in range(many)]
    return top + [PAD + count - 1 - depth - (many - 1) + i for i in range(many)]


def edge_kernel(
    flag_ref, gates_ref, strip_gates_ref, rows_ref, above_ref, below_ref, cell_strip_ref,
    forcing_ref, forcing_strip_ref, f_above_ref, f_below_ref, in_weight_ref, weight_ref, bias_ref,
    inner_hidden_ref, inner_cell_ref, sums_ref, first_ref, second_ref, memory_ref,
    hidden_ref, cell_ref,
    f_three, first, second, h_rows, c_rows,
):
    units = rows_ref.shape[1] // 2
    count = rows_ref.shape[0]
    has_above = flag_ref[0].astype(F32)
    has_below = flag_ref[1].astype(F32)
    bf_above, bf_below = has_above.astype(BF), has_below.astype(BF)
    bias = bias_ref[...]
    tiles = (0, 2)

    def ends(strip):
        return jnp.concatenate([strip[:, t * LANES : (t + 1) * LANES] for t in (0, 2, 3, 5)], axis=1)

    strip = ends(full_strip(forcing_strip_ref[...], f_above_ref[3], f_below_ref[3], bf_above, bf_below))
    strip_forcing = matmul(in_weight_ref[...], strip_taps(strip)) + jnp.concatenate([bias] * 2, axis=1)
    f_patches = patches_of(strip, tiles, 1, 7)
    f_patches.update(patches_of(strip, tiles, count + PAD - 3, count + PAD + 3))
    for i in range(3):
        store_three(f_three, 1 + i, f_above_ref[i] * bf_above, f_patches[1 + i])
        r = count + PAD + i
        store_three(f_three, r, f_below_ref[i] * bf_below, f_patches[r])
    for r in (PAD, PAD + 1, count + PAD - 2, count + PAD - 1):
        store_three(f_three, r, forcing_ref[r - PAD], f_patches[r])

    lane = lane_of((units, len(tiles) * 2 * LANES))
    row_of_lane = (lane % LANES) // 8 + 32 * (lane // LANES % 2)
    keep = jnp.where(row_of_lane < PAD, has_above, 1.0)
    keep = jnp.where(row_of_lane >= PAD + count, has_below, keep)

    def kept(hidden, r):
        if r < PAD:
            hidden = hidden * has_above
        elif r >= PAD + count:
            hidden = hidden * has_below
        return hidden.astype(BF)

    strip_memory = ends(cell_strip_ref[...]).astype(F32)
    strip_hidden, strip_memory = update(ends(strip_gates_ref[...]) + strip_forcing, strip_memory)
    strip_hidden = (strip_hidden * keep).astype(BF)
    marks = patches_of(strip_hidden, tiles, 2, PAD + 1)
    marks.update(patches_of(strip_hidden, tiles, count + PAD - 1, count + PAD + 2))

    def taps(rows):
        return jnp.concatenate(rows, axis=0)

    sums, memory = {}, {}
    for i, r in enumerate(edge_rows(count, 1, 2)):
        sums[r] = sums_ref[i]
        memory[r] = memory_ref[i]
    group = edge_rows(count, -2, 3)
    olds = [above_ref[1, units:], above_ref[2, units:], rows_ref[0, units:]]
    olds += [rows_ref[count - 1, units:], below_ref[0, units:], below_ref[1, units:]]
    for r, old in zip(group, olds):
        sums[r] = matmul(in_weight_ref[...], row_taps(f_three, r)) + bias
        hidden, memory[r] = update(gates_ref[r - 2] + sums[r], old.astype(F32))
        store_three(first, r, kept(hidden, r), marks[r])
    for i, r in enumerate(edge_rows(count, 1, 2)):
        first[r] = first_ref[i]

    strip_gates = matmul(weight_ref[...], strip_taps(strip_hidden)) + strip_forcing
    strip_hidden, strip_memory = update(strip_gates, strip_memory)
    strip_hidden = (strip_hidden * keep).astype(BF)
    marks = patches_of(strip_hidden, tiles, 3, PAD + 2)
    marks.update(patches_of(strip_hidden, tiles, count + PAD - 2, count + PAD + 1))
    for r in edge_rows(count, -1, 3):
        hidden, memory[r] = update(sums[r] + matmul(weight_ref[...], row_taps(first, r)), memory[r])
        store_three(second, r, kept(hidden, r), marks[r])
    for i, r in enumerate(edge_rows(count, 2, 2)):
        second[r] = second_ref[i]

    for r in edge_rows(count, 0, 3):
        hidden, new = update(sums[r] + matmul(weight_ref[...], row_taps(second, r)), memory[r])
        h_rows[r - PAD] = hidden.astype(BF)
        c_rows[r - PAD] = new.astype(BF)
    h_rows[3 : count - 3] = inner_hidden_ref[...]
    c_rows[3 : count - 3] = inner_cell_ref[...]
    hidden_ref[...] = jnp.swapaxes(h_rows[...], 0, 1)
    cell_ref[...] = jnp.swapaxes(c_rows[...], 0, 1)


def beside(incoming_ref, mark_ref, row_count, channels):
    sources = incoming_ref.shape[0]
    base = incoming_ref.shape[1] - channels // 2
    lane = lane_of((channels // 2, LANES))
    group_lanes = 8 * ((base // channels) % 16)
    tiles = [[jnp.zeros((channels // 2, LANES), F32) for _ in range(2)] for _ in range(STRIP // LANES)]
    for start in range(0, row_count, 16):
        sums = [jnp.zeros((channels // 2, LANES), F32) for _ in range(16)]
        for p in range(sources):
            edges = incoming_ref[p, base:, :].astype(F32)
            mark = jnp.broadcast_to(mark_ref[p : p + 1, :], edges.shape)
            for i in range(16):
                sums[i] = sums[i] + jnp.where(mark == float(start + i), edges, 0.0)
        for i in range(16):
            total = sums[i] + pltpu.roll(sums[i], LANES - 8, axis=1)
            total = total + pltpu.roll(total, LANES - 16, axis=1)
            r = start + i + PAD
            for part in range(2):
                moved = pltpu.roll(total, (8 * (r % 16) - part * group_lanes) % LANES, axis=1)
                tiles[r // 16][part] = jnp.where(lane // 8 == r % 16, moved, tiles[r // 16][part])
    halves = [jnp.concatenate([t[part] for t in tiles], axis=1) for part in range(2)]
    return jnp.concatenate(halves, axis=0).astype(BF)


def scatter_kernel(
    target_ref, count_ref, incoming_ref, mark_ref, rows_ref, strip_ref, up_ref, down_ref, total
):
    cap, sources = target_ref.shape
    row_count, channels, width = rows_ref.shape
    width = width // 2
    spare = 2 * row_count
    total[...] = jnp.zeros(total.shape, F32)
    for p in range(sources):
        live = count_ref[0, p]
        for s in range(cap):
            block = jnp.where(s < live, target_ref[s, p], spare)
            total[block] = total[block] + incoming_ref[p, s * channels : (s + 1) * channels, :].astype(F32)
    for y in range(row_count):
        rows_ref[y, :, :width] = total[2 * y].astype(BF)
        rows_ref[y, :, width:] = total[2 * y + 1].astype(BF)
    own = jnp.concatenate(edge_tiles(lambda y: rows_ref[y], row_count, channels), axis=1)
    others = beside(incoming_ref, mark_ref, row_count, channels)
    lay_out(rows_ref, own, others, others, strip_ref, up_ref, down_ref)


def around(count):
    return [(i, (i + 1) % count) for i in range(count)]


def back(count):
    return [((i + 1) % count, i) for i in range(count)]


def exchange_columns(edge):
    count = lax.axis_size("lon")
    from_left = lax.ppermute(edge, "lon", around(count))
    from_right = lax.ppermute(edge, "lon", back(count))
    return from_left, from_right


def exchange_rows(up, down):
    count = lax.axis_size("lat")
    from_above = lax.ppermute(down, "lat", around(count))
    from_below = lax.ppermute(up, "lat", back(count))
    return from_above, from_below


def marks_of(target, live_count, row_count):
    cap = target.shape[1]
    live = jnp.arange(cap, dtype=jnp.int32)[None, :] < live_count[:, None]
    sides = jnp.arange(2, dtype=jnp.int32)
    wanted = live[:, :, None] & (target[:, :, None] % 2 != sides)
    row = jnp.where(wanted, target[:, :, None] // 2, -1)
    row = jnp.repeat(row, 4, axis=2).reshape(target.shape[0], 8 * cap)
    row = jnp.concatenate([row, row], axis=1)
    return jnp.pad(row, ((0, 0), (0, LANES - row.shape[1])), constant_values=-1).astype(BF)


def on_device(
    satellite_blocks,
    slot_source,
    slot_weight,
    slot_target,
    tile_counts,
    gate_input_weight,
    gate_state_weight,
    gate_bias,
    hidden_init,
    cell_init,
):
    _, tiles, cap, band, block = slot_weight.shape
    channels = satellite_blocks.shape[1]
    units, row_count, column_count = hidden_init.shape
    gates = gate_bias.shape[0]
    slots = tiles * cap
    half = jnp.where(jnp.arange(gates) < 3 * units, 0.5, 1.0)
    in_weight = gate_input_weight * half[:, None].astype(BF)
    state_weight = gate_state_weight * half[:, None].astype(BF)
    bias = (gate_bias * half)[:, None]
    lat = lax.axis_index("lat")
    flags = jnp.stack([lat > 0, lat < lax.axis_size("lat") - 1]).astype(jnp.int32)

    ring = lax.axis_size("lon")
    height = cap * channels + channels // 2
    message = jax.ShapeDtypeStruct((tiles, height, block), BF)
    groups = tiles // ring
    outgoing = pl.pallas_call(
        functools.partial(gather_kernel, ring),
        out_shape=message,
        in_specs=scalars(1) + [pl.BlockSpec(memory_space=pl.ANY)] * 2,
        out_specs=pl.BlockSpec(memory_space=pl.ANY),
        scratch_shapes=[
            pltpu.VMEM(satellite_blocks.shape, BF),
            pltpu.VMEM((slots, band, block), BF),
            pltpu.VMEM(message.shape, BF),
            pltpu.SemaphoreType.DMA,
            pltpu.SemaphoreType.DMA((groups,)),
            pltpu.SemaphoreType.DMA((groups,)),
        ],
        compiler_params=pltpu.CompilerParams(vmem_limit_bytes=40 * 2**20),
        name="gather_band",
    )(slot_source[0].T, satellite_blocks, slot_weight.reshape(slots, band, block))
    incoming = lax.all_to_all(outgoing, ("lat", "lon"), split_axis=0, concat_axis=0, tiled=True)

    rows, edge = call(
        prepare_kernel,
        [
            jax.ShapeDtypeStruct((row_count, 2 * units, column_count), BF),
            jax.ShapeDtypeStruct((2 * units + tiles, STRIP), BF),
        ],
        3, 0, [], "prepare", 1000,
        (hidden_init, cell_init, marks_of(slot_target[0], tile_counts[0], row_count)),
    )
    from_left, from_right = exchange_columns(edge)
    ends = jax.ShapeDtypeStruct((4, 2 * units, column_count), BF)
    strip, up, down, marks = call(
        strips_kernel,
        [
            jax.ShapeDtypeStruct((2 * units, 2 * STRIP), BF),
            ends,
            ends,
            jax.ShapeDtypeStruct((tiles, LANES), F32),
        ],
        4, 0, [], "state_strips", 1000, (rows, edge, from_left, from_right),
    )
    above, below = exchange_rows(up, down)
    extended = row_count + 4
    padded = row_count + 8
    state_gates, strip_gates, cell_strip, bias = call(
        state_kernel,
        [
            jax.ShapeDtypeStruct((extended, gates, column_count), F32),
            jax.ShapeDtypeStruct((gates, 2 * STRIP), F32),
            jax.ShapeDtypeStruct((units, 2 * STRIP), BF),
            jax.ShapeDtypeStruct((gates, column_count), F32),
        ],
        6, 1,
        [
            pltpu.VMEM((padded, 3 * units, column_count), BF),
            pltpu.VMEM((padded, units, LANES), BF),
        ],
        "state_gates", 2 * gates * 9 * units * extended * column_count,
        (flags, rows, strip, above, below, state_weight, bias),
    )
    incoming, state_gates, strip_gates, cell_strip, bias, in_weight = lax.optimization_barrier(
        (incoming, state_gates, strip_gates, cell_strip, bias, in_weight)
    )

    ends = jax.ShapeDtypeStruct((4, channels, column_count), BF)
    forcing, forcing_strip, up, down = call(
        scatter_kernel,
        [
            jax.ShapeDtypeStruct((row_count, channels, column_count), BF),
            jax.ShapeDtypeStruct((channels, 2 * STRIP), BF),
            ends,
            ends,
        ],
        2, 2,
        [pltpu.VMEM((2 * row_count + 1, channels, block), F32)],
        "scatter_add", slots * channels * block,
        (slot_target[0].T, tile_counts, incoming, marks),
    )
    f_above, f_below = exchange_rows(up, down)
    inner_rows = jax.ShapeDtypeStruct((row_count - 6, units, column_count), BF)
    threes = jax.ShapeDtypeStruct((4, 3 * units, column_count), BF)
    inner = call(
        inner_kernel,
        [
            inner_rows,
            inner_rows,
            jax.ShapeDtypeStruct((4, gates, column_count), F32),
            threes,
            threes,
            jax.ShapeDtypeStruct((4, units, column_count), F32),
        ],
        9, 0,
        [
            pltpu.VMEM((padded, 3 * channels, column_count), BF),
            pltpu.VMEM((padded, channels, LANES), BF),
            pltpu.VMEM((padded, gates, column_count), F32),
            pltpu.VMEM((padded, 3 * units, column_count), BF),
            pltpu.VMEM((padded, 3 * units, column_count), BF),
            pltpu.VMEM((padded, units, LANES), BF),
            pltpu.VMEM((padded, units, column_count), F32),
        ],
        "inner", 2 * gates * 9 * (channels + 2 * units) * row_count * column_count,
        (state_gates, strip_gates, rows, cell_strip, forcing, forcing_strip, in_weight, state_weight, bias),
    )
    out = jax.ShapeDtypeStruct((units, row_count, column_count), BF)
    return call(
        edge_kernel,
        [out, out],
        19, 1,
        [
            pltpu.VMEM((padded, 3 * channels, column_count), BF),
            pltpu.VMEM((padded, 3 * units, column_count), BF),
            pltpu.VMEM((padded, 3 * units, column_count), BF),
            pltpu.VMEM((row_count, units, column_count), BF),
            pltpu.VMEM((row_count, units, column_count), BF),
        ],
        "edges", 2 * gates * 9 * (channels + 2 * units) * 6 * column_count,
        (flags, state_gates, strip_gates, rows, above, below, cell_strip, forcing, forcing_strip,
         f_above, f_below, in_weight, state_weight, bias, *inner),
    )


def solution(mesh):
    placed = (
        P(("lat", "lon"), None, None),
        P(("lat", "lon"), None, None),
        P(("lat", "lon"), None, None, None, None),
        P(("lat", "lon"), None, None),
        P(("lat", "lon"), None),
        P(),
        P(),
        P(),
        P(None, "lat", "lon"),
        P(None, "lat", "lon"),
    )
    return jax.shard_map(
        on_device,
        mesh=mesh,
        in_specs=placed,
        out_specs=(P(None, "lat", "lon"), P(None, "lat", "lon")),
        check_vma=False,
    )
```

time: 52.8 us -> 58.7 us (1.11)
  Pallas kernels: 14.1 us -> 18.9 us
  local copies, waits for them, and re-layouts: 7.13 us -> 11.3 us
  waiting for transfers between devices: 11 us -> 7.56 us
  other arithmetic: 0.25 us -> 1.7 us
  starting transfers between devices: 19 us -> 17.9 us
    pallas_call x0 -> x1, Pallas kernels: none -> 6.16 us  [on_device(): pl.pallas_call(functools.partial(gather_kernel, ring), out_shape=message,...]
    all_to_all x1, waiting for transfers between devices: 4.65 us -> 0.01 us  [on_device(): lax.all_to_all(outgoing, ('lat', 'lon'), split_axis=0, concat_axis=0, til...]
    unnamed x18 -> x24, local copies, waits for them, and re-layouts: 6.81 us -> 11.1 us
    ppermute x2, waiting for transfers between devices: 0.01 us -> 2.84 us  [exchange_rows(): from_above = lax.ppermute(down, 'lat', around(count))]
    ppermute x2 -> x1, waiting for transfers between devices: 5.06 us -> 2.59 us  [exchange_columns(): from_left = lax.ppermute(edge, 'lon', around(count))]
    ppermute x2, waiting for transfers between devices: 0.01 us -> 2.11 us  [exchange_rows(): from_below = lax.ppermute(up, 'lat', back(count))]
    ppermute x2, starting transfers between devices: 1.93 us -> 3.76 us  [exchange_rows(): from_above = lax.ppermute(down, 'lat', around(count))]
    ppermute x2 -> x1, starting transfers between devices: 3.93 us -> 2.47 us  [exchange_columns(): from_right = lax.ppermute(edge, 'lon', back(count))]
  transfers between devices with their start and end apart: 9 -> 7, of which waited for: 5 -> 3; matrix products, arithmetic and copies ran while one was open for 5% -> 6% of each run, Pallas kernels for 9% -> 13%
where the time goes in v2:
time: 58.7 us; the launch traced here: 58.2 us
  Pallas kernels  18.9 us (32%)
  starting transfers between devices  17.9 us (30%)
  local copies, waits for them, and re-layouts  11.3 us (19%)
  waiting for transfers between devices  7.56 us (13%)
  other arithmetic  1.7 us (3%)
  between operations  0.81 us (1%)
    pallas_call x6, Pallas kernels, call(): pl.pallas_call(kernel, out_shape=tuple(outs), in_specs=scalars(scalar_cou...  12.7 us
    unnamed x24, local copies, waits for them, and re-layouts  11.1 us
    all_to_all x1, starting transfers between devices, on_device(): lax.all_to_all(outgoing, ('lat', 'lon'), split_axis=0, concat_axis=0, til...  7.3 us
    pallas_call x1, Pallas kernels, on_device(): pl.pallas_call(functools.partial(gather_kernel, ring), out_shape=message,...  6.16 us
    ppermute x2, starting transfers between devices, exchange_rows(): from_below = lax.ppermute(up, 'lat', back(count))  4.4 us
    ppermute x2, starting transfers between devices, exchange_rows(): from_above = lax.ppermute(down, 'lat', around(count))  3.76 us
    ppermute x2, waiting for transfers between devices, exchange_rows(): from_above = lax.ppermute(down, 'lat', around(count))  2.84 us
    ppermute x1, waiting for transfers between devices, exchange_columns(): from_left = lax.ppermute(edge, 'lon', around(count))  2.59 us
  transfers between devices with their start and end apart: 7, of which 3 were waited for; matrix products, arithmetic and copies ran while one was open for 6% of the time, Pallas kernels for 13%

profile of v2, /device:TPU:0, one launch (start us, length us, event | category | flops | bytes accessed | tf_op | source)
XLA Modules:
  0.0 58.2 jit_solution(2268036662199152105)
XLA Ops:
  0.6 0.0 copy-start.9
  0.6 0.0 copy-start.7
  0.7 0.0 copy-start.10
  0.7 0.0 copy-start.3
  0.7 1.0 %copy-done.3 = bf16[128,16,128]{2,1,0:T(8,128)(2,1)S(1)} copy-done((bf16[128,16,128]{2,1,0:T(8,128)(2,1)S(1)}, bf16[128,16,128]{2,1,0:T(8,128)(2,1)}, u32[]{:S(2)}) %copy-start.3) | copy-done | bytes 524312
  1.7 0.0 copy-start.6
  1.7 0.9 %copy-done.6 = bf16[1,32,4,8,128]{4,3,2,1,0:T(8,128)(2,1)S(1)} copy-done((bf16[1,32,4,8,128]{4,3,2,1,0:T(8,128)(2,1)S(1)}, bf16[1,32,4,8,128]{4,3,2,1,0:T(8,128)(2,1)}, u32[]{:S(2)}) %copy-start.6) | copy-done | bytes 262168
  2.7 0.0 copy-start.8
  2.7 0.7 %copy-done.8 = s32[1,32,4]{1,2,0:T(4,128)S(1)} copy-done((s32[1,32,4]{1,2,0:T(4,128)S(1)}, s32[1,32,4]{1,2,0:T(4,128)}, u32[]{:S(2)}) %copy-start.8) | copy-done | bytes 536
  3.4 6.2 %gather_band.1 = bf16[32,72,128]{2,1,0:T(8,128)(2,1)} custom-call(s32[4,32]{1,0:T(4,128)S(1)} %bitcast.36, bf16[128,16,128]{2,1,0:T(8,128)(2,1)S(1)} %copy-done.3, bf16[128,8,128]{2,1,0:T(8,128)(2,1)S(1)} %bitcast.34), custom_call_target="tpu_custom_call" | custom-call | tf_op jit(solution)/shard_map/gather_band/pallas_call | solution.py:513
  9.5 7.3 %all-to-all-start = ((bf16[32,72,128]{2,1,0:T(8,128)(2,1)}), bf16[32,72,128]{2,1,0:T(8,128)(2,1)S(1)}, u32[]{:S(2)}, u32[]{:S(2)}) async-start(bf16[32,72,128]{2,1,0:T(8,128)(2,1)} %gather_band.1), calls=%async_computation | async-start | bytes 1179648 | tf_op jit(solution)/shard_map/all_to_all | solution.py:529
  16.8 0.7 %iota_compare_fusion.1 = pred[32,4]{0,1:T(4,128)(4,1)S(1)} fusion(s32[32]{0:T(128)} %bitcast.37), kind=kLoop, calls=%fused_computation.16 | loop fusion | flops 128 | bytes 256 | tf_op jit(solution)/shard_map/lt | solution.py:476
  17.5 0.7 %add_select_fusion.1 = (s32[32,4]{0,1:T(4,128)S(1)}, s32[32,4]{0,1:T(4,128)S(1)}) fusion(s32[1,32,4]{1,2,0:T(4,128)} %param.13), kind=kLoop, calls=%fused_computation.10 | loop fusion | flops 2432 | bytes 1536 | tf_op jit(solution)/shard_map/jit(remainder)/select_n | solution.py:478
  18.2 0.1 copy.17
  18.3 0.1 fusion.2.mark_ref
  18.4 0.0 copy-start.4
  18.4 1.0 %copy-done.4 = bf16[32,32,256]{2,1,0:T(8,128)(2,1)S(1)} copy-done((bf16[32,32,256]{2,1,0:T(8,128)(2,1)S(1)}, bf16[32,32,256]{2,1,0:T(8,128)(2,1)}, u32[]{:S(2)}) %copy-start.4) | copy-done | bytes 524312
  19.4 0.0 copy-start.5
  19.4 1.0 %copy-done.5 = bf16[32,32,256]{2,1,0:T(8,128)(2,1)S(1)} copy-done((bf16[32,32,256]{2,1,0:T(8,128)(2,1)S(1)}, bf16[32,32,256]{2,1,0:T(8,128)(2,1)}, u32[]{:S(2)}) %copy-start.5) | copy-done | bytes 524312
  20.5 0.4 prepare.1
  20.9 2.5 %collective-permute-start.1 = (bf16[96,384]{1,0:T(8,128)(2,1)S(1)}, bf16[96,384]{1,0:T(8,128)(2,1)S(1)}, u32[]{:S(2)}, u32[]{:S(2)}) collective-permute-start(bf16[96,384]{1,0:T(8,128)(2,1)S(1)} %get-tuple-element.29.edge_ref), channel_id=1, source_target_pairs={{1,0},{2,1},{3,2},{4,3},{5,4},{6,5},{7,6},{0,7},{9,8},{10,9},{11,1... | collective-permute-start | bytes 221192 | tf_op jit(solution)/shard_map/ppermute | solution.py:463
  23.4 0.0 collective-permute-start
  23.4 0.9 %copy.21 = bf16[128,144]{1,0:T(8,128)(2,1)S(1)} copy(bf16[128,144]{0,1:T(8,128)(2,1)} %param.15) | data formatting | bytes 73728 | tf_op args[5]
  24.3 1.0 %copy.19 = bf16[128,288]{1,0:T(8,128)(2,1)S(1)} copy(bf16[128,288]{0,1:T(8,128)(2,1)} %param.16) | data formatting | bytes 147456 | tf_op args[6]
  25.3 0.1 broadcast_multiply_fusion.weight_ref
  25.4 0.1 broadcast_multiply_fusion.1.in_weight_ref
  25.5 0.0 collective-permute-done.1.right_ref
  25.5 2.6 %collective-permute-done.left_ref = bf16[96,384]{1,0:T(8,128)(2,1)S(1)} collective-permute-done((bf16[96,384]{1,0:T(8,128)(2,1)S(1)}, bf16[96,384]{1,0:T(8,128)(2,1)S(1)}, u32[]{:S(2)}, u32[]{:S(2)}) %collective-permute-start) | collective-permute-done | bytes 73760 | tf_op jit(solution)/shard_map/ppermute | solution.py:462
  28.1 1.8 %collective-permute-start.2 = (bf16[4,64,256]{2,1,0:T(8,128)(2,1)S(1)}, bf16[4,64,256]{2,1,0:T(8,128)(2,1)S(1)}, u32[]{:S(2)}, u32[]{:S(2)}) collective-permute-start(bf16[4,64,256]{2,1,0:T(8,128)(2,1)S(1)} %get-tuple-element.31), channel_id=1, source_target_pairs={{0,8},{8,16},{16,24},{24,0},{1,9},{9,17},{17,25},{25,1},{2,10},{10... | collective-permute-start | bytes 393224 | tf_op jit(solution)/shard_map/ppermute | solution.py:469
  29.9 2.4 %collective-permute-start.3 = (bf16[4,64,256]{2,1,0:T(8,128)(2,1)S(1)}, bf16[4,64,256]{2,1,0:T(8,128)(2,1)S(1)}, u32[]{:S(2)}, u32[]{:S(2)}) collective-permute-start(bf16[4,64,256]{2,1,0:T(8,128)(2,1)S(1)} %get-tuple-element.32), channel_id=1, source_target_pairs={{8,0},{16,8},{24,16},{0,24},{9,1},{17,9},{25,17},{1,25},{10,2},{18... | collective-permute-start | bytes 393224 | tf_op jit(solution)/shard_map/ppermute | solution.py:470
  32.4 0.0 copy-done.10
  32.4 0.1 copy.20.bias_ref
  32.5 0.1 add_convert_fusion.flag_ref
  32.6 2.8 %collective-permute-done.2.above_ref = bf16[4,64,256]{2,1,0:T(8,128)(2,1)S(1)} collective-permute-done((bf16[4,64,256]{2,1,0:T(8,128)(2,1)S(1)}, bf16[4,64,256]{2,1,0:T(8,128)(2,1)S(1)}, u32[]{:S(2)}, u32[]{:S(2)}) %collective-permute-start.2) | collective-permute-done | bytes 131104 | tf_op jit(solution)/shard_map/ppermute | solution.py:469
  35.4 2.1 %collective-permute-done.3.below_ref = bf16[4,64,256]{2,1,0:T(8,128)(2,1)S(1)} collective-permute-done((bf16[4,64,256]{2,1,0:T(8,128)(2,1)S(1)}, bf16[4,64,256]{2,1,0:T(8,128)(2,1)S(1)}, u32[]{:S(2)}, u32[]{:S(2)}) %collective-permute-start.3) | collective-permute-done | bytes 131104 | tf_op jit(solution)/shard_map/ppermute | solution.py:470
  37.5 2.8 %state_gates.1 = (f32[36,128,256]{2,1,0:T(8,128)S(1)}, f32[128,768]{1,0:T(8,128)S(1)}, bf16[32,768]{1,0:T(8,128)(2,1)S(1)}, f32[128,256]{1,0:T(8,128)S(1)}) custom-call(s32[2]{0:T(128)S(1)} %add_convert_fusion.flag_ref, bf16[32,64,256]{2,1,0:T(8,128)(2,1)S(1)} %get-tuple-element.28.rows_ref, bf16[64,768]{1,0:T(8,128)(2,1)S(1)} %get-tuple-element.30.strip_ref, ...), custom_call_target="tpu_custom_call" | custom-call | flops 679477248 | bytes 6775304 | tf_op jit(solution)/shard_map/state_gates/pallas_call | solution.py:33
  40.3 0.0 copy-start
  40.3 2.1 %copy-done = f32[36,128,256]{2,1,0:T(8,128)} copy-done((f32[36,128,256]{2,1,0:T(8,128)}, f32[36,128,256]{2,1,0:T(8,128)S(1)}, u32[]{:S(2)}) %copy-start) | copy-done | bytes 4718616
  42.5 0.0 all-to-all-done.incoming_ref
  42.5 0.0 copy-done.9
  42.5 0.0 copy-done.7
  42.5 1.8 %scatter_add.1 = (bf16[32,16,256]{2,1,0:T(8,128)(2,1)S(1)}, bf16[16,768]{1,0:T(8,128)(2,1)S(1)}, bf16[4,16,256]{2,1,0:T(8,128)(2,1)S(1)}, bf16[4,16,256]{2,1,0:T(8,128)(2,1)S(1)}) custom-call(s32[4,32]{1,0:T(4,128)S(1)} %bitcast.35, s32[1,32]{1,0:T(1,128)S(1)} %copy-done.9, bf16[32,72,128]{2,1,0:T(8,128)(2,1)S(1)} %all-to-all-done.incoming_ref, ...), custom_call_target="tpu_custom_call" | custom-call | flops 262144 | bytes 959104 | tf_op jit(solution)/shard_map/scatter_add/pallas_call | solution.py:33
  44.3 1.9 %collective-permute-start.4 = (bf16[4,16,256]{2,1,0:T(8,128)(2,1)S(1)}, bf16[4,16,256]{2,1,0:T(8,128)(2,1)S(1)}, u32[]{:S(2)}, u32[]{:S(2)}) collective-permute-start(bf16[4,16,256]{2,1,0:T(8,128)(2,1)S(1)} %get-tuple-element.44), channel_id=1, source_target_pairs={{0,8},{8,16},{16,24},{24,0},{1,9},{9,17},{17,25},{25,1},{2,10},{10... | collective-permute-start | bytes 98312 | tf_op jit(solution)/shard_map/ppermute | solution.py:469
  46.2 2.0 %collective-permute-start.5 = (bf16[4,16,256]{2,1,0:T(8,128)(2,1)S(1)}, bf16[4,16,256]{2,1,0:T(8,128)(2,1)S(1)}, u32[]{:S(2)}, u32[]{:S(2)}) collective-permute-start(bf16[4,16,256]{2,1,0:T(8,128)(2,1)S(1)} %get-tuple-element.45), channel_id=1, source_target_pairs={{8,0},{16,8},{24,16},{0,24},{9,1},{17,9},{25,17},{1,25},{10,2},{18... | collective-permute-start | bytes 98312 | tf_op jit(solution)/shard_map/ppermute | solution.py:470
  48.2 0.0 copy-start.1
  48.2 2.3 %copy-done.1 = f32[36,128,256]{2,1,0:T(8,128)S(1)} copy-done((f32[36,128,256]{2,1,0:T(8,128)S(1)}, f32[36,128,256]{2,1,0:T(8,128)}, u32[]{:S(2)}) %copy-start.1) | copy-done | bytes 4718616
  50.5 0.0 copy-start.2
  50.5 4.6 %inner.1 = (bf16[26,32,256]{2,1,0:T(8,128)(2,1)S(1)}, bf16[26,32,256]{2,1,0:T(8,128)(2,1)S(1)}, f32[4,128,256]{2,1,0:T(8,128)S(1)}, bf16[4,96,256]{2,1,0:T(8,128...) custom-call(f32[36,128,256]{2,1,0:T(8,128)S(1)} %copy-done.1, ...), custom_call_target="tpu_custom_call" | custom-call | flops 1509949440 | bytes 8638464 | tf_op jit(solution)/shard_map/inner/pallas_call | solution.py:33
  55.1 0.0 collective-permute-done.4.f_above_ref
  55.1 0.0 collective-permute-done.5.f_below_ref
  55.1 0.0 copy-done.2
  55.1 3.0 %edges.1 = (bf16[32,32,256]{2,1,0:T(8,128)(2,1)}, bf16[32,32,256]{2,1,0:T(8,128)(2,1)}) custom-call(s32[2]{0:T(128)S(1)} %add_convert_fusion.flag_ref, f32[36,128,256]{2,1,0:T(8,128)S(1)} %copy-done.2, f32[128,768]{1,0:T(8,128)S(1)} %get-tuple-element.38.strip_gates_ref, bf16[32,64,256]{2,1,0:T(8,128)(2,1)S(1)} %get-tuple-element.28.rows_ref, ...), custom_call_target="tpu_custom_call" | custom-call | flops 283115520 | bytes 10014728 | tf_op jit(solution)/shard_map/edges/pallas_call | solution.py:33
  (5 shorter events, 0.1 us)
Async XLA Ops:
  0.6 41.8 %copy-start.9 = (s32[1,32]{1,0:T(1,128)S(1)}, s32[1,32]{1,0:T(1,128)}, u32[]{:S(2)}) copy-start(s32[1,32]{1,0:T(1,128)} %count_ref.1) | copy-start | bytes 388
  0.6 41.8 %copy-start.7 = (s32[1,32,4]{1,2,0:T(4,128)S(1)}, s32[1,32,4]{1,2,0:T(4,128)}, u32[]{:S(2)}) copy-start(s32[1,32,4]{1,2,0:T(4,128)} %param.13) | copy-start | bytes 1540
  0.7 31.7 %copy-start.10 = (f32[128]{0:T(128)S(1)}, f32[128]{0:T(128)}, u32[]{:S(2)}) copy-start(f32[128]{0:T(128)} %param.17) | copy-start | bytes 1540
  0.7 1.1 %copy-start.3 = (bf16[128,16,128]{2,1,0:T(8,128)(2,1)S(1)}, bf16[128,16,128]{2,1,0:T(8,128)(2,1)}, u32[]{:S(2)}) copy-start(bf16[128,16,128]{2,1,0:T(8,128)(2,1)} %blocks_hbm.1) | copy-start | bytes 1572868
  1.7 0.9 %copy-start.6 = (bf16[1,32,4,8,128]{4,3,2,1,0:T(8,128)(2,1)S(1)}, bf16[1,32,4,8,128]{4,3,2,1,0:T(8,128)(2,1)}, u32[]{:S(2)}) copy-start(bf16[1,32,4,8,128]{4,3,2,1,0:T(8,128)(2,1)} %param.12) | copy-start | bytes 786436
  2.7 0.7 %copy-start.8 = (s32[1,32,4]{1,2,0:T(4,128)S(1)}, s32[1,32,4]{1,2,0:T(4,128)}, u32[]{:S(2)}) copy-start(s32[1,32,4]{1,2,0:T(4,128)} %param.11) | copy-start | bytes 1540
  9.5 32.9 %all-to-all-start = ((bf16[32,72,128]{2,1,0:T(8,128)(2,1)}), bf16[32,72,128]{2,1,0:T(8,128)(2,1)S(1)}, u32[]{:S(2)}, u32[]{:S(2)}) async-start(bf16[32,72,128]{2,1,0:T(8,128)(2,1)} %gather_band.1), calls=%async_computation | async-start | bytes 1179648 | tf_op jit(solution)/shard_map/all_to_all | solution.py:529
  18.4 1.1 %copy-start.4 = (bf16[32,32,256]{2,1,0:T(8,128)(2,1)S(1)}, bf16[32,32,256]{2,1,0:T(8,128)(2,1)}, u32[]{:S(2)}) copy-start(bf16[32,32,256]{2,1,0:T(8,128)(2,1)} %hidden_ref.1) | copy-start | bytes 1572868
  19.4 1.0 %copy-start.5 = (bf16[32,32,256]{2,1,0:T(8,128)(2,1)S(1)}, bf16[32,32,256]{2,1,0:T(8,128)(2,1)}, u32[]{:S(2)}) copy-start(bf16[32,32,256]{2,1,0:T(8,128)(2,1)} %cell_ref.1) | copy-start | bytes 1572868
  20.9 4.6 %collective-permute-start.1 = (bf16[96,384]{1,0:T(8,128)(2,1)S(1)}, bf16[96,384]{1,0:T(8,128)(2,1)S(1)}, u32[]{:S(2)}, u32[]{:S(2)}) collective-permute-start(bf16[96,384]{1,0:T(8,128)(2,1)S(1)} %get-tuple-element.29.edge_ref), channel_id=1, source_target_pairs={{1,0},{2,1},{3,2},{4,3},{5,4},{6,5},{7,6},{0,7},{9,8},{10,9},{11,1... | collective-permute-start | bytes 221192 | tf_op jit(solution)/shard_map/ppermute | solution.py:463
  23.4 4.7 %collective-permute-start = (bf16[96,384]{1,0:T(8,128)(2,1)S(1)}, bf16[96,384]{1,0:T(8,128)(2,1)S(1)}, u32[]{:S(2)}, u32[]{:S(2)}) collective-permute-start(bf16[96,384]{1,0:T(8,128)(2,1)S(1)} %get-tuple-element.29.edge_ref), channel_id=1, source_target_pairs={{0,1},{1,2},{2,3},{3,4},{4,5},{5,6},{6,7},{7,0},{8,9},{9,10},{10,1... | collective-permute-start | bytes 221192 | tf_op jit(solution)/shard_map/ppermute | solution.py:462
  28.1 7.3 %collective-permute-start.2 = (bf16[4,64,256]{2,1,0:T(8,128)(2,1)S(1)}, bf16[4,64,256]{2,1,0:T(8,128)(2,1)S(1)}, u32[]{:S(2)}, u32[]{:S(2)}) collective-permute-start(bf16[4,64,256]{2,1,0:T(8,128)(2,1)S(1)} %get-tuple-element.31), channel_id=1, source_target_pairs={{0,8},{8,16},{16,24},{24,0},{1,9},{9,17},{17,25},{25,1},{2,10},{10... | collective-permute-start | bytes 393224 | tf_op jit(solution)/shard_map/ppermute | solution.py:469
  29.9 7.6 %collective-permute-start.3 = (bf16[4,64,256]{2,1,0:T(8,128)(2,1)S(1)}, bf16[4,64,256]{2,1,0:T(8,128)(2,1)S(1)}, u32[]{:S(2)}, u32[]{:S(2)}) collective-permute-start(bf16[4,64,256]{2,1,0:T(8,128)(2,1)S(1)} %get-tuple-element.32), channel_id=1, source_target_pairs={{8,0},{16,8},{24,16},{0,24},{9,1},{17,9},{25,17},{1,25},{10,2},{18... | collective-permute-start | bytes 393224 | tf_op jit(solution)/shard_map/ppermute | solution.py:470
  40.3 2.1 %copy-start = (f32[36,128,256]{2,1,0:T(8,128)}, f32[36,128,256]{2,1,0:T(8,128)S(1)}, u32[]{:S(2)}) copy-start(f32[36,128,256]{2,1,0:T(8,128)S(1)} %get-tuple-element.37.gates_ref) | copy-start | bytes 14155780
  44.3 10.8 %collective-permute-start.4 = (bf16[4,16,256]{2,1,0:T(8,128)(2,1)S(1)}, bf16[4,16,256]{2,1,0:T(8,128)(2,1)S(1)}, u32[]{:S(2)}, u32[]{:S(2)}) collective-permute-start(bf16[4,16,256]{2,1,0:T(8,128)(2,1)S(1)} %get-tuple-element.44), channel_id=1, source_target_pairs={{0,8},{8,16},{16,24},{24,0},{1,9},{9,17},{17,25},{25,1},{2,10},{10... | collective-permute-start | bytes 98312 | tf_op jit(solution)/shard_map/ppermute | solution.py:469
  46.2 8.9 %collective-permute-start.5 = (bf16[4,16,256]{2,1,0:T(8,128)(2,1)S(1)}, bf16[4,16,256]{2,1,0:T(8,128)(2,1)S(1)}, u32[]{:S(2)}, u32[]{:S(2)}) collective-permute-start(bf16[4,16,256]{2,1,0:T(8,128)(2,1)S(1)} %get-tuple-element.45), channel_id=1, source_target_pairs={{8,0},{16,8},{24,16},{0,24},{9,1},{17,9},{25,17},{1,25},{10,2},{18... | collective-permute-start | bytes 98312 | tf_op jit(solution)/shard_map/ppermute | solution.py:470
  48.2 2.3 %copy-start.1 = (f32[36,128,256]{2,1,0:T(8,128)S(1)}, f32[36,128,256]{2,1,0:T(8,128)}, u32[]{:S(2)}) copy-start(f32[36,128,256]{2,1,0:T(8,128)} %copy-done) | copy-start | bytes 14155780
  50.5 4.6 %copy-start.2 = (f32[36,128,256]{2,1,0:T(8,128)S(1)}, f32[36,128,256]{2,1,0:T(8,128)}, u32[]{:S(2)}) copy-start(f32[36,128,256]{2,1,0:T(8,128)} %copy-done) | copy-start | bytes 14155780

commit v3 on v2

--- a/solution.py
+++ b/solution.py
@@ -28,7 +28,7 @@
     return [pl.BlockSpec(memory_space=pltpu.SMEM)] * count
 
 
-def call(kernel, outs, ins, scalar_count, scratch, name, flops, args):
+def call(kernel, outs, ins, scalar_count, scratch, name, flops, args, mib=8):
     nbytes = sum(a.size * a.dtype.itemsize for a in list(args) + list(outs))
     return pl.pallas_call(
         kernel,
@@ -36,7 +36,7 @@
         in_specs=scalars(scalar_count) + whole(ins),
         out_specs=tuple(whole(len(outs))),
         scratch_shapes=scratch,
-        compiler_params=pltpu.CompilerParams(vmem_limit_bytes=40 * 2**20),
+        compiler_params=pltpu.CompilerParams(vmem_limit_bytes=mib * 2**20),
         cost_estimate=pl.CostEstimate(flops=flops, bytes_accessed=nbytes, transcendentals=0),
         name=name,
     )(*args)
@@ -56,7 +56,7 @@
 
 
 def gather_kernel(
-    ring, source_ref, blocks_hbm, weight_hbm, out_hbm, blocks, weights, out, block_sem, weight_sem, out_sem
+    ring, source_hbm, blocks_hbm, weight_hbm, out_hbm, blocks, weights, out, source_ref, source_sem, block_sem, weight_sem, out_sem
 ):
     cap, tiles = source_ref.shape
     band, width = weights.shape[1:]
@@ -65,6 +65,8 @@
     share = ring * cap
     fetch = pltpu.make_async_copy(blocks_hbm, blocks, block_sem)
     fetch.start()
+    places = pltpu.make_async_copy(source_hbm, source_ref, source_sem)
+    places.start()
     parts = [
         pltpu.make_async_copy(
             weight_hbm.at[pl.ds(g * share, share)], weights.at[pl.ds(g * share, share)], weight_sem.at[g]
@@ -78,6 +80,7 @@
     inside = (spot >= 0) & (spot < width)
     lane = lane_of((channels, width))
     near = lane_of((channels // 2, width)) % 8 < 4
+    places.wait()
     fetch.wait()
     sends = []
     for g in range(groups):
@@ -85,7 +88,6 @@
         folded = []
         for j in range(ring):
             q = g * ring + j
-            edges = jnp.zeros((channels, width), BF)
             for s in range(cap):
                 block = blocks[source_ref[s, q]]
                 factor = jnp.where(inside, weights[q * cap + s].astype(F32), 0.0)
@@ -95,6 +97,10 @@
                     total = total + factor[k : k + 1, :] * moved.astype(F32)
                 rounded = total.astype(BF)
                 out[q, s * channels : (s + 1) * channels, :] = rounded
+        for j in range(ring):
+            edges = jnp.zeros((channels, width), BF)
+            for s in range(cap):
+                rounded = out[g * ring + j, s * channels : (s + 1) * channels, :]
                 edges = jnp.where(lane // 8 == s, pltpu.roll(rounded, 8 * s + 4, axis=1), edges)
             wide = edges.astype(F32)
             folded.append(wide[: channels // 2] + pltpu.roll(wide[channels // 2 :], 8 * cap, axis=1))
@@ -110,16 +116,44 @@
         send.wait()
 
 
-def prepare_kernel(hidden_ref, cell_ref, mark_ref, rows_ref, edge_ref):
-    units = hidden_ref.shape[0]
-    row_count = hidden_ref.shape[1]
-    rows_ref[:, :units, :] = jnp.swapaxes(hidden_ref[...], 0, 1)
-    rows_ref[:, units:, :] = jnp.swapaxes(cell_ref[...], 0, 1)
+def prepare_kernel(
+    hidden_hbm, cell_hbm, target_ref, count_ref, rows_ref, edge_ref, hidden, cell, hidden_sem, cell_sem
+):
+    fetches = [
+        pltpu.make_async_copy(hidden_hbm, hidden, hidden_sem),
+        pltpu.make_async_copy(cell_hbm, cell, cell_sem),
+    ]
+    for fetch in fetches:
+        fetch.start()
+    units, row_count, _ = hidden.shape
+    edge_ref[2 * units :, :LANES] = marks_of(target_ref[...], count_ref[...]).astype(BF)
+    edge_ref[2 * units :, LANES:] = jnp.zeros((target_ref.shape[1], STRIP - LANES), BF)
+    fetches[0].wait()
+    rows_ref[:, :units, :] = jnp.swapaxes(hidden[...], 0, 1)
+    fetches[1].wait()
+    rows_ref[:, units:, :] = jnp.swapaxes(cell[...], 0, 1)
     tiles = edge_tiles(lambda y: rows_ref[y], row_count, 2 * units)
     for t, tile in enumerate(tiles):
         edge_ref[: 2 * units, t * LANES : (t + 1) * LANES] = tile
-    edge_ref[2 * units :, :LANES] = mark_ref[...]
-    edge_ref[2 * units :, LANES:] = jnp.zeros((mark_ref.shape[0], STRIP - LANES), BF)
+
+
+def marks_of(target, live_count):
+    cap, sources = target.shape
+    slot = lax.broadcasted_iota(jnp.int32, target.shape, 0)
+    live = slot < live_count
+    row = target // 2
+    odd = target % 2 == 1
+    picked = [jnp.where(live & odd, row, -1), jnp.where(live & ~odd, row, -1)]
+    rows = jnp.concatenate([p.astype(F32) for p in picked], axis=0)
+    lane = lane_of((2 * cap, LANES))
+    which = lax.broadcasted_iota(jnp.int32, (2 * cap, LANES), 0)
+    spread = (lane // 8 % cap == which % cap) & ((lane % 8 < 4) == (which < cap))
+    return lax.dot_general(
+        rows.astype(BF),
+        jnp.where(spread, 1.0, 0.0).astype(BF),
+        (((0,), (0,)), ((), ())),
+        preferred_element_type=F32,
+    )
 
 
 def lay_out(rows_ref, own, from_left, from_right, strip_ref, up_ref, down_ref):
@@ -211,28 +245,53 @@
 
 
 def state_kernel(
-    flag_ref, rows_ref, strip_ref, above_ref, below_ref, weight_ref, bias_ref,
-    gates_ref, strip_gates_ref, cell_strip_ref, wide_bias_ref, three, patches,
+    rows_ref, strip_ref, weight_ref, bias_ref,
+    gates_ref, strip_gates_ref, wide_bias_ref, three, patches,
+):
+    units = rows_ref.shape[1] // 2
+    count = rows_ref.shape[0]
+    wide_bias_ref[...] = jnp.broadcast_to(bias_ref[...], wide_bias_ref.shape)
+    strip = strip_ref[:units]
+    strip_gates_ref[...] = matmul(weight_ref[...], strip_taps(strip))
+    store_patches(strip, patches, PAD, count + PAD)
+    for y in range(count):
+        store_three(three, y + PAD, rows_ref[y, :units], patches[y + PAD])
+    for y in range(1, count - 1):
+        gates_ref[y - 1] = matmul(weight_ref[...], row_taps(three, y + PAD))
+
+
+def ends_of(strip):
+    return jnp.concatenate([strip[:, t * LANES : (t + 1) * LANES] for t in (0, 2, 3, 5)], axis=1)
+
+
+def edge_patches(strip, first, last, count):
+    found = patches_of(strip, (0, 2), first, last)
+    mirror = count + 2 * PAD - 1
+    found.update(patches_of(strip, (0, 2), mirror - last + 1, mirror - first + 1))
+    return found
+
+
+def state_edge_kernel(
+    flag_ref, rows_ref, strip_ref, above_ref, below_ref, weight_ref,
+    gates_ref, strip_gates_ref, cell_strip_ref, three,
 ):
     units = rows_ref.shape[1] // 2
     count = rows_ref.shape[0]
     has_above = flag_ref[0].astype(F32).astype(BF)
     has_below = flag_ref[1].astype(F32).astype(BF)
-    strip = full_strip(strip_ref[...], above_ref[3], below_ref[3], has_above, has_below)
+    strip = ends_of(full_strip(strip_ref[...], above_ref[3], below_ref[3], has_above, has_below))
     cell_strip_ref[...] = strip[units:]
-    wide_bias_ref[...] = jnp.broadcast_to(bias_ref[...], wide_bias_ref.shape)
     strip = strip[:units]
     strip_gates_ref[...] = matmul(weight_ref[...], strip_taps(strip))
-    store_patches(strip, patches, 1, count + 7)
+    patches = edge_patches(strip, 1, PAD + 2, count)
     for i in range(3):
         store_three(three, 1 + i, above_ref[i, :units] * has_above, patches[1 + i])
         r = count + PAD + i
         store_three(three, r, below_ref[i, :units] * has_below, patches[r])
-
-    for y in range(count):
-        store_three(three, y + PAD, rows_ref[y, :units], patches[y + PAD])
-    for i in range(count + 4):
-        gates_ref[i] = matmul(weight_ref[...], row_taps(three, i + 2))
+    for r in edge_rows(count, 0, 2):
+        store_three(three, r, rows_ref[r - PAD, :units], patches[r])
+    for i, r in enumerate(edge_rows(count, -2, 3)):
+        gates_ref[i] = matmul(weight_ref[...], row_taps(three, r))
 
 
 def update(gates, memory):
@@ -245,7 +304,7 @@
 
 
 def inner_kernel(
-    gates_ref, strip_gates_ref, rows_ref, cell_strip_ref, forcing_ref, forcing_strip_ref,
+    gates_ref, strip_gates_ref, rows_ref, strip_ref, forcing_ref, forcing_strip_ref,
     in_weight_ref, weight_ref, bias_ref,
     hidden_ref, cell_ref, sums_ref, first_ref, second_ref, memory_ref,
     f_three, f_patches, f_gates, first, second, patches, memory,
@@ -260,7 +319,7 @@
     for y in range(count):
         store_three(f_three, y + PAD, forcing_ref[y], f_patches[y + PAD])
 
-    strip_memory = cell_strip_ref[...].astype(F32)
+    strip_memory = strip_ref[units:].astype(F32)
     strip_hidden, strip_memory = update(strip_gates_ref[...] + strip_forcing, strip_memory)
     strip_hidden = strip_hidden.astype(BF)
     store_patches(strip_hidden, patches, PAD + 1, count + PAD - 1)
@@ -273,7 +332,7 @@
     def first_rows(group):
         sums = [matmul(in_weight_ref[...], row_taps(f_three, r)) + bias for r in group]
         states = [
-            update(gates_ref[r - 2] + s, rows_ref[r - PAD, units:].astype(F32)) for r, s in zip(group, sums)
+            update(gates_ref[r - PAD - 1] + s, rows_ref[r - PAD, units:].astype(F32)) for r, s in zip(group, sums)
         ]
         marks = [patches[r] for r in group]
         for r, s, (hidden, new), mark in zip(group, sums, states, marks):
@@ -332,23 +391,18 @@
     has_below = flag_ref[1].astype(F32)
     bf_above, bf_below = has_above.astype(BF), has_below.astype(BF)
     bias = bias_ref[...]
-    tiles = (0, 2)
-
-    def ends(strip):
-        return jnp.concatenate([strip[:, t * LANES : (t + 1) * LANES] for t in (0, 2, 3, 5)], axis=1)
-
-    strip = ends(full_strip(forcing_strip_ref[...], f_above_ref[3], f_below_ref[3], bf_above, bf_below))
+
+    strip = ends_of(full_strip(forcing_strip_ref[...], f_above_ref[3], f_below_ref[3], bf_above, bf_below))
     strip_forcing = matmul(in_weight_ref[...], strip_taps(strip)) + jnp.concatenate([bias] * 2, axis=1)
-    f_patches = patches_of(strip, tiles, 1, 7)
-    f_patches.update(patches_of(strip, tiles, count + PAD - 3, count + PAD + 3))
+    f_patches = edge_patches(strip, 1, PAD + 2, count)
     for i in range(3):
         store_three(f_three, 1 + i, f_above_ref[i] * bf_above, f_patches[1 + i])
         r = count + PAD + i
         store_three(f_three, r, f_below_ref[i] * bf_below, f_patches[r])
-    for r in (PAD, PAD + 1, count + PAD - 2, count + PAD - 1):
+    for r in edge_rows(count, 0, 2):
         store_three(f_three, r, forcing_ref[r - PAD], f_patches[r])
 
-    lane = lane_of((units, len(tiles) * 2 * LANES))
+    lane = lane_of((units, strip.shape[1]))
     row_of_lane = (lane % LANES) // 8 + 32 * (lane // LANES % 2)
     keep = jnp.where(row_of_lane < PAD, has_above, 1.0)
     keep = jnp.where(row_of_lane >= PAD + count, has_below, keep)
@@ -360,11 +414,10 @@
             hidden = hidden * has_below
         return hidden.astype(BF)
 
-    strip_memory = ends(cell_strip_ref[...]).astype(F32)
-    strip_hidden, strip_memory = update(ends(strip_gates_ref[...]) + strip_forcing, strip_memory)
+    strip_memory = cell_strip_ref[...].astype(F32)
+    strip_hidden, strip_memory = update(strip_gates_ref[...] + strip_forcing, strip_memory)
     strip_hidden = (strip_hidden * keep).astype(BF)
-    marks = patches_of(strip_hidden, tiles, 2, PAD + 1)
-    marks.update(patches_of(strip_hidden, tiles, count + PAD - 1, count + PAD + 2))
+    marks = edge_patches(strip_hidden, 2, PAD + 1, count)
 
     def taps(rows):
         return jnp.concatenate(rows, axis=0)
@@ -376,9 +429,9 @@
     group = edge_rows(count, -2, 3)
     olds = [above_ref[1, units:], above_ref[2, units:], rows_ref[0, units:]]
     olds += [rows_ref[count - 1, units:], below_ref[0, units:], below_ref[1, units:]]
-    for r, old in zip(group, olds):
+    for i, (r, old) in enumerate(zip(group, olds)):
         sums[r] = matmul(in_weight_ref[...], row_taps(f_three, r)) + bias
-        hidden, memory[r] = update(gates_ref[r - 2] + sums[r], old.astype(F32))
+        hidden, memory[r] = update(gates_ref[i] + sums[r], old.astype(F32))
         store_three(first, r, kept(hidden, r), marks[r])
     for i, r in enumerate(edge_rows(count, 1, 2)):
         first[r] = first_ref[i]
@@ -386,8 +439,7 @@
     strip_gates = matmul(weight_ref[...], strip_taps(strip_hidden)) + strip_forcing
     strip_hidden, strip_memory = update(strip_gates, strip_memory)
     strip_hidden = (strip_hidden * keep).astype(BF)
-    marks = patches_of(strip_hidden, tiles, 3, PAD + 2)
-    marks.update(patches_of(strip_hidden, tiles, count + PAD - 2, count + PAD + 1))
+    marks = edge_patches(strip_hidden, 3, PAD + 2, count)
     for r in edge_rows(count, -1, 3):
         hidden, memory[r] = update(sums[r] + matmul(weight_ref[...], row_taps(first, r)), memory[r])
         store_three(second, r, kept(hidden, r), marks[r])
@@ -469,17 +521,6 @@
     from_above = lax.ppermute(down, "lat", around(count))
     from_below = lax.ppermute(up, "lat", back(count))
     return from_above, from_below
-
-
-def marks_of(target, live_count, row_count):
-    cap = target.shape[1]
-    live = jnp.arange(cap, dtype=jnp.int32)[None, :] < live_count[:, None]
-    sides = jnp.arange(2, dtype=jnp.int32)
-    wanted = live[:, :, None] & (target[:, :, None] % 2 != sides)
-    row = jnp.where(wanted, target[:, :, None] // 2, -1)
-    row = jnp.repeat(row, 4, axis=2).reshape(target.shape[0], 8 * cap)
-    row = jnp.concatenate([row, row], axis=1)
-    return jnp.pad(row, ((0, 0), (0, LANES - row.shape[1])), constant_values=-1).astype(BF)
 
 
 def on_device(
@@ -513,30 +554,40 @@
     outgoing = pl.pallas_call(
         functools.partial(gather_kernel, ring),
         out_shape=message,
-        in_specs=scalars(1) + [pl.BlockSpec(memory_space=pl.ANY)] * 2,
+        in_specs=[pl.BlockSpec(memory_space=pl.ANY)] * 3,
         out_specs=pl.BlockSpec(memory_space=pl.ANY),
         scratch_shapes=[
             pltpu.VMEM(satellite_blocks.shape, BF),
             pltpu.VMEM((slots, band, block), BF),
             pltpu.VMEM(message.shape, BF),
+            pltpu.SMEM((cap, tiles), jnp.int32),
+            pltpu.SemaphoreType.DMA,
             pltpu.SemaphoreType.DMA,
             pltpu.SemaphoreType.DMA((groups,)),
             pltpu.SemaphoreType.DMA((groups,)),
         ],
-        compiler_params=pltpu.CompilerParams(vmem_limit_bytes=40 * 2**20),
+        compiler_params=pltpu.CompilerParams(vmem_limit_bytes=60 * 2**20),
         name="gather_band",
     )(slot_source[0].T, satellite_blocks, slot_weight.reshape(slots, band, block))
     incoming = lax.all_to_all(outgoing, ("lat", "lon"), split_axis=0, concat_axis=0, tiled=True)
 
-    rows, edge = call(
+    rows, edge = pl.pallas_call(
         prepare_kernel,
-        [
+        out_shape=(
             jax.ShapeDtypeStruct((row_count, 2 * units, column_count), BF),
             jax.ShapeDtypeStruct((2 * units + tiles, STRIP), BF),
-        ],
-        3, 0, [], "prepare", 1000,
-        (hidden_init, cell_init, marks_of(slot_target[0], tile_counts[0], row_count)),
-    )
+        ),
+        in_specs=[pl.BlockSpec(memory_space=pl.ANY)] * 2 + whole(2),
+        out_specs=tuple(whole(2)),
+        scratch_shapes=[
+            pltpu.VMEM(hidden_init.shape, BF),
+            pltpu.VMEM(cell_init.shape, BF),
+            pltpu.SemaphoreType.DMA,
+            pltpu.SemaphoreType.DMA,
+        ],
+        compiler_params=pltpu.CompilerParams(vmem_limit_bytes=60 * 2**20),
+        name="prepare",
+    )(hidden_init, cell_init, slot_target[0].T, tile_counts)
     from_left, from_right = exchange_columns(edge)
     ends = jax.ShapeDtypeStruct((4, 2 * units, column_count), BF)
     strip, up, down, marks = call(
@@ -550,26 +601,36 @@
         4, 0, [], "state_strips", 1000, (rows, edge, from_left, from_right),
     )
     above, below = exchange_rows(up, down)
-    extended = row_count + 4
     padded = row_count + 8
-    state_gates, strip_gates, cell_strip, bias = call(
+    state_gates, strip_gates, bias = call(
         state_kernel,
         [
-            jax.ShapeDtypeStruct((extended, gates, column_count), F32),
+            jax.ShapeDtypeStruct((row_count - 2, gates, column_count), F32),
             jax.ShapeDtypeStruct((gates, 2 * STRIP), F32),
-            jax.ShapeDtypeStruct((units, 2 * STRIP), BF),
             jax.ShapeDtypeStruct((gates, column_count), F32),
         ],
-        6, 1,
+        4, 0,
         [
             pltpu.VMEM((padded, 3 * units, column_count), BF),
             pltpu.VMEM((padded, units, LANES), BF),
         ],
-        "state_gates", 2 * gates * 9 * units * extended * column_count,
-        (flags, rows, strip, above, below, state_weight, bias),
-    )
-    incoming, state_gates, strip_gates, cell_strip, bias, in_weight = lax.optimization_barrier(
-        (incoming, state_gates, strip_gates, cell_strip, bias, in_weight)
+        "state_gates", 2 * gates * 9 * units * row_count * column_count,
+        (rows, strip, state_weight, bias), 16,
+    )
+    edge_gates, edge_strip_gates, cell_strip = call(
+        state_edge_kernel,
+        [
+            jax.ShapeDtypeStruct((6, gates, column_count), F32),
+            jax.ShapeDtypeStruct((gates, 4 * LANES), F32),
+            jax.ShapeDtypeStruct((units, 4 * LANES), BF),
+        ],
+        5, 1,
+        [pltpu.VMEM((padded, 3 * units, column_count), BF)],
+        "state_edges", 2 * gates * 9 * units * 8 * column_count,
+        (flags, rows, strip, above, below, state_weight),
+    )
+    incoming, state_gates, strip_gates, bias, in_weight = lax.optimization_barrier(
+        (incoming, state_gates, strip_gates, bias, in_weight)
     )
 
     ends = jax.ShapeDtypeStruct((4, channels, column_count), BF)
@@ -610,7 +671,7 @@
             pltpu.VMEM((padded, units, column_count), F32),
         ],
         "inner", 2 * gates * 9 * (channels + 2 * units) * row_count * column_count,
-        (state_gates, strip_gates, rows, cell_strip, forcing, forcing_strip, in_weight, state_weight, bias),
+        (state_gates, strip_gates, rows, strip, forcing, forcing_strip, in_weight, state_weight, bias), 24,
     )
     out = jax.ShapeDtypeStruct((units, row_count, column_count), BF)
     return call(
@@ -625,8 +686,8 @@
             pltpu.VMEM((row_count, units, column_count), BF),
         ],
         "edges", 2 * gates * 9 * (channels + 2 * units) * 6 * column_count,
-        (flags, state_gates, strip_gates, rows, above, below, cell_strip, forcing, forcing_strip,
-         f_above, f_below, in_weight, state_weight, bias, *inner),
+        (flags, edge_gates, edge_strip_gates, rows, above, below, cell_strip, forcing, forcing_strip,
+         f_above, f_below, in_weight, state_weight, bias, *inner), 16,
     )
 
 

time: 58.7 us -> 52.5 us (0.89)
  waiting for transfers between devices: 7.56 us -> 3.2 us
  other arithmetic: 1.7 us -> 0.25 us
  local copies, waits for them, and re-layouts: 11.3 us -> 10 us
  Pallas kernels: 18.9 us -> 20 us
    pallas_call x0 -> x1, Pallas kernels: none -> 3.11 us  [on_device(): pl.pallas_call(prepare_kernel, out_shape=(jax.ShapeDtypeStruct((row_count...]
    ppermute x2, waiting for transfers between devices: 2.84 us -> 0.01 us  [exchange_rows(): from_above = lax.ppermute(down, 'lat', around(count))]
    pallas_call x1, Pallas kernels: 6.16 us -> 3.93 us  [on_device(): pl.pallas_call(functools.partial(gather_kernel, ring), out_shape=message,...]
    ppermute x2, starting transfers between devices: 3.76 us -> 2.08 us  [exchange_rows(): from_above = lax.ppermute(down, 'lat', around(count))]
    ppermute x2, starting transfers between devices: 4.4 us -> 5.67 us  [exchange_rows(): from_below = lax.ppermute(up, 'lat', back(count))]
    unnamed x24, local copies, waits for them, and re-layouts: 11.1 us -> 9.89 us
    ppermute x2, waiting for transfers between devices: 2.11 us -> 1.18 us  [exchange_rows(): from_below = lax.ppermute(up, 'lat', back(count))]
    select_n x1 -> x0, other arithmetic: 0.69 us -> none  [marks_of(): wanted = live[:, :, None] & (target[:, :, None] % 2 != sides)]
  transfers between devices with their start and end apart: 7 -> 7, of which waited for: 3 -> 2; matrix products, arithmetic and copies ran while one was open for 6% -> 4% of each run, Pallas kernels for 13% -> 21%
where the time goes in v3:
time: 52.5 us; the launch traced here: 52 us
  Pallas kernels  20 us (38%)
  starting transfers between devices  17.8 us (34%)
  local copies, waits for them, and re-layouts  10 us (19%)
  waiting for transfers between devices  3.2 us (6%)
  between operations  0.81 us (2%)
    pallas_call x6, Pallas kernels, call(): pl.pallas_call(kernel, out_shape=tuple(outs), in_specs=scalars(scalar_cou...  12.9 us
    unnamed x24, local copies, waits for them, and re-layouts  9.89 us
    all_to_all x1, starting transfers between devices, on_device(): lax.all_to_all(outgoing, ('lat', 'lon'), split_axis=0, concat_axis=0, til...  7.3 us
    ppermute x2, starting transfers between devices, exchange_rows(): from_below = lax.ppermute(up, 'lat', back(count))  5.67 us
    pallas_call x1, Pallas kernels, on_device(): pl.pallas_call(functools.partial(gather_kernel, ring), out_shape=message,...  3.93 us
    pallas_call x1, Pallas kernels, on_device(): pl.pallas_call(prepare_kernel, out_shape=(jax.ShapeDtypeStruct((row_count...  3.11 us
    ppermute x1, starting transfers between devices, exchange_columns(): from_right = lax.ppermute(edge, 'lon', back(count))  2.39 us
    ppermute x2, starting transfers between devices, exchange_rows(): from_above = lax.ppermute(down, 'lat', around(count))  2.08 us
  transfers between devices with their start and end apart: 7, of which 2 were waited for; matrix products, arithmetic and copies ran while one was open for 4% of the time, Pallas kernels for 21%

profile of v3, /device:TPU:0, one launch (start us, length us, event | category | flops | bytes accessed | tf_op | source)
XLA Modules:
  0.0 52.0 jit_solution(1186875278868192599)
XLA Ops:
  0.6 0.0 copy-start.10
  0.6 3.9 %gather_band.1 = bf16[32,72,128]{2,1,0:T(8,128)(2,1)} custom-call(s32[4,32]{1,0:T(4,128)} %bitcast.14, bf16[128,16,128]{2,1,0:T(8,128)(2,1)} %blocks_hbm.1, bf16[128,8,128]{2,1,0:T(8,128)(2,1)} %bitcast.13), custom_call_target="tpu_custom_call" | custom-call | tf_op jit(solution)/shard_map/gather_band/pallas_call | solution.py:554
  4.6 0.0 copy-start.8
  4.6 0.0 copy-start.9
  4.6 7.3 %all-to-all-start = ((bf16[32,72,128]{2,1,0:T(8,128)(2,1)}), bf16[32,72,128]{2,1,0:T(8,128)(2,1)S(1)}, u32[]{:S(2)}, u32[]{:S(2)}) async-start(bf16[32,72,128]{2,1,0:T(8,128)(2,1)} %gather_band.1), calls=%async_computation | async-start | bytes 1179648 | tf_op jit(solution)/shard_map/all_to_all | solution.py:572
  11.9 3.1 %prepare.1 = (bf16[32,64,256]{2,1,0:T(8,128)(2,1)}, bf16[96,384]{1,0:T(8,128)(2,1)}) custom-call(bf16[32,32,256]{2,1,0:T(8,128)(2,1)} %hidden_hbm.1, bf16[32,32,256]{2,1,0:T(8,128)(2,1)} %cell_hbm.1, s32[4,32]{1,0:T(4,128)} %bitcast.11, s32[1,32]{1,0:T(1,128)} %count_ref.3), custom_call_target="tpu_custom_call" | custom-call | tf_op jit(solution)/shard_map/prepare/pallas_call | solution.py:574
  15.0 0.3 collective-permute-start
  15.3 2.4 %collective-permute-start.1 = (bf16[96,384]{1,0:T(8,128)(2,1)}, bf16[96,384]{1,0:T(8,128)(2,1)S(1)}, u32[]{:S(2)}, u32[]{:S(2)}) collective-permute-start(bf16[96,384]{1,0:T(8,128)(2,1)} %get-tuple-element.30.edge_ref), channel_id=1, source_target_pairs={{1,0},{2,1},{3,2},{4,3},{5,4},{6,5},{7,6},{0,7},{9,8},{10,9},{11,1... | collective-permute-start | bytes 221192 | tf_op jit(solution)/shard_map/ppermute | solution.py:515
  17.7 1.0 %copy.12 = bf16[128,288]{1,0:T(8,128)(2,1)S(1)} copy(bf16[128,288]{0,1:T(8,128)(2,1)} %param.16) | data formatting | bytes 147456 | tf_op args[6]
  18.7 0.9 %copy.14 = bf16[128,144]{1,0:T(8,128)(2,1)S(1)} copy(bf16[128,144]{0,1:T(8,128)(2,1)} %param.15) | data formatting | bytes 73728 | tf_op args[5]
  19.6 0.1 broadcast_multiply_fusion.1.in_weight_ref
  19.7 0.1 broadcast_multiply_fusion.weight_ref
  19.8 0.0 copy-done.10
  19.8 0.1 copy.13.bias_ref
  19.9 2.0 %collective-permute-done.left_ref = bf16[96,384]{1,0:T(8,128)(2,1)S(1)} collective-permute-done((bf16[96,384]{1,0:T(8,128)(2,1)}, bf16[96,384]{1,0:T(8,128)(2,1)S(1)}, u32[]{:S(2)}, u32[]{:S(2)}) %collective-permute-start) | collective-permute-done | bytes 73760 | tf_op jit(solution)/shard_map/ppermute | solution.py:514
  21.9 0.0 collective-permute-done.1.right_ref
  21.9 0.0 copy-start
  21.9 1.2 %copy-done = bf16[32,64,256]{2,1,0:T(8,128)(2,1)S(1)} copy-done((bf16[32,64,256]{2,1,0:T(8,128)(2,1)S(1)}, bf16[32,64,256]{2,1,0:T(8,128)(2,1)}, u32[]{:S(2)}) %copy-start) | copy-done | bytes 1048600
  23.2 0.0 copy-start.7
  23.2 0.9 %copy-done.7 = bf16[96,384]{1,0:T(8,128)(2,1)S(1)} copy-done((bf16[96,384]{1,0:T(8,128)(2,1)S(1)}, bf16[96,384]{1,0:T(8,128)(2,1)}, u32[]{:S(2)}) %copy-start.7) | copy-done | bytes 73752
  24.1 0.0 copy-start.2
  24.1 1.5 %collective-permute-start.2 = (bf16[4,64,256]{2,1,0:T(8,128)(2,1)S(1)}, bf16[4,64,256]{2,1,0:T(8,128)(2,1)S(1)}, u32[]{:S(2)}, u32[]{:S(2)}) collective-permute-start(bf16[4,64,256]{2,1,0:T(8,128)(2,1)S(1)} %get-tuple-element.32), channel_id=1, source_target_pairs={{0,8},{8,16},{16,24},{24,0},{1,9},{9,17},{17,25},{25,1},{2,10},{10... | collective-permute-start | bytes 393224 | tf_op jit(solution)/shard_map/ppermute | solution.py:521
  25.6 2.4 %collective-permute-start.3 = (bf16[4,64,256]{2,1,0:T(8,128)(2,1)S(1)}, bf16[4,64,256]{2,1,0:T(8,128)(2,1)S(1)}, u32[]{:S(2)}, u32[]{:S(2)}) collective-permute-start(bf16[4,64,256]{2,1,0:T(8,128)(2,1)S(1)} %get-tuple-element.33), channel_id=1, source_target_pairs={{8,0},{16,8},{24,16},{0,24},{9,1},{17,9},{25,17},{1,25},{10,2},{18... | collective-permute-start | bytes 393224 | tf_op jit(solution)/shard_map/ppermute | solution.py:522
  28.0 0.1 add_convert_fusion.flag_ref
  28.1 0.0 copy-start.1
  28.1 1.2 %copy-done.1 = bf16[32,64,256]{2,1,0:T(8,128)(2,1)S(1)} copy-done((bf16[32,64,256]{2,1,0:T(8,128)(2,1)S(1)}, bf16[32,64,256]{2,1,0:T(8,128)(2,1)}, u32[]{:S(2)}) %copy-start.1) | copy-done | bytes 1048600
  29.3 1.9 %state_gates.1 = (f32[30,128,256]{2,1,0:T(8,128)S(1)}, f32[128,768]{1,0:T(8,128)S(1)}, f32[128,256]{1,0:T(8,128)S(1)}) custom-call(bf16[32,64,256]{2,1,0:T(8,128)(2,1)S(1)} %copy-done.1, bf16[64,768]{1,0:T(8,128)(2,1)S(1)} %get-tuple-element.31.strip_ref, bf16[128,288]{1,0:T(8,128)(2,1)S(1)} %broadcast_multiply_fusion.weight_ref, f32[128,1]{1,0:T(8,128)S(1)} %copy.13.bias_ref), custom_call_target="tpu_custom_call" | custom-call | flops 603979776 | bytes 5677568 | tf_op jit(solution)/shard_map/state_gates/pallas_call | solution.py:33
  31.2 0.0 copy-start.3
  31.2 1.9 %copy-done.3 = f32[30,128,256]{2,1,0:T(8,128)} copy-done((f32[30,128,256]{2,1,0:T(8,128)}, f32[30,128,256]{2,1,0:T(8,128)S(1)}, u32[]{:S(2)}) %copy-start.3) | copy-done | bytes 3932184
  33.1 0.0 collective-permute-done.2.above_ref
  33.1 1.2 %collective-permute-done.3.below_ref = bf16[4,64,256]{2,1,0:T(8,128)(2,1)S(1)} collective-permute-done((bf16[4,64,256]{2,1,0:T(8,128)(2,1)S(1)}, bf16[4,64,256]{2,1,0:T(8,128)(2,1)S(1)}, u32[]{:S(2)}, u32[]{:S(2)}) %collective-permute-start.3) | collective-permute-done | bytes 131104 | tf_op jit(solution)/shard_map/ppermute | solution.py:522
  34.2 1.2 %state_edges.1 = (f32[6,128,256]{2,1,0:T(8,128)S(1)}, f32[128,512]{1,0:T(8,128)S(1)}, bf16[32,512]{1,0:T(8,128)(2,1)S(1)}) custom-call(s32[2]{0:T(128)S(1)} %add_convert_fusion.flag_ref, bf16[32,64,256]{2,1,0:T(8,128)(2,1)S(1)} %copy-done.1, bf16[64,768]{1,0:T(8,128)(2,1)S(1)} %get-tuple-element.31.strip_ref, ...), custom_call_target="tpu_custom_call" | custom-call | flops 150994944 | bytes 2564104 | tf_op jit(solution)/shard_map/state_edges/pallas_call | solution.py:33
  35.5 0.0 copy-start.5
  35.5 0.7 %copy-done.5 = f32[128,512]{1,0:T(8,128)} copy-done((f32[128,512]{1,0:T(8,128)}, f32[128,512]{1,0:T(8,128)S(1)}, u32[]{:S(2)}) %copy-start.5) | copy-done | bytes 262168
  36.2 0.0 all-to-all-done.incoming_ref
  36.2 0.0 copy-start.6
  36.2 0.0 copy-done.8
  36.2 0.0 copy-done.9
  36.2 1.8 %scatter_add.1 = (bf16[32,16,256]{2,1,0:T(8,128)(2,1)S(1)}, bf16[16,768]{1,0:T(8,128)(2,1)S(1)}, bf16[4,16,256]{2,1,0:T(8,128)(2,1)S(1)}, bf16[4,16,256]{2,1,0:T(8,128)(2,1)S(1)}) custom-call(s32[4,32]{1,0:T(4,128)S(1)} %bitcast.12, s32[1,32]{1,0:T(1,128)S(1)} %copy-done.9, bf16[32,72,128]{2,1,0:T(8,128)(2,1)S(1)} %all-to-all-done.incoming_ref, ...), custom_call_target="tpu_custom_call" | custom-call | flops 262144 | bytes 959104 | tf_op jit(solution)/shard_map/scatter_add/pallas_call | solution.py:33
  38.0 0.6 %collective-permute-start.4 = (bf16[4,16,256]{2,1,0:T(8,128)(2,1)S(1)}, bf16[4,16,256]{2,1,0:T(8,128)(2,1)S(1)}, u32[]{:S(2)}, u32[]{:S(2)}) collective-permute-start(bf16[4,16,256]{2,1,0:T(8,128)(2,1)S(1)} %get-tuple-element.44), channel_id=1, source_target_pairs={{0,8},{8,16},{16,24},{24,0},{1,9},{9,17},{17,25},{25,1},{2,10},{10... | collective-permute-start | bytes 98312 | tf_op jit(solution)/shard_map/ppermute | solution.py:521
  38.6 3.3 %collective-permute-start.5 = (bf16[4,16,256]{2,1,0:T(8,128)(2,1)S(1)}, bf16[4,16,256]{2,1,0:T(8,128)(2,1)S(1)}, u32[]{:S(2)}, u32[]{:S(2)}) collective-permute-start(bf16[4,16,256]{2,1,0:T(8,128)(2,1)S(1)} %get-tuple-element.45), channel_id=1, source_target_pairs={{8,0},{16,8},{24,16},{0,24},{9,1},{17,9},{25,17},{1,25},{10,2},{18... | collective-permute-start | bytes 98312 | tf_op jit(solution)/shard_map/ppermute | solution.py:522
  41.9 0.0 copy-done.2
  41.9 0.0 copy-start.4
  41.9 2.1 %copy-done.4 = f32[30,128,256]{2,1,0:T(8,128)S(1)} copy-done((f32[30,128,256]{2,1,0:T(8,128)S(1)}, f32[30,128,256]{2,1,0:T(8,128)}, u32[]{:S(2)}) %copy-start.4) | copy-done | bytes 3932184
  44.0 4.9 %inner.1 = (bf16[26,32,256]{2,1,0:T(8,128)(2,1)S(1)}, bf16[26,32,256]{2,1,0:T(8,128)(2,1)S(1)}, f32[4,128,256]{2,1,0:T(8,128)S(1)}, bf16[4,96,256]{2,1,0:T(8,128...) custom-call(f32[30,128,256]{2,1,0:T(8,128)S(1)} %copy-done.4, ...), custom_call_target="tpu_custom_call" | custom-call | flops 1509949440 | bytes 7901184 | tf_op jit(solution)/shard_map/inner/pallas_call | solution.py:33
  48.9 0.0 collective-permute-done.4.f_above_ref
  48.9 0.0 collective-permute-done.5.f_below_ref
  48.9 0.0 copy-done.6
  48.9 3.1 %edges.1 = (bf16[32,32,256]{2,1,0:T(8,128)(2,1)}, bf16[32,32,256]{2,1,0:T(8,128)(2,1)}) custom-call(s32[2]{0:T(128)S(1)} %add_convert_fusion.flag_ref, f32[6,128,256]{2,1,0:T(8,128)S(1)} %get-tuple-element.34.gates_ref, f32[128,512]{1,0:T(8,128)S(1)} %copy-done.6, bf16[32,64,256]{2,1,0:T(8,128)(2,1)S(1)} %copy-done.2, ...), custom_call_target="tpu_custom_call" | custom-call | flops 283115520 | bytes 5935112 | tf_op jit(solution)/shard_map/edges/pallas_call | solution.py:33
  (3 shorter events, 0.0 us)
Async XLA Ops:
  0.6 19.2 %copy-start.10 = (f32[128]{0:T(128)S(1)}, f32[128]{0:T(128)}, u32[]{:S(2)}) copy-start(f32[128]{0:T(128)} %param.17) | copy-start | bytes 1540
  4.6 31.6 %copy-start.8 = (s32[1,32,4]{1,2,0:T(4,128)S(1)}, s32[1,32,4]{1,2,0:T(4,128)}, u32[]{:S(2)}) copy-start(s32[1,32,4]{1,2,0:T(4,128)} %param.13) | copy-start | bytes 1540
  4.6 31.6 %copy-start.9 = (s32[1,32]{1,0:T(1,128)S(1)}, s32[1,32]{1,0:T(1,128)}, u32[]{:S(2)}) copy-start(s32[1,32]{1,0:T(1,128)} %count_ref.3) | copy-start | bytes 388
  4.6 31.6 %all-to-all-start = ((bf16[32,72,128]{2,1,0:T(8,128)(2,1)}), bf16[32,72,128]{2,1,0:T(8,128)(2,1)S(1)}, u32[]{:S(2)}, u32[]{:S(2)}) async-start(bf16[32,72,128]{2,1,0:T(8,128)(2,1)} %gather_band.1), calls=%async_computation | async-start | bytes 1179648 | tf_op jit(solution)/shard_map/all_to_all | solution.py:572
  15.0 6.9 %collective-permute-start = (bf16[96,384]{1,0:T(8,128)(2,1)}, bf16[96,384]{1,0:T(8,128)(2,1)S(1)}, u32[]{:S(2)}, u32[]{:S(2)}) collective-permute-start(bf16[96,384]{1,0:T(8,128)(2,1)} %get-tuple-element.30.edge_ref), channel_id=1, source_target_pairs={{0,1},{1,2},{2,3},{3,4},{4,5},{5,6},{6,7},{7,0},{8,9},{9,10},{10,1... | collective-permute-start | bytes 221192 | tf_op jit(solution)/shard_map/ppermute | solution.py:514
  15.3 6.6 %collective-permute-start.1 = (bf16[96,384]{1,0:T(8,128)(2,1)}, bf16[96,384]{1,0:T(8,128)(2,1)S(1)}, u32[]{:S(2)}, u32[]{:S(2)}) collective-permute-start(bf16[96,384]{1,0:T(8,128)(2,1)} %get-tuple-element.30.edge_ref), channel_id=1, source_target_pairs={{1,0},{2,1},{3,2},{4,3},{5,4},{6,5},{7,6},{0,7},{9,8},{10,9},{11,1... | collective-permute-start | bytes 221192 | tf_op jit(solution)/shard_map/ppermute | solution.py:515
  21.9 1.2 %copy-start = (bf16[32,64,256]{2,1,0:T(8,128)(2,1)S(1)}, bf16[32,64,256]{2,1,0:T(8,128)(2,1)}, u32[]{:S(2)}) copy-start(bf16[32,64,256]{2,1,0:T(8,128)(2,1)} %get-tuple-element.29.rows_ref) | copy-start | bytes 3145732
  23.2 0.9 %copy-start.7 = (bf16[96,384]{1,0:T(8,128)(2,1)S(1)}, bf16[96,384]{1,0:T(8,128)(2,1)}, u32[]{:S(2)}) copy-start(bf16[96,384]{1,0:T(8,128)(2,1)} %get-tuple-element.30.edge_ref) | copy-start | bytes 221188
  24.1 17.8 %copy-start.2 = (bf16[32,64,256]{2,1,0:T(8,128)(2,1)S(1)}, bf16[32,64,256]{2,1,0:T(8,128)(2,1)}, u32[]{:S(2)}) copy-start(bf16[32,64,256]{2,1,0:T(8,128)(2,1)} %get-tuple-element.29.rows_ref) | copy-start | bytes 3145732
  24.1 9.0 %collective-permute-start.2 = (bf16[4,64,256]{2,1,0:T(8,128)(2,1)S(1)}, bf16[4,64,256]{2,1,0:T(8,128)(2,1)S(1)}, u32[]{:S(2)}, u32[]{:S(2)}) collective-permute-start(bf16[4,64,256]{2,1,0:T(8,128)(2,1)S(1)} %get-tuple-element.32), channel_id=1, source_target_pairs={{0,8},{8,16},{16,24},{24,0},{1,9},{9,17},{17,25},{25,1},{2,10},{10... | collective-permute-start | bytes 393224 | tf_op jit(solution)/shard_map/ppermute | solution.py:521
  25.6 8.6 %collective-permute-start.3 = (bf16[4,64,256]{2,1,0:T(8,128)(2,1)S(1)}, bf16[4,64,256]{2,1,0:T(8,128)(2,1)S(1)}, u32[]{:S(2)}, u32[]{:S(2)}) collective-permute-start(bf16[4,64,256]{2,1,0:T(8,128)(2,1)S(1)} %get-tuple-element.33), channel_id=1, source_target_pairs={{8,0},{16,8},{24,16},{0,24},{9,1},{17,9},{25,17},{1,25},{10,2},{18... | collective-permute-start | bytes 393224 | tf_op jit(solution)/shard_map/ppermute | solution.py:522
  28.1 1.2 %copy-start.1 = (bf16[32,64,256]{2,1,0:T(8,128)(2,1)S(1)}, bf16[32,64,256]{2,1,0:T(8,128)(2,1)}, u32[]{:S(2)}) copy-start(bf16[32,64,256]{2,1,0:T(8,128)(2,1)} %get-tuple-element.29.rows_ref) | copy-start | bytes 3145732
  31.2 1.9 %copy-start.3 = (f32[30,128,256]{2,1,0:T(8,128)}, f32[30,128,256]{2,1,0:T(8,128)S(1)}, u32[]{:S(2)}) copy-start(f32[30,128,256]{2,1,0:T(8,128)S(1)} %get-tuple-element.48.gates_ref) | copy-start | bytes 11796484
  35.5 0.7 %copy-start.5 = (f32[128,512]{1,0:T(8,128)}, f32[128,512]{1,0:T(8,128)S(1)}, u32[]{:S(2)}) copy-start(f32[128,512]{1,0:T(8,128)S(1)} %get-tuple-element.35.strip_gates_ref) | copy-start | bytes 786436
  36.2 12.7 %copy-start.6 = (f32[128,512]{1,0:T(8,128)S(1)}, f32[128,512]{1,0:T(8,128)}, u32[]{:S(2)}) copy-start(f32[128,512]{1,0:T(8,128)} %copy-done.5) | copy-start | bytes 786436
  38.0 10.9 %collective-permute-start.4 = (bf16[4,16,256]{2,1,0:T(8,128)(2,1)S(1)}, bf16[4,16,256]{2,1,0:T(8,128)(2,1)S(1)}, u32[]{:S(2)}, u32[]{:S(2)}) collective-permute-start(bf16[4,16,256]{2,1,0:T(8,128)(2,1)S(1)} %get-tuple-element.44), channel_id=1, source_target_pairs={{0,8},{8,16},{16,24},{24,0},{1,9},{9,17},{17,25},{25,1},{2,10},{10... | collective-permute-start | bytes 98312 | tf_op jit(solution)/shard_map/ppermute | solution.py:521
  38.6 10.3 %collective-permute-start.5 = (bf16[4,16,256]{2,1,0:T(8,128)(2,1)S(1)}, bf16[4,16,256]{2,1,0:T(8,128)(2,1)S(1)}, u32[]{:S(2)}, u32[]{:S(2)}) collective-permute-start(bf16[4,16,256]{2,1,0:T(8,128)(2,1)S(1)} %get-tuple-element.45), channel_id=1, source_target_pairs={{8,0},{16,8},{24,16},{0,24},{9,1},{17,9},{25,17},{1,25},{10,2},{18... | collective-permute-start | bytes 98312 | tf_op jit(solution)/shard_map/ppermute | solution.py:522
  41.9 2.1 %copy-start.4 = (f32[30,128,256]{2,1,0:T(8,128)S(1)}, f32[30,128,256]{2,1,0:T(8,128)}, u32[]{:S(2)}) copy-start(f32[30,128,256]{2,1,0:T(8,128)} %copy-done.3) | copy-start | bytes 11796484

commit v4 on v3

--- a/solution.py
+++ b/solution.py
@@ -12,6 +12,7 @@
 LANES = 128
 STRIP = 3 * LANES
 BATCH = 2
+PIECE = 6
 BF = jnp.bfloat16
 F32 = jnp.float32
 
@@ -24,17 +25,23 @@
     return [pl.BlockSpec(memory_space=pltpu.VMEM)] * count
 
 
+def in_hbm(x):
+    return pltpu.with_memory_space_constraint(x, pltpu.HBM)
+
+
 def scalars(count):
     return [pl.BlockSpec(memory_space=pltpu.SMEM)] * count
 
 
-def call(kernel, outs, ins, scalar_count, scratch, name, flops, args, mib=8):
-    nbytes = sum(a.size * a.dtype.itemsize for a in list(args) + list(outs))
+def call(
+    kernel, outs, ins, scalar_count, scratch, name, flops, args, mib=8, in_specs=None, out_specs=None
+):
+    nbytes = sum(a.size * a.dtype.itemsize for a in args)
     return pl.pallas_call(
         kernel,
         out_shape=tuple(outs),
-        in_specs=scalars(scalar_count) + whole(ins),
-        out_specs=tuple(whole(len(outs))),
+        in_specs=in_specs or scalars(scalar_count) + whole(ins),
+        out_specs=tuple(out_specs or whole(len(outs))),
         scratch_shapes=scratch,
         compiler_params=pltpu.CompilerParams(vmem_limit_bytes=mib * 2**20),
         cost_estimate=pl.CostEstimate(flops=flops, bytes_accessed=nbytes, transcendentals=0),
@@ -246,7 +253,7 @@
 
 def state_kernel(
     rows_ref, strip_ref, weight_ref, bias_ref,
-    gates_ref, strip_gates_ref, wide_bias_ref, three, patches,
+    gates_hbm, strip_gates_ref, wide_bias_ref, gates, three, patches, sems,
 ):
     units = rows_ref.shape[1] // 2
     count = rows_ref.shape[0]
@@ -256,8 +263,19 @@
     store_patches(strip, patches, PAD, count + PAD)
     for y in range(count):
         store_three(three, y + PAD, rows_ref[y, :units], patches[y + PAD])
+    sends = pieces(gates, gates_hbm, sems)
     for y in range(1, count - 1):
-        gates_ref[y - 1] = matmul(weight_ref[...], row_taps(three, y + PAD))
+        gates[y - 1] = matmul(weight_ref[...], row_taps(three, y + PAD))
+        if y % PIECE == 0:
+            sends[y // PIECE - 1].start()
+    for send in sends:
+        send.wait()
+
+
+def pieces(source, target, sems):
+    count = source.shape[0] // PIECE
+    spots = [pl.ds(i * PIECE, PIECE) for i in range(count)]
+    return [pltpu.make_async_copy(source.at[s], target.at[s], sems.at[i]) for i, s in enumerate(spots)]
 
 
 def ends_of(strip):
@@ -304,14 +322,17 @@
 
 
 def inner_kernel(
-    gates_ref, strip_gates_ref, rows_ref, strip_ref, forcing_ref, forcing_strip_ref,
+    gates_hbm, strip_gates_ref, rows_ref, strip_ref, forcing_ref, forcing_strip_ref,
     in_weight_ref, weight_ref, bias_ref,
     hidden_ref, cell_ref, sums_ref, first_ref, second_ref, memory_ref,
-    f_three, f_patches, f_gates, first, second, patches, memory,
+    gates, f_three, f_patches, f_gates, first, second, patches, memory, sems,
 ):
     units = rows_ref.shape[1] // 2
     count = rows_ref.shape[0]
     bias = bias_ref[...]
+    fetches = pieces(gates_hbm, gates, sems)
+    for fetch in fetches:
+        fetch.start()
 
     strip = forcing_strip_ref[...]
     strip_forcing = matmul(in_weight_ref[...], strip_taps(strip)) + jnp.concatenate([bias] * 3, axis=1)
@@ -330,9 +351,12 @@
             body(range(start, min(start + BATCH, stop)))
 
     def first_rows(group):
+        for r in group:
+            if (r - PAD - 1) % PIECE == 0:
+                fetches[(r - PAD - 1) // PIECE].wait()
         sums = [matmul(in_weight_ref[...], row_taps(f_three, r)) + bias for r in group]
         states = [
-            update(gates_ref[r - PAD - 1] + s, rows_ref[r - PAD, units:].astype(F32)) for r, s in zip(group, sums)
+            update(gates[r - PAD - 1] + s, rows_ref[r - PAD, units:].astype(F32)) for r, s in zip(group, sums)
         ]
         marks = [patches[r] for r in group]
         for r, s, (hidden, new), mark in zip(group, sums, states, marks):
@@ -553,7 +577,7 @@
     groups = tiles // ring
     outgoing = pl.pallas_call(
         functools.partial(gather_kernel, ring),
-        out_shape=message,
+        out_shape=pltpu.HBM(message.shape, BF),
         in_specs=[pl.BlockSpec(memory_space=pl.ANY)] * 3,
         out_specs=pl.BlockSpec(memory_space=pl.ANY),
         scratch_shapes=[
@@ -566,9 +590,9 @@
             pltpu.SemaphoreType.DMA((groups,)),
             pltpu.SemaphoreType.DMA((groups,)),
         ],
-        compiler_params=pltpu.CompilerParams(vmem_limit_bytes=60 * 2**20),
+        compiler_params=pltpu.CompilerParams(vmem_limit_bytes=8 * 2**20),
         name="gather_band",
-    )(slot_source[0].T, satellite_blocks, slot_weight.reshape(slots, band, block))
+    )(in_hbm(slot_source[0].T), in_hbm(satellite_blocks), in_hbm(slot_weight.reshape(slots, band, block)))
     incoming = lax.all_to_all(outgoing, ("lat", "lon"), split_axis=0, concat_axis=0, tiled=True)
 
     rows, edge = pl.pallas_call(
@@ -585,9 +609,9 @@
             pltpu.SemaphoreType.DMA,
             pltpu.SemaphoreType.DMA,
         ],
-        compiler_params=pltpu.CompilerParams(vmem_limit_bytes=60 * 2**20),
+        compiler_params=pltpu.CompilerParams(vmem_limit_bytes=8 * 2**20),
         name="prepare",
-    )(hidden_init, cell_init, slot_target[0].T, tile_counts)
+    )(in_hbm(hidden_init), in_hbm(cell_init), slot_target[0].T, tile_counts)
     from_left, from_right = exchange_columns(edge)
     ends = jax.ShapeDtypeStruct((4, 2 * units, column_count), BF)
     strip, up, down, marks = call(
@@ -602,20 +626,25 @@
     )
     above, below = exchange_rows(up, down)
     padded = row_count + 8
+    inside = (row_count - 2, gates, column_count)
+    parts = inside[0] // PIECE
     state_gates, strip_gates, bias = call(
         state_kernel,
         [
-            jax.ShapeDtypeStruct((row_count - 2, gates, column_count), F32),
+            pltpu.HBM(inside, F32),
             jax.ShapeDtypeStruct((gates, 2 * STRIP), F32),
             jax.ShapeDtypeStruct((gates, column_count), F32),
         ],
         4, 0,
         [
+            pltpu.VMEM(inside, F32),
             pltpu.VMEM((padded, 3 * units, column_count), BF),
             pltpu.VMEM((padded, units, LANES), BF),
+            pltpu.SemaphoreType.DMA((parts,)),
         ],
         "state_gates", 2 * gates * 9 * units * row_count * column_count,
         (rows, strip, state_weight, bias), 16,
+        out_specs=[pl.BlockSpec(memory_space=pl.ANY)] + whole(2),
     )
     edge_gates, edge_strip_gates, cell_strip = call(
         state_edge_kernel,
@@ -662,6 +691,7 @@
         ],
         9, 0,
         [
+            pltpu.VMEM(inside, F32),
             pltpu.VMEM((padded, 3 * channels, column_count), BF),
             pltpu.VMEM((padded, channels, LANES), BF),
             pltpu.VMEM((padded, gates, column_count), F32),
@@ -669,9 +699,11 @@
             pltpu.VMEM((padded, 3 * units, column_count), BF),
             pltpu.VMEM((padded, units, LANES), BF),
             pltpu.VMEM((padded, units, column_count), F32),
+            pltpu.SemaphoreType.DMA((parts,)),
         ],
         "inner", 2 * gates * 9 * (channels + 2 * units) * row_count * column_count,
-        (state_gates, strip_gates, rows, strip, forcing, forcing_strip, in_weight, state_weight, bias), 24,
+        (in_hbm(state_gates), strip_gates, rows, strip, forcing, forcing_strip, in_weight, state_weight, bias), 24,
+        in_specs=[pl.BlockSpec(memory_space=pl.ANY)] + whole(8),
     )
     out = jax.ShapeDtypeStruct((units, row_count, column_count), BF)
     return call(

time: 52.5 us -> 49.9 us (0.950)
  local copies, waits for them, and re-layouts: 10 us -> 4.03 us
  waiting for transfers between devices: 3.2 us -> 6.76 us
    unnamed x24 -> x16, local copies, waits for them, and re-layouts: 9.89 us -> 3.92 us
    ppermute x2, waiting for transfers between devices: 1.18 us -> 3.36 us  [exchange_rows(): from_below = lax.ppermute(up, 'lat', back(count))]
    pallas_call x1, Pallas kernels: 3.11 us -> 1.51 us  [on_device(): pl.pallas_call(prepare_kernel, out_shape=(jax.ShapeDtypeStruct((row_count...]
    pallas_call x7, Pallas kernels: 16.9 us -> 18.4 us  [the longest x6 14.5 us: call(): pl.pallas_call(kernel, out_shape=tuple(outs), in_specs=in_specs or scalar...]
    ppermute x2, waiting for transfers between devices: 0.01 us -> 1.36 us  [exchange_rows(): from_above = lax.ppermute(down, 'lat', around(count))]
    ppermute x2, starting transfers between devices: 2.08 us -> 2.79 us  [exchange_rows(): from_above = lax.ppermute(down, 'lat', around(count))]
    ppermute x2, starting transfers between devices: 5.67 us -> 4.96 us  [exchange_rows(): from_below = lax.ppermute(up, 'lat', back(count))]
  transfers between devices with their start and end apart: 7 -> 7, of which waited for: 2 -> 3; matrix products, arithmetic and copies ran while one was open for 4% -> 5% of each run, Pallas kernels for 21% -> 22%
where the time goes in v4:
time: 49.9 us; the launch traced here: 49.5 us
  Pallas kernels  19.9 us (40%)
  starting transfers between devices  17.8 us (36%)
  waiting for transfers between devices  6.76 us (14%)
  local copies, waits for them, and re-layouts  4.03 us (8%)
  between operations  0.82 us (2%)
    pallas_call x6, Pallas kernels, call(): pl.pallas_call(kernel, out_shape=tuple(outs), in_specs=in_specs or scalar...  14.5 us
    all_to_all x1, starting transfers between devices, on_device(): lax.all_to_all(outgoing, ('lat', 'lon'), split_axis=0, concat_axis=0, til...  7.3 us
    ppermute x2, starting transfers between devices, exchange_rows(): from_below = lax.ppermute(up, 'lat', back(count))  4.96 us
    pallas_call x1, Pallas kernels, on_device(): pl.pallas_call(functools.partial(gather_kernel, ring), out_shape=pltpu.HB...  3.93 us
    unnamed x16, local copies, waits for them, and re-layouts  3.92 us
    ppermute x2, waiting for transfers between devices, exchange_rows(): from_below = lax.ppermute(up, 'lat', back(count))  3.36 us
    ppermute x2, starting transfers between devices, exchange_rows(): from_above = lax.ppermute(down, 'lat', around(count))  2.79 us
    ppermute x1, starting transfers between devices, exchange_columns(): from_right = lax.ppermute(edge, 'lon', back(count))  2.39 us
  transfers between devices with their start and end apart: 7, of which 3 were waited for; matrix products, arithmetic and copies ran while one was open for 5% of the time, Pallas kernels for 22%

profile of v4, /device:TPU:0, one launch (start us, length us, event | category | flops | bytes accessed | tf_op | source)
XLA Modules:
  0.0 49.5 jit_solution(9375426555167715072)
XLA Ops:
  0.6 0.0 copy-start.6
  0.6 3.9 %gather_band.1 = bf16[32,72,128]{2,1,0:T(8,128)(2,1)} custom-call(s32[4,32]{1,0:T(4,128)} %bitcast.14, bf16[128,16,128]{2,1,0:T(8,128)(2,1)} %blocks_hbm.1, bf16[128,8,128]{2,1,0:T(8,128)(2,1)} %bitcast.13), custom_call_target="tpu_custom_call" | custom-call | tf_op jit(solution)/shard_map/gather_band/pallas_call | solution.py:578
  4.6 0.0 copy-start.3
  4.6 0.0 copy-start.5
  4.6 7.3 %all-to-all-start = ((bf16[32,72,128]{2,1,0:T(8,128)(2,1)}), bf16[32,72,128]{2,1,0:T(8,128)(2,1)S(1)}, u32[]{:S(2)}, u32[]{:S(2)}) async-start(bf16[32,72,128]{2,1,0:T(8,128)(2,1)} %gather_band.1), calls=%async_computation | async-start | bytes 1179648 | tf_op jit(solution)/shard_map/all_to_all | solution.py:596
  11.9 0.0 copy-start.2
  11.9 0.7 %copy-done.2 = s32[1,32,4]{1,2,0:T(4,128)S(1)} copy-done((s32[1,32,4]{1,2,0:T(4,128)S(1)}, s32[1,32,4]{1,2,0:T(4,128)}, u32[]{:S(2)}) %copy-start.2) | copy-done | bytes 536
  12.6 0.0 copy-start.4
  12.6 0.7 %copy-done.4 = s32[1,32]{1,0:T(1,128)S(1)} copy-done((s32[1,32]{1,0:T(1,128)S(1)}, s32[1,32]{1,0:T(1,128)}, u32[]{:S(2)}) %copy-start.4) | copy-done | bytes 152
  13.3 1.5 %prepare.1 = (bf16[32,64,256]{2,1,0:T(8,128)(2,1)S(1)}, bf16[96,384]{1,0:T(8,128)(2,1)S(1)}) custom-call(bf16[32,32,256]{2,1,0:T(8,128)(2,1)} %hidden_hbm.1, bf16[32,32,256]{2,1,0:T(8,128)(2,1)} %cell_hbm.1, s32[4,32]{1,0:T(4,128)S(1)} %bitcast.11, s32[1,32]{1,0:T(1,128)S(1)} %copy-done.4), custom_call_target="tpu_custom_call" | custom-call | tf_op jit(solution)/shard_map/prepare/pallas_call | solution.py:598
  14.8 0.3 collective-permute-start
  15.1 2.4 %collective-permute-start.1 = (bf16[96,384]{1,0:T(8,128)(2,1)S(1)}, bf16[96,384]{1,0:T(8,128)(2,1)S(1)}, u32[]{:S(2)}, u32[]{:S(2)}) collective-permute-start(bf16[96,384]{1,0:T(8,128)(2,1)S(1)} %get-tuple-element.30.edge_ref), channel_id=1, source_target_pairs={{1,0},{2,1},{3,2},{4,3},{5,4},{6,5},{7,6},{0,7},{9,8},{10,9},{11,1... | collective-permute-start | bytes 221192 | tf_op jit(solution)/shard_map/ppermute | solution.py:539
  17.5 1.0 %copy.12 = bf16[128,288]{1,0:T(8,128)(2,1)S(1)} copy(bf16[128,288]{0,1:T(8,128)(2,1)} %param.16) | data formatting | bytes 147456 | tf_op args[6]
  18.5 0.9 %copy.14 = bf16[128,144]{1,0:T(8,128)(2,1)S(1)} copy(bf16[128,144]{0,1:T(8,128)(2,1)} %param.15) | data formatting | bytes 73728 | tf_op args[5]
  19.4 0.1 broadcast_multiply_fusion.1.in_weight_ref
  19.5 0.1 broadcast_multiply_fusion.weight_ref
  19.5 0.0 copy-done.6
  19.6 0.1 copy.13.bias_ref
  19.7 2.0 %collective-permute-done.left_ref = bf16[96,384]{1,0:T(8,128)(2,1)S(1)} collective-permute-done((bf16[96,384]{1,0:T(8,128)(2,1)S(1)}, bf16[96,384]{1,0:T(8,128)(2,1)S(1)}, u32[]{:S(2)}, u32[]{:S(2)}) %collective-permute-start) | collective-permute-done | bytes 73760 | tf_op jit(solution)/shard_map/ppermute | solution.py:538
  21.7 0.0 collective-permute-done.1.right_ref
  21.8 1.5 %collective-permute-start.2 = (bf16[4,64,256]{2,1,0:T(8,128)(2,1)S(1)}, bf16[4,64,256]{2,1,0:T(8,128)(2,1)S(1)}, u32[]{:S(2)}, u32[]{:S(2)}) collective-permute-start(bf16[4,64,256]{2,1,0:T(8,128)(2,1)S(1)} %get-tuple-element.32), channel_id=1, source_target_pairs={{0,8},{8,16},{16,24},{24,0},{1,9},{9,17},{17,25},{25,1},{2,10},{10... | collective-permute-start | bytes 393224 | tf_op jit(solution)/shard_map/ppermute | solution.py:545
  23.3 2.3 %collective-permute-start.3 = (bf16[4,64,256]{2,1,0:T(8,128)(2,1)S(1)}, bf16[4,64,256]{2,1,0:T(8,128)(2,1)S(1)}, u32[]{:S(2)}, u32[]{:S(2)}) collective-permute-start(bf16[4,64,256]{2,1,0:T(8,128)(2,1)S(1)} %get-tuple-element.33), channel_id=1, source_target_pairs={{8,0},{16,8},{24,16},{0,24},{9,1},{17,9},{25,17},{1,25},{10,2},{18... | collective-permute-start | bytes 393224 | tf_op jit(solution)/shard_map/ppermute | solution.py:546
  25.6 0.1 add_convert_fusion.flag_ref
  25.7 2.9 %state_gates.1 = (f32[30,128,256]{2,1,0:T(8,128)}, f32[128,768]{1,0:T(8,128)S(1)}, f32[128,256]{1,0:T(8,128)S(1)}) custom-call(bf16[32,64,256]{2,1,0:T(8,128)(2,1)S(1)} %get-tuple-element.29.rows_ref, bf16[64,768]{1,0:T(8,128)(2,1)S(1)} %get-tuple-element.31.strip_ref, bf16[128,288]{1,0:T(8,128)(2,1)S(1)} %broadcast_multiply_fusion.weight_ref, ...), custom_call_target="tpu_custom_call" | custom-call | flops 603979776 | bytes 1221120 | tf_op jit(solution)/shard_map/state_gates/pallas_call | solution.py:40
  28.6 1.4 %collective-permute-done.2.above_ref = bf16[4,64,256]{2,1,0:T(8,128)(2,1)S(1)} collective-permute-done((bf16[4,64,256]{2,1,0:T(8,128)(2,1)S(1)}, bf16[4,64,256]{2,1,0:T(8,128)(2,1)S(1)}, u32[]{:S(2)}, u32[]{:S(2)}) %collective-permute-start.2) | collective-permute-done | bytes 131104 | tf_op jit(solution)/shard_map/ppermute | solution.py:545
  30.0 3.4 %collective-permute-done.3.below_ref = bf16[4,64,256]{2,1,0:T(8,128)(2,1)S(1)} collective-permute-done((bf16[4,64,256]{2,1,0:T(8,128)(2,1)S(1)}, bf16[4,64,256]{2,1,0:T(8,128)(2,1)S(1)}, u32[]{:S(2)}, u32[]{:S(2)}) %collective-permute-start.3) | collective-permute-done | bytes 131104 | tf_op jit(solution)/shard_map/ppermute | solution.py:546
  33.3 1.2 %state_edges.1 = (f32[6,128,256]{2,1,0:T(8,128)S(1)}, f32[128,512]{1,0:T(8,128)S(1)}, bf16[32,512]{1,0:T(8,128)(2,1)S(1)}) custom-call(s32[2]{0:T(128)S(1)} %add_convert_fusion.flag_ref, bf16[32,64,256]{2,1,0:T(8,128)(2,1)S(1)} %get-tuple-element.29.rows_ref, bf16[64,768]{1,0:T(8,128)(2,1)S(1)} %get-tuple-element.31.strip_ref, ...), custom_call_target="tpu_custom_call" | custom-call | flops 150994944 | bytes 1482760 | tf_op jit(solution)/shard_map/state_edges/pallas_call | solution.py:40
  34.6 0.0 copy-start
  34.6 0.7 %copy-done = f32[128,512]{1,0:T(8,128)} copy-done((f32[128,512]{1,0:T(8,128)}, f32[128,512]{1,0:T(8,128)S(1)}, u32[]{:S(2)}) %copy-start) | copy-done | bytes 262168
  35.3 0.0 all-to-all-done.incoming_ref
  35.3 0.0 copy-start.1
  35.3 0.0 copy-done.3
  35.3 0.0 copy-done.5
  35.3 1.8 %scatter_add.1 = (bf16[32,16,256]{2,1,0:T(8,128)(2,1)S(1)}, bf16[16,768]{1,0:T(8,128)(2,1)S(1)}, bf16[4,16,256]{2,1,0:T(8,128)(2,1)S(1)}, bf16[4,16,256]{2,1,0:T(8,128)(2,1)S(1)}) custom-call(s32[4,32]{1,0:T(4,128)S(1)} %bitcast.12, s32[1,32]{1,0:T(1,128)S(1)} %copy-done.5, bf16[32,72,128]{2,1,0:T(8,128)(2,1)S(1)} %all-to-all-done.incoming_ref, ...), custom_call_target="tpu_custom_call" | custom-call | flops 262144 | bytes 606848 | tf_op jit(solution)/shard_map/scatter_add/pallas_call | solution.py:40
  37.1 1.3 %collective-permute-start.4 = (bf16[4,16,256]{2,1,0:T(8,128)(2,1)S(1)}, bf16[4,16,256]{2,1,0:T(8,128)(2,1)S(1)}, u32[]{:S(2)}, u32[]{:S(2)}) collective-permute-start(bf16[4,16,256]{2,1,0:T(8,128)(2,1)S(1)} %get-tuple-element.44), channel_id=1, source_target_pairs={{0,8},{8,16},{16,24},{24,0},{1,9},{9,17},{17,25},{25,1},{2,10},{10... | collective-permute-start | bytes 98312 | tf_op jit(solution)/shard_map/ppermute | solution.py:545
  38.4 2.6 %collective-permute-start.5 = (bf16[4,16,256]{2,1,0:T(8,128)(2,1)S(1)}, bf16[4,16,256]{2,1,0:T(8,128)(2,1)S(1)}, u32[]{:S(2)}, u32[]{:S(2)}) collective-permute-start(bf16[4,16,256]{2,1,0:T(8,128)(2,1)S(1)} %get-tuple-element.45), channel_id=1, source_target_pairs={{8,0},{16,8},{24,16},{0,24},{9,1},{17,9},{25,17},{1,25},{10,2},{18... | collective-permute-start | bytes 98312 | tf_op jit(solution)/shard_map/ppermute | solution.py:546
  41.0 5.4 %inner.1 = (bf16[26,32,256]{2,1,0:T(8,128)(2,1)S(1)}, bf16[26,32,256]{2,1,0:T(8,128)(2,1)S(1)}, f32[4,128,256]{2,1,0:T(8,128)S(1)}, bf16[4,96,256]{2,1,0:T(8,128...) custom-call(f32[30,128,256]{2,1,0:T(8,128)} %get-tuple-element.48.gates_hbm, ...), custom_call_target="tpu_custom_call" | custom-call | flops 1509949440 | bytes 6000640 | tf_op jit(solution)/shard_map/inner/pallas_call | solution.py:40
  46.4 0.0 collective-permute-done.4.f_above_ref
  46.4 0.0 collective-permute-done.5.f_below_ref
  46.4 0.0 copy-done.1
  46.4 3.1 %edges.1 = (bf16[32,32,256]{2,1,0:T(8,128)(2,1)}, bf16[32,32,256]{2,1,0:T(8,128)(2,1)}) custom-call(s32[2]{0:T(128)S(1)} %add_convert_fusion.flag_ref, f32[6,128,256]{2,1,0:T(8,128)S(1)} %get-tuple-element.34.gates_ref, f32[128,512]{1,0:T(8,128)S(1)} %copy-done.1, bf16[32,64,256]{2,1,0:T(8,128)(2,1)S(1)} %get-tuple-element.29.rows_ref, ...), custom_call_target="tpu_custom_call" | custom-call | flops 283115520 | bytes 4886536 | tf_op jit(solution)/shard_map/edges/pallas_call | solution.py:40
  (3 shorter events, 0.0 us)
Async XLA Ops:
  0.6 18.9 %copy-start.6 = (f32[128]{0:T(128)S(1)}, f32[128]{0:T(128)}, u32[]{:S(2)}) copy-start(f32[128]{0:T(128)} %param.17) | copy-start | bytes 1540
  4.6 30.7 %copy-start.3 = (s32[1,32,4]{1,2,0:T(4,128)S(1)}, s32[1,32,4]{1,2,0:T(4,128)}, u32[]{:S(2)}) copy-start(s32[1,32,4]{1,2,0:T(4,128)} %param.13) | copy-start | bytes 1540
  4.6 30.7 %copy-start.5 = (s32[1,32]{1,0:T(1,128)S(1)}, s32[1,32]{1,0:T(1,128)}, u32[]{:S(2)}) copy-start(s32[1,32]{1,0:T(1,128)} %count_ref.3) | copy-start | bytes 388
  4.6 30.7 %all-to-all-start = ((bf16[32,72,128]{2,1,0:T(8,128)(2,1)}), bf16[32,72,128]{2,1,0:T(8,128)(2,1)S(1)}, u32[]{:S(2)}, u32[]{:S(2)}) async-start(bf16[32,72,128]{2,1,0:T(8,128)(2,1)} %gather_band.1), calls=%async_computation | async-start | bytes 1179648 | tf_op jit(solution)/shard_map/all_to_all | solution.py:596
  11.9 0.7 %copy-start.2 = (s32[1,32,4]{1,2,0:T(4,128)S(1)}, s32[1,32,4]{1,2,0:T(4,128)}, u32[]{:S(2)}) copy-start(s32[1,32,4]{1,2,0:T(4,128)} %param.13) | copy-start | bytes 1540
  12.6 0.7 %copy-start.4 = (s32[1,32]{1,0:T(1,128)S(1)}, s32[1,32]{1,0:T(1,128)}, u32[]{:S(2)}) copy-start(s32[1,32]{1,0:T(1,128)} %count_ref.3) | copy-start | bytes 388
  14.8 7.0 %collective-permute-start = (bf16[96,384]{1,0:T(8,128)(2,1)S(1)}, bf16[96,384]{1,0:T(8,128)(2,1)S(1)}, u32[]{:S(2)}, u32[]{:S(2)}) collective-permute-start(bf16[96,384]{1,0:T(8,128)(2,1)S(1)} %get-tuple-element.30.edge_ref), channel_id=1, source_target_pairs={{0,1},{1,2},{2,3},{3,4},{4,5},{5,6},{6,7},{7,0},{8,9},{9,10},{10,1... | collective-permute-start | bytes 221192 | tf_op jit(solution)/shard_map/ppermute | solution.py:538
  15.1 6.7 %collective-permute-start.1 = (bf16[96,384]{1,0:T(8,128)(2,1)S(1)}, bf16[96,384]{1,0:T(8,128)(2,1)S(1)}, u32[]{:S(2)}, u32[]{:S(2)}) collective-permute-start(bf16[96,384]{1,0:T(8,128)(2,1)S(1)} %get-tuple-element.30.edge_ref), channel_id=1, source_target_pairs={{1,0},{2,1},{3,2},{4,3},{5,4},{6,5},{7,6},{0,7},{9,8},{10,9},{11,1... | collective-permute-start | bytes 221192 | tf_op jit(solution)/shard_map/ppermute | solution.py:539
  21.8 8.2 %collective-permute-start.2 = (bf16[4,64,256]{2,1,0:T(8,128)(2,1)S(1)}, bf16[4,64,256]{2,1,0:T(8,128)(2,1)S(1)}, u32[]{:S(2)}, u32[]{:S(2)}) collective-permute-start(bf16[4,64,256]{2,1,0:T(8,128)(2,1)S(1)} %get-tuple-element.32), channel_id=1, source_target_pairs={{0,8},{8,16},{16,24},{24,0},{1,9},{9,17},{17,25},{25,1},{2,10},{10... | collective-permute-start | bytes 393224 | tf_op jit(solution)/shard_map/ppermute | solution.py:545
  23.3 10.0 %collective-permute-start.3 = (bf16[4,64,256]{2,1,0:T(8,128)(2,1)S(1)}, bf16[4,64,256]{2,1,0:T(8,128)(2,1)S(1)}, u32[]{:S(2)}, u32[]{:S(2)}) collective-permute-start(bf16[4,64,256]{2,1,0:T(8,128)(2,1)S(1)} %get-tuple-element.33), channel_id=1, source_target_pairs={{8,0},{16,8},{24,16},{0,24},{9,1},{17,9},{25,17},{1,25},{10,2},{18... | collective-permute-start | bytes 393224 | tf_op jit(solution)/shard_map/ppermute | solution.py:546
  34.6 0.7 %copy-start = (f32[128,512]{1,0:T(8,128)}, f32[128,512]{1,0:T(8,128)S(1)}, u32[]{:S(2)}) copy-start(f32[128,512]{1,0:T(8,128)S(1)} %get-tuple-element.35.strip_gates_ref) | copy-start | bytes 786436
  35.3 11.2 %copy-start.1 = (f32[128,512]{1,0:T(8,128)S(1)}, f32[128,512]{1,0:T(8,128)}, u32[]{:S(2)}) copy-start(f32[128,512]{1,0:T(8,128)} %copy-done) | copy-start | bytes 786436
  37.1 9.3 %collective-permute-start.4 = (bf16[4,16,256]{2,1,0:T(8,128)(2,1)S(1)}, bf16[4,16,256]{2,1,0:T(8,128)(2,1)S(1)}, u32[]{:S(2)}, u32[]{:S(2)}) collective-permute-start(bf16[4,16,256]{2,1,0:T(8,128)(2,1)S(1)} %get-tuple-element.44), channel_id=1, source_target_pairs={{0,8},{8,16},{16,24},{24,0},{1,9},{9,17},{17,25},{25,1},{2,10},{10... | collective-permute-start | bytes 98312 | tf_op jit(solution)/shard_map/ppermute | solution.py:545
  38.4 8.1 %collective-permute-start.5 = (bf16[4,16,256]{2,1,0:T(8,128)(2,1)S(1)}, bf16[4,16,256]{2,1,0:T(8,128)(2,1)S(1)}, u32[]{:S(2)}, u32[]{:S(2)}) collective-permute-start(bf16[4,16,256]{2,1,0:T(8,128)(2,1)S(1)} %get-tuple-element.45), channel_id=1, source_target_pairs={{8,0},{16,8},{24,16},{0,24},{9,1},{17,9},{25,17},{1,25},{10,2},{18... | collective-permute-start | bytes 98312 | tf_op jit(solution)/shard_map/ppermute | solution.py:546

commit v5 on v4

--- a/solution.py
+++ b/solution.py
@@ -124,20 +124,24 @@
 
 
 def prepare_kernel(
-    hidden_hbm, cell_hbm, target_ref, count_ref, rows_ref, edge_ref, hidden, cell, hidden_sem, cell_sem
+    hidden_hbm, cell_hbm, target_hbm, count_hbm, rows_ref, edge_ref, hidden, cell, target_ref, count_ref, sems
 ):
     fetches = [
-        pltpu.make_async_copy(hidden_hbm, hidden, hidden_sem),
-        pltpu.make_async_copy(cell_hbm, cell, cell_sem),
+        pltpu.make_async_copy(source, target, sems.at[i])
+        for i, (source, target) in enumerate(
+            [(target_hbm, target_ref), (count_hbm, count_ref), (hidden_hbm, hidden), (cell_hbm, cell)]
+        )
     ]
     for fetch in fetches:
         fetch.start()
     units, row_count, _ = hidden.shape
+    fetches[0].wait()
+    fetches[1].wait()
     edge_ref[2 * units :, :LANES] = marks_of(target_ref[...], count_ref[...]).astype(BF)
     edge_ref[2 * units :, LANES:] = jnp.zeros((target_ref.shape[1], STRIP - LANES), BF)
-    fetches[0].wait()
+    fetches[2].wait()
     rows_ref[:, :units, :] = jnp.swapaxes(hidden[...], 0, 1)
-    fetches[1].wait()
+    fetches[3].wait()
     rows_ref[:, units:, :] = jnp.swapaxes(cell[...], 0, 1)
     tiles = edge_tiles(lambda y: rows_ref[y], row_count, 2 * units)
     for t, tile in enumerate(tiles):
@@ -163,29 +167,9 @@
     )
 
 
-def lay_out(rows_ref, own, from_left, from_right, strip_ref, up_ref, down_ref):
+def strips_of(own, from_left, from_right):
     near = lane_of(own.shape) % 8 < 4
-    left = jnp.where(near, from_left, own)
-    right = jnp.where(near, own, from_right)
-    strip_ref[:, :STRIP] = left
-    strip_ref[:, STRIP:] = right
-    rows = rows_ref.shape[0]
-    up_ref[:3] = rows_ref[:3]
-    up_ref[3, :, :LANES] = left[:, :LANES]
-    up_ref[3, :, LANES:] = right[:, :LANES]
-    down_ref[:3] = rows_ref[rows - 3 :]
-    down_ref[3, :, :LANES] = left[:, 2 * LANES :]
-    down_ref[3, :, LANES:] = right[:, 2 * LANES :]
-
-
-def strips_kernel(rows_ref, edge_ref, left_ref, right_ref, strip_ref, up_ref, down_ref, mark_ref):
-    channels = rows_ref.shape[1]
-    lay_out(
-        rows_ref, edge_ref[:channels], left_ref[:channels], right_ref[:channels], strip_ref, up_ref, down_ref
-    )
-    near = lane_of(mark_ref.shape) % 8 < 4
-    from_left = left_ref[channels:, :LANES].astype(F32)
-    mark_ref[...] = jnp.where(near, from_left, right_ref[channels:, :LANES].astype(F32))
+    return jnp.where(near, from_left, own), jnp.where(near, own, from_right)
 
 
 def full_strip(strip, above, below, has_above, has_below):
@@ -252,13 +236,20 @@
 
 
 def state_kernel(
-    rows_ref, strip_ref, weight_ref, bias_ref,
-    gates_hbm, strip_gates_ref, wide_bias_ref, gates, three, patches, sems,
+    rows_ref, edge_ref, left_ref, right_ref, weight_ref, bias_ref,
+    gates_hbm, strip_gates_ref, wide_bias_ref, strip_ref, mark_ref, gates, three, patches, sems,
 ):
     units = rows_ref.shape[1] // 2
     count = rows_ref.shape[0]
     wide_bias_ref[...] = jnp.broadcast_to(bias_ref[...], wide_bias_ref.shape)
-    strip = strip_ref[:units]
+    channels = 2 * units
+    left, right = strips_of(edge_ref[:channels], left_ref[:channels], right_ref[:channels])
+    strip_ref[:, :STRIP] = left
+    strip_ref[:, STRIP:] = right
+    near = lane_of(mark_ref.shape) % 8 < 4
+    from_left = left_ref[channels:, :LANES].astype(F32)
+    mark_ref[...] = jnp.where(near, from_left, right_ref[channels:, :LANES].astype(F32))
+    strip = jnp.concatenate([left[:units], right[:units]], axis=1)
     strip_gates_ref[...] = matmul(weight_ref[...], strip_taps(strip))
     store_patches(strip, patches, PAD, count + PAD)
     for y in range(count):
@@ -287,29 +278,6 @@
     mirror = count + 2 * PAD - 1
     found.update(patches_of(strip, (0, 2), mirror - last + 1, mirror - first + 1))
     return found
-
-
-def state_edge_kernel(
-    flag_ref, rows_ref, strip_ref, above_ref, below_ref, weight_ref,
-    gates_ref, strip_gates_ref, cell_strip_ref, three,
-):
-    units = rows_ref.shape[1] // 2
-    count = rows_ref.shape[0]
-    has_above = flag_ref[0].astype(F32).astype(BF)
-    has_below = flag_ref[1].astype(F32).astype(BF)
-    strip = ends_of(full_strip(strip_ref[...], above_ref[3], below_ref[3], has_above, has_below))
-    cell_strip_ref[...] = strip[units:]
-    strip = strip[:units]
-    strip_gates_ref[...] = matmul(weight_ref[...], strip_taps(strip))
-    patches = edge_patches(strip, 1, PAD + 2, count)
-    for i in range(3):
-        store_three(three, 1 + i, above_ref[i, :units] * has_above, patches[1 + i])
-        r = count + PAD + i
-        store_three(three, r, below_ref[i, :units] * has_below, patches[r])
-    for r in edge_rows(count, 0, 2):
-        store_three(three, r, rows_ref[r - PAD, :units], patches[r])
-    for i, r in enumerate(edge_rows(count, -2, 3)):
-        gates_ref[i] = matmul(weight_ref[...], row_taps(three, r))
 
 
 def update(gates, memory):
@@ -403,11 +371,11 @@
 
 
 def edge_kernel(
-    flag_ref, gates_ref, strip_gates_ref, rows_ref, above_ref, below_ref, cell_strip_ref,
-    forcing_ref, forcing_strip_ref, f_above_ref, f_below_ref, in_weight_ref, weight_ref, bias_ref,
+    flag_ref, rows_ref, strip_ref, forcing_ref, forcing_strip_ref, above_ref, below_ref,
+    in_weight_ref, weight_ref, bias_ref,
     inner_hidden_ref, inner_cell_ref, sums_ref, first_ref, second_ref, memory_ref,
     hidden_ref, cell_ref,
-    f_three, first, second, h_rows, c_rows,
+    f_three, three, first, second, h_rows, c_rows,
 ):
     units = rows_ref.shape[1] // 2
     count = rows_ref.shape[0]
@@ -416,15 +384,26 @@
     bf_above, bf_below = has_above.astype(BF), has_below.astype(BF)
     bias = bias_ref[...]
 
-    strip = ends_of(full_strip(forcing_strip_ref[...], f_above_ref[3], f_below_ref[3], bf_above, bf_below))
+    channels = forcing_ref.shape[1]
+    joined = jnp.concatenate([forcing_strip_ref[...], strip_ref[...]], axis=0)
+    joined = ends_of(full_strip(joined, above_ref[3], below_ref[3], bf_above, bf_below))
+    strip = joined[:channels]
+    state_strip = joined[channels : channels + units]
     strip_forcing = matmul(in_weight_ref[...], strip_taps(strip)) + jnp.concatenate([bias] * 2, axis=1)
-    f_patches = edge_patches(strip, 1, PAD + 2, count)
+    strip_gates = strip_forcing + matmul(weight_ref[...], strip_taps(state_strip))
+    patches = edge_patches(joined[: channels + units], 1, PAD + 2, count)
+
+    def place(r, forcing, hidden):
+        store_three(f_three, r, forcing, patches[r][:channels])
+        store_three(three, r, hidden, patches[r][channels:])
+
     for i in range(3):
-        store_three(f_three, 1 + i, f_above_ref[i] * bf_above, f_patches[1 + i])
-        r = count + PAD + i
-        store_three(f_three, r, f_below_ref[i] * bf_below, f_patches[r])
+        ahead = above_ref[i, : channels + units] * bf_above
+        place(1 + i, ahead[:channels], ahead[channels:])
+        ahead = below_ref[i, : channels + units] * bf_below
+        place(count + PAD + i, ahead[:channels], ahead[channels:])
     for r in edge_rows(count, 0, 2):
-        store_three(f_three, r, forcing_ref[r - PAD], f_patches[r])
+        place(r, forcing_ref[r - PAD], rows_ref[r - PAD, :units])
 
     lane = lane_of((units, strip.shape[1]))
     row_of_lane = (lane % LANES) // 8 + 32 * (lane // LANES % 2)
@@ -438,24 +417,23 @@
             hidden = hidden * has_below
         return hidden.astype(BF)
 
-    strip_memory = cell_strip_ref[...].astype(F32)
-    strip_hidden, strip_memory = update(strip_gates_ref[...] + strip_forcing, strip_memory)
+    strip_memory = joined[channels + units :].astype(F32)
+    strip_hidden, strip_memory = update(strip_gates, strip_memory)
     strip_hidden = (strip_hidden * keep).astype(BF)
     marks = edge_patches(strip_hidden, 2, PAD + 1, count)
-
-    def taps(rows):
-        return jnp.concatenate(rows, axis=0)
 
     sums, memory = {}, {}
     for i, r in enumerate(edge_rows(count, 1, 2)):
         sums[r] = sums_ref[i]
         memory[r] = memory_ref[i]
     group = edge_rows(count, -2, 3)
-    olds = [above_ref[1, units:], above_ref[2, units:], rows_ref[0, units:]]
-    olds += [rows_ref[count - 1, units:], below_ref[0, units:], below_ref[1, units:]]
-    for i, (r, old) in enumerate(zip(group, olds)):
+    cells = channels + units
+    olds = [above_ref[1, cells:], above_ref[2, cells:], rows_ref[0, units:]]
+    olds += [rows_ref[count - 1, units:], below_ref[0, cells:], below_ref[1, cells:]]
+    for r, old in zip(group, olds):
         sums[r] = matmul(in_weight_ref[...], row_taps(f_three, r)) + bias
-        hidden, memory[r] = update(gates_ref[i] + sums[r], old.astype(F32))
+        first_gates = sums[r] + matmul(weight_ref[...], row_taps(three, r))
+        hidden, memory[r] = update(first_gates, old.astype(F32))
         store_three(first, r, kept(hidden, r), marks[r])
     for i, r in enumerate(edge_rows(count, 1, 2)):
         first[r] = first_ref[i]
@@ -505,7 +483,8 @@
 
 
 def scatter_kernel(
-    target_ref, count_ref, incoming_ref, mark_ref, rows_ref, strip_ref, up_ref, down_ref, total
+    target_ref, count_ref, incoming_ref, mark_ref, state_ref, state_strip_ref,
+    rows_ref, strip_ref, up_ref, down_ref, total,
 ):
     cap, sources = target_ref.shape
     row_count, channels, width = rows_ref.shape
@@ -522,7 +501,17 @@
         rows_ref[y, :, width:] = total[2 * y + 1].astype(BF)
     own = jnp.concatenate(edge_tiles(lambda y: rows_ref[y], row_count, channels), axis=1)
     others = beside(incoming_ref, mark_ref, row_count, channels)
-    lay_out(rows_ref, own, others, others, strip_ref, up_ref, down_ref)
+    left, right = strips_of(own, others, others)
+    strip_ref[:, :STRIP] = left
+    strip_ref[:, STRIP:] = right
+    for ref, first, tile in ((up_ref, 0, 0), (down_ref, row_count - 3, 2)):
+        ref[:3, :channels] = rows_ref[first : first + 3]
+        ref[:3, channels:] = state_ref[first : first + 3]
+        spot = tile * LANES
+        ref[3, :channels, :LANES] = left[:, spot : spot + LANES]
+        ref[3, :channels, LANES:] = right[:, spot : spot + LANES]
+        ref[3, channels:, :LANES] = state_strip_ref[:, spot : spot + LANES]
+        ref[3, channels:, LANES:] = state_strip_ref[:, STRIP + spot : STRIP + spot + LANES]
 
 
 def around(count):
@@ -601,41 +590,32 @@
             jax.ShapeDtypeStruct((row_count, 2 * units, column_count), BF),
             jax.ShapeDtypeStruct((2 * units + tiles, STRIP), BF),
         ),
-        in_specs=[pl.BlockSpec(memory_space=pl.ANY)] * 2 + whole(2),
+        in_specs=[pl.BlockSpec(memory_space=pl.ANY)] * 4,
         out_specs=tuple(whole(2)),
         scratch_shapes=[
             pltpu.VMEM(hidden_init.shape, BF),
             pltpu.VMEM(cell_init.shape, BF),
-            pltpu.SemaphoreType.DMA,
-            pltpu.SemaphoreType.DMA,
+            pltpu.VMEM((cap, tiles), jnp.int32),
+            pltpu.VMEM((1, tiles), jnp.int32),
+            pltpu.SemaphoreType.DMA((4,)),
         ],
         compiler_params=pltpu.CompilerParams(vmem_limit_bytes=8 * 2**20),
         name="prepare",
-    )(in_hbm(hidden_init), in_hbm(cell_init), slot_target[0].T, tile_counts)
+    )(in_hbm(hidden_init), in_hbm(cell_init), in_hbm(slot_target[0].T), in_hbm(tile_counts))
     from_left, from_right = exchange_columns(edge)
-    ends = jax.ShapeDtypeStruct((4, 2 * units, column_count), BF)
-    strip, up, down, marks = call(
-        strips_kernel,
-        [
-            jax.ShapeDtypeStruct((2 * units, 2 * STRIP), BF),
-            ends,
-            ends,
-            jax.ShapeDtypeStruct((tiles, LANES), F32),
-        ],
-        4, 0, [], "state_strips", 1000, (rows, edge, from_left, from_right),
-    )
-    above, below = exchange_rows(up, down)
     padded = row_count + 8
     inside = (row_count - 2, gates, column_count)
     parts = inside[0] // PIECE
-    state_gates, strip_gates, bias = call(
+    state_gates, strip_gates, bias, strip, marks = call(
         state_kernel,
         [
             pltpu.HBM(inside, F32),
             jax.ShapeDtypeStruct((gates, 2 * STRIP), F32),
             jax.ShapeDtypeStruct((gates, column_count), F32),
+            jax.ShapeDtypeStruct((2 * units, 2 * STRIP), BF),
+            jax.ShapeDtypeStruct((tiles, LANES), F32),
         ],
-        4, 0,
+        6, 0,
         [
             pltpu.VMEM(inside, F32),
             pltpu.VMEM((padded, 3 * units, column_count), BF),
@@ -643,26 +623,14 @@
             pltpu.SemaphoreType.DMA((parts,)),
         ],
         "state_gates", 2 * gates * 9 * units * row_count * column_count,
-        (rows, strip, state_weight, bias), 16,
-        out_specs=[pl.BlockSpec(memory_space=pl.ANY)] + whole(2),
-    )
-    edge_gates, edge_strip_gates, cell_strip = call(
-        state_edge_kernel,
-        [
-            jax.ShapeDtypeStruct((6, gates, column_count), F32),
-            jax.ShapeDtypeStruct((gates, 4 * LANES), F32),
-            jax.ShapeDtypeStruct((units, 4 * LANES), BF),
-        ],
-        5, 1,
-        [pltpu.VMEM((padded, 3 * units, column_count), BF)],
-        "state_edges", 2 * gates * 9 * units * 8 * column_count,
-        (flags, rows, strip, above, below, state_weight),
+        (rows, edge, from_left, from_right, state_weight, bias), 16,
+        out_specs=[pl.BlockSpec(memory_space=pl.ANY)] + whole(4),
     )
     incoming, state_gates, strip_gates, bias, in_weight = lax.optimization_barrier(
         (incoming, state_gates, strip_gates, bias, in_weight)
     )
 
-    ends = jax.ShapeDtypeStruct((4, channels, column_count), BF)
+    ends = jax.ShapeDtypeStruct((4, channels + 2 * units, column_count), BF)
     forcing, forcing_strip, up, down = call(
         scatter_kernel,
         [
@@ -671,12 +639,12 @@
             ends,
             ends,
         ],
-        2, 2,
+        4, 2,
         [pltpu.VMEM((2 * row_count + 1, channels, block), F32)],
         "scatter_add", slots * channels * block,
-        (slot_target[0].T, tile_counts, incoming, marks),
+        (slot_target[0].T, tile_counts, incoming, marks, rows, strip),
     )
-    f_above, f_below = exchange_rows(up, down)
+    above, below = exchange_rows(up, down)
     inner_rows = jax.ShapeDtypeStruct((row_count - 6, units, column_count), BF)
     threes = jax.ShapeDtypeStruct((4, 3 * units, column_count), BF)
     inner = call(
@@ -709,17 +677,17 @@
     return call(
         edge_kernel,
         [out, out],
-        19, 1,
+        15, 1,
         [
             pltpu.VMEM((padded, 3 * channels, column_count), BF),
+            pltpu.VMEM((padded, 3 * units, column_count), BF),
             pltpu.VMEM((padded, 3 * units, column_count), BF),
             pltpu.VMEM((padded, 3 * units, column_count), BF),
             pltpu.VMEM((row_count, units, column_count), BF),
             pltpu.VMEM((row_count, units, column_count), BF),
         ],
-        "edges", 2 * gates * 9 * (channels + 2 * units) * 6 * column_count,
-        (flags, edge_gates, edge_strip_gates, rows, above, below, cell_strip, forcing, forcing_strip,
-         f_above, f_below, in_weight, state_weight, bias, *inner), 16,
+        "edges", 2 * gates * 9 * (channels + 3 * units) * 6 * column_count,
+        (flags, rows, strip, forcing, forcing_strip, above, below, in_weight, state_weight, bias, *inner), 16,
     )
 
 

time: 49.9 us -> 44.7 us (0.90)
  starting transfers between devices: 17.8 us -> 13.9 us
  local copies, waits for them, and re-layouts: 4.03 us -> 2 us
  waiting for transfers between devices: 6.76 us -> 8.21 us
  Pallas kernels: 19.9 us -> 19.2 us
    all_to_all x1, waiting for transfers between devices: 0.01 us -> 5.34 us  [on_device(): lax.all_to_all(outgoing, ('lat', 'lon'), split_axis=0, concat_axis=0, til...]
    ppermute x2 -> x1, waiting for transfers between devices: 3.36 us -> 0.87 us  [exchange_rows(): from_below = lax.ppermute(up, 'lat', back(count))]
    ppermute x2 -> x1, starting transfers between devices: 4.96 us -> 2.51 us  [exchange_rows(): from_below = lax.ppermute(up, 'lat', back(count))]
    unnamed x16 -> x8, local copies, waits for them, and re-layouts: 3.92 us -> 1.88 us
    ppermute x2 -> x1, starting transfers between devices: 2.79 us -> 1.36 us  [exchange_rows(): from_above = lax.ppermute(down, 'lat', around(count))]
    ppermute x2 -> x1, waiting for transfers between devices: 1.36 us -> 0.01 us  [exchange_rows(): from_above = lax.ppermute(down, 'lat', around(count))]
    pallas_call x6 -> x4, Pallas kernels: 14.5 us -> 13.7 us  [call(): pl.pallas_call(kernel, out_shape=tuple(outs), in_specs=in_specs or scalar...]
  transfers between devices with their start and end apart: 7 -> 5, of which waited for: 3 -> 3; matrix products, arithmetic and copies ran while one was open for 5% -> 5% of each run, Pallas kernels for 22% -> 23%
where the time goes in v5:
time: 44.7 us; the launch traced here: 44.3 us
  Pallas kernels  19.2 us (43%)
  starting transfers between devices  13.9 us (31%)
  waiting for transfers between devices  8.21 us (18%)
  local copies, waits for them, and re-layouts  2 us (4%)
  between operations  0.77 us (2%)
    pallas_call x4, Pallas kernels, call(): pl.pallas_call(kernel, out_shape=tuple(outs), in_specs=in_specs or scalar...  13.7 us
    all_to_all x1, starting transfers between devices, on_device(): lax.all_to_all(outgoing, ('lat', 'lon'), split_axis=0, concat_axis=0, til...  7.3 us
    all_to_all x1, waiting for transfers between devices, on_device(): lax.all_to_all(outgoing, ('lat', 'lon'), split_axis=0, concat_axis=0, til...  5.34 us
    pallas_call x1, Pallas kernels, on_device(): pl.pallas_call(functools.partial(gather_kernel, ring), out_shape=pltpu.HB...  3.92 us
    ppermute x1, starting transfers between devices, exchange_rows(): from_below = lax.ppermute(up, 'lat', back(count))  2.51 us
    ppermute x1, starting transfers between devices, exchange_columns(): from_right = lax.ppermute(edge, 'lon', back(count))  2.39 us
    ppermute x1, waiting for transfers between devices, exchange_columns(): from_left = lax.ppermute(edge, 'lon', around(count))  1.99 us
    unnamed x8, local copies, waits for them, and re-layouts  1.88 us
  transfers between devices with their start and end apart: 5, of which 3 were waited for; matrix products, arithmetic and copies ran while one was open for 5% of the time, Pallas kernels for 23%

profile of v5, /device:TPU:0, one launch (start us, length us, event | category | flops | bytes accessed | tf_op | source)
XLA Modules:
  0.0 44.3 jit_solution(15335879962293921070)
XLA Ops:
  0.6 0.0 copy-start
  0.6 0.0 copy-start.1
  0.7 0.0 copy-start.2
  0.7 3.9 %gather_band.1 = bf16[32,72,128]{2,1,0:T(8,128)(2,1)} custom-call(s32[4,32]{1,0:T(4,128)} %bitcast.14, bf16[128,16,128]{2,1,0:T(8,128)(2,1)} %blocks_hbm.1, bf16[128,8,128]{2,1,0:T(8,128)(2,1)} %bitcast.13), custom_call_target="tpu_custom_call" | custom-call | tf_op jit(solution)/shard_map/gather_band/pallas_call | solution.py:567
  4.6 7.3 %all-to-all-start = ((bf16[32,72,128]{2,1,0:T(8,128)(2,1)}), bf16[32,72,128]{2,1,0:T(8,128)(2,1)S(1)}, u32[]{:S(2)}, u32[]{:S(2)}) async-start(bf16[32,72,128]{2,1,0:T(8,128)(2,1)} %gather_band.1), calls=%async_computation | async-start | bytes 1179648 | tf_op jit(solution)/shard_map/all_to_all | solution.py:585
  11.9 1.6 %prepare.1 = (bf16[32,64,256]{2,1,0:T(8,128)(2,1)S(1)}, bf16[96,384]{1,0:T(8,128)(2,1)S(1)}) custom-call(bf16[32,32,256]{2,1,0:T(8,128)(2,1)} %hidden_hbm.1, bf16[32,32,256]{2,1,0:T(8,128)(2,1)} %cell_hbm.1, s32[4,32]{1,0:T(4,128)} %bitcast.11, s32[1,32]{1,0:T(1,128)} %count_ref.1), custom_call_target="tpu_custom_call" | custom-call | tf_op jit(solution)/shard_map/prepare/pallas_call | solution.py:587
  13.5 0.3 collective-permute-start
  13.8 2.4 %collective-permute-start.1 = (bf16[96,384]{1,0:T(8,128)(2,1)S(1)}, bf16[96,384]{1,0:T(8,128)(2,1)S(1)}, u32[]{:S(2)}, u32[]{:S(2)}) collective-permute-start(bf16[96,384]{1,0:T(8,128)(2,1)S(1)} %get-tuple-element.25.edge_ref), channel_id=1, source_target_pairs={{1,0},{2,1},{3,2},{4,3},{5,4},{6,5},{7,6},{0,7},{9,8},{10,9},{11,1... | collective-permute-start | bytes 221192 | tf_op jit(solution)/shard_map/ppermute | solution.py:528
  16.2 1.0 %copy.12 = bf16[128,288]{1,0:T(8,128)(2,1)S(1)} copy(bf16[128,288]{0,1:T(8,128)(2,1)} %param.16) | data formatting | bytes 147456 | tf_op args[6]
  17.2 0.9 %copy.14 = bf16[128,144]{1,0:T(8,128)(2,1)S(1)} copy(bf16[128,144]{0,1:T(8,128)(2,1)} %param.15) | data formatting | bytes 73728 | tf_op args[5]
  18.1 0.1 broadcast_multiply_fusion.1.in_weight_ref
  18.2 0.1 broadcast_multiply_fusion.weight_ref
  18.2 0.0 copy-done.2
  18.3 0.1 copy.13.bias_ref
  18.4 2.0 %collective-permute-done.left_ref = bf16[96,384]{1,0:T(8,128)(2,1)S(1)} collective-permute-done((bf16[96,384]{1,0:T(8,128)(2,1)S(1)}, bf16[96,384]{1,0:T(8,128)(2,1)S(1)}, u32[]{:S(2)}, u32[]{:S(2)}) %collective-permute-start) | collective-permute-done | bytes 73760 | tf_op jit(solution)/shard_map/ppermute | solution.py:527
  20.4 0.0 collective-permute-done.1.right_ref
  20.4 2.9 %state_gates.1 = (f32[30,128,256]{2,1,0:T(8,128)}, f32[128,768]{1,0:T(8,128)S(1)}, f32[128,256]{1,0:T(8,128)S(1)}, bf16[64,768]{1,0:T(8,128)(2,1)S(1)}, f32[32,128]{1,0:T(8,128)S(1)}) custom-call(bf16[32,64,256]{2,1,0:T(8,128)(2,1)S(1)} %get-tuple-element.24.rows_ref.state_ref, bf16[96,384]{1,0:T(8,128)(2,1)S(1)} %get-tuple-element.25.edge_ref, ...), custom_call_target="tpu_custom_call" | custom-call | flops 603979776 | bytes 1344000 | tf_op jit(solution)/shard_map/state_gates/pallas_call | solution.py:40
  23.3 5.3 %all-to-all-done.incoming_ref = bf16[32,72,128]{2,1,0:T(8,128)(2,1)S(1)} async-done(((bf16[32,72,128]{2,1,0:T(8,128)(2,1)}), bf16[32,72,128]{2,1,0:T(8,128)(2,1)S(1)}, u32[]{:S(2)}, u32[]{:S(2)}) %all-to-all-start) | async-done | bytes 589856 | tf_op jit(solution)/shard_map/all_to_all | solution.py:585
  28.6 0.0 copy-done
  28.6 0.0 copy-done.1
  28.6 1.8 %scatter_add.1 = (bf16[32,16,256]{2,1,0:T(8,128)(2,1)S(1)}, bf16[16,768]{1,0:T(8,128)(2,1)S(1)}, bf16[4,80,256]{2,1,0:T(8,128)(2,1)S(1)}, bf16[4,80,256]{2,1,0:T(8,128)(2,1)S(1)}) custom-call(s32[4,32]{1,0:T(4,128)S(1)} %bitcast.12, s32[1,32]{1,0:T(1,128)S(1)} %copy-done.1, bf16[32,72,128]{2,1,0:T(8,128)(2,1)S(1)} %all-to-all-done.incoming_ref, ...), custom_call_target="tpu_custom_call" | custom-call | flops 262144 | bytes 1753728 | tf_op jit(solution)/shard_map/scatter_add/pallas_call | solution.py:40
  30.5 1.4 %collective-permute-start.2 = (bf16[4,80,256]{2,1,0:T(8,128)(2,1)S(1)}, bf16[4,80,256]{2,1,0:T(8,128)(2,1)S(1)}, u32[]{:S(2)}, u32[]{:S(2)}) collective-permute-start(bf16[4,80,256]{2,1,0:T(8,128)(2,1)S(1)} %get-tuple-element.34), channel_id=1, source_target_pairs={{0,8},{8,16},{16,24},{24,0},{1,9},{9,17},{17,25},{25,1},{2,10},{10... | collective-permute-start | bytes 491528 | tf_op jit(solution)/shard_map/ppermute | solution.py:534
  31.8 2.5 %collective-permute-start.3 = (bf16[4,80,256]{2,1,0:T(8,128)(2,1)S(1)}, bf16[4,80,256]{2,1,0:T(8,128)(2,1)S(1)}, u32[]{:S(2)}, u32[]{:S(2)}) collective-permute-start(bf16[4,80,256]{2,1,0:T(8,128)(2,1)S(1)} %get-tuple-element.35), channel_id=1, source_target_pairs={{8,0},{16,8},{24,16},{0,24},{9,1},{17,9},{25,17},{1,25},{10,2},{18... | collective-permute-start | bytes 491528 | tf_op jit(solution)/shard_map/ppermute | solution.py:535
  34.4 0.1 add_convert_fusion.flag_ref
  34.4 5.6 %inner.1 = (bf16[26,32,256]{2,1,0:T(8,128)(2,1)S(1)}, bf16[26,32,256]{2,1,0:T(8,128)(2,1)S(1)}, f32[4,128,256]{2,1,0:T(8,128)S(1)}, bf16[4,96,256]{2,1,0:T(8,128...) custom-call(f32[30,128,256]{2,1,0:T(8,128)} %get-tuple-element.38.gates_hbm, ...), custom_call_target="tpu_custom_call" | custom-call | flops 1509949440 | bytes 6000640 | tf_op jit(solution)/shard_map/inner/pallas_call | solution.py:40
  40.1 0.0 collective-permute-done.2.above_ref
  40.1 0.9 %collective-permute-done.3.below_ref = bf16[4,80,256]{2,1,0:T(8,128)(2,1)S(1)} collective-permute-done((bf16[4,80,256]{2,1,0:T(8,128)(2,1)S(1)}, bf16[4,80,256]{2,1,0:T(8,128)(2,1)S(1)}, u32[]{:S(2)}, u32[]{:S(2)}) %collective-permute-start.3) | collective-permute-done | bytes 163872 | tf_op jit(solution)/shard_map/ppermute | solution.py:535
  40.9 3.4 %edges.1 = (bf16[32,32,256]{2,1,0:T(8,128)(2,1)}, bf16[32,32,256]{2,1,0:T(8,128)(2,1)}) custom-call(s32[2]{0:T(128)S(1)} %add_convert_fusion.flag_ref, bf16[32,64,256]{2,1,0:T(8,128)(2,1)S(1)} %get-tuple-element.24.rows_ref.state_ref, bf16[64,768]{1,0:T(8,128)(2,1)S(1)} %get-tuple-element.26.state_strip_ref.strip_ref, ...), custom_call_target="tpu_custom_call" | custom-call | flops 396361728 | bytes 3903496 | tf_op jit(solution)/shard_map/edges/pallas_call | solution.py:40
  (2 shorter events, 0.0 us)
Async XLA Ops:
  0.6 28.0 %copy-start = (s32[1,32,4]{1,2,0:T(4,128)S(1)}, s32[1,32,4]{1,2,0:T(4,128)}, u32[]{:S(2)}) copy-start(s32[1,32,4]{1,2,0:T(4,128)} %param.13) | copy-start | bytes 1540
  0.6 28.0 %copy-start.1 = (s32[1,32]{1,0:T(1,128)S(1)}, s32[1,32]{1,0:T(1,128)}, u32[]{:S(2)}) copy-start(s32[1,32]{1,0:T(1,128)} %count_ref.1) | copy-start | bytes 388
  0.7 17.6 %copy-start.2 = (f32[128]{0:T(128)S(1)}, f32[128]{0:T(128)}, u32[]{:S(2)}) copy-start(f32[128]{0:T(128)} %param.17) | copy-start | bytes 1540
  4.6 24.0 %all-to-all-start = ((bf16[32,72,128]{2,1,0:T(8,128)(2,1)}), bf16[32,72,128]{2,1,0:T(8,128)(2,1)S(1)}, u32[]{:S(2)}, u32[]{:S(2)}) async-start(bf16[32,72,128]{2,1,0:T(8,128)(2,1)} %gather_band.1), calls=%async_computation | async-start | bytes 1179648 | tf_op jit(solution)/shard_map/all_to_all | solution.py:585
  13.5 6.9 %collective-permute-start = (bf16[96,384]{1,0:T(8,128)(2,1)S(1)}, bf16[96,384]{1,0:T(8,128)(2,1)S(1)}, u32[]{:S(2)}, u32[]{:S(2)}) collective-permute-start(bf16[96,384]{1,0:T(8,128)(2,1)S(1)} %get-tuple-element.25.edge_ref), channel_id=1, source_target_pairs={{0,1},{1,2},{2,3},{3,4},{4,5},{5,6},{6,7},{7,0},{8,9},{9,10},{10,1... | collective-permute-start | bytes 221192 | tf_op jit(solution)/shard_map/ppermute | solution.py:527
  13.8 6.6 %collective-permute-start.1 = (bf16[96,384]{1,0:T(8,128)(2,1)S(1)}, bf16[96,384]{1,0:T(8,128)(2,1)S(1)}, u32[]{:S(2)}, u32[]{:S(2)}) collective-permute-start(bf16[96,384]{1,0:T(8,128)(2,1)S(1)} %get-tuple-element.25.edge_ref), channel_id=1, source_target_pairs={{1,0},{2,1},{3,2},{4,3},{5,4},{6,5},{7,6},{0,7},{9,8},{10,9},{11,1... | collective-permute-start | bytes 221192 | tf_op jit(solution)/shard_map/ppermute | solution.py:528
  30.5 9.6 %collective-permute-start.2 = (bf16[4,80,256]{2,1,0:T(8,128)(2,1)S(1)}, bf16[4,80,256]{2,1,0:T(8,128)(2,1)S(1)}, u32[]{:S(2)}, u32[]{:S(2)}) collective-permute-start(bf16[4,80,256]{2,1,0:T(8,128)(2,1)S(1)} %get-tuple-element.34), channel_id=1, source_target_pairs={{0,8},{8,16},{16,24},{24,0},{1,9},{9,17},{17,25},{25,1},{2,10},{10... | collective-permute-start | bytes 491528 | tf_op jit(solution)/shard_map/ppermute | solution.py:534
  31.8 9.1 %collective-permute-start.3 = (bf16[4,80,256]{2,1,0:T(8,128)(2,1)S(1)}, bf16[4,80,256]{2,1,0:T(8,128)(2,1)S(1)}, u32[]{:S(2)}, u32[]{:S(2)}) collective-permute-start(bf16[4,80,256]{2,1,0:T(8,128)(2,1)S(1)} %get-tuple-element.35), channel_id=1, source_target_pairs={{8,0},{16,8},{24,16},{0,24},{9,1},{17,9},{25,17},{1,25},{10,2},{18... | collective-permute-start | bytes 491528 | tf_op jit(solution)/shard_map/ppermute | solution.py:535

commit v6 on v5

--- a/solution.py
+++ b/solution.py
@@ -172,18 +172,22 @@
     return jnp.where(near, from_left, own), jnp.where(near, own, from_right)
 
 
-def full_strip(strip, above, below, has_above, has_below):
-    lane = lane_of(above[:, :LANES].shape)
+def pack_strips(left, right):
+    return jnp.where(lane_of(left.shape) < 64, left, pltpu.roll(right, 64, axis=1))
+
+
+def full_strip(strip, above, below):
+    lane = lane_of(above.shape)
     from_above = (lane >= 8) & (lane < 32)
     from_below = (lane >= 32) & (lane < 56)
     parts = []
     for side in range(2):
         base = side * STRIP
-        theirs = above[:, side * LANES : (side + 1) * LANES] * has_above
-        parts.append(jnp.where(from_above, theirs, strip[:, base : base + LANES]))
+        if side:
+            above, below = pltpu.roll(above, 64, axis=1), pltpu.roll(below, 64, axis=1)
+        parts.append(jnp.where(from_above, above, strip[:, base : base + LANES]))
         parts.append(strip[:, base + LANES : base + 2 * LANES])
-        theirs = below[:, side * LANES : (side + 1) * LANES] * has_below
-        parts.append(jnp.where(from_below, theirs, strip[:, base + 2 * LANES : base + STRIP]))
+        parts.append(jnp.where(from_below, below, strip[:, base + 2 * LANES : base + STRIP]))
     return jnp.concatenate(parts, axis=1)
 
 
@@ -237,7 +241,8 @@
 
 def state_kernel(
     rows_ref, edge_ref, left_ref, right_ref, weight_ref, bias_ref,
-    gates_hbm, strip_gates_ref, wide_bias_ref, strip_ref, mark_ref, gates, three, patches, sems,
+    gates_hbm, strip_gates_ref, wide_bias_ref, strip_ref, mark_ref, up_ref, down_ref,
+    gates, three, patches, sems,
 ):
     units = rows_ref.shape[1] // 2
     count = rows_ref.shape[0]
@@ -246,6 +251,9 @@
     left, right = strips_of(edge_ref[:channels], left_ref[:channels], right_ref[:channels])
     strip_ref[:, :STRIP] = left
     strip_ref[:, STRIP:] = right
+    for ref, hidden_row, cell_row in ((up_ref, 0, 0), (down_ref, count - 3, count - 2)):
+        ref[:3] = rows_ref[hidden_row : hidden_row + 3, :units]
+        ref[3:] = rows_ref[cell_row : cell_row + 2, units:]
     near = lane_of(mark_ref.shape) % 8 < 4
     from_left = left_ref[channels:, :LANES].astype(F32)
     mark_ref[...] = jnp.where(near, from_left, right_ref[channels:, :LANES].astype(F32))
@@ -371,7 +379,8 @@
 
 
 def edge_kernel(
-    flag_ref, rows_ref, strip_ref, forcing_ref, forcing_strip_ref, above_ref, below_ref,
+    flag_ref, rows_ref, strip_ref, forcing_ref, forcing_strip_ref,
+    above_ref, below_ref, f_above_ref, f_below_ref,
     in_weight_ref, weight_ref, bias_ref,
     inner_hidden_ref, inner_cell_ref, sums_ref, first_ref, second_ref, memory_ref,
     hidden_ref, cell_ref,
@@ -386,7 +395,13 @@
 
     channels = forcing_ref.shape[1]
     joined = jnp.concatenate([forcing_strip_ref[...], strip_ref[...]], axis=0)
-    joined = ends_of(full_strip(joined, above_ref[3], below_ref[3], bf_above, bf_below))
+
+    def strips_in(ref, present):
+        packed = ref[3 * channels :] * present
+        return jnp.concatenate([packed[:, :LANES], packed[channels:, LANES:]], axis=0)
+
+    joined = full_strip(joined, strips_in(f_above_ref, bf_above), strips_in(f_below_ref, bf_below))
+    joined = ends_of(joined)
     strip = joined[:channels]
     state_strip = joined[channels : channels + units]
     strip_forcing = matmul(in_weight_ref[...], strip_taps(strip)) + jnp.concatenate([bias] * 2, axis=1)
@@ -398,10 +413,9 @@
         store_three(three, r, hidden, patches[r][channels:])
 
     for i in range(3):
-        ahead = above_ref[i, : channels + units] * bf_above
-        place(1 + i, ahead[:channels], ahead[channels:])
-        ahead = below_ref[i, : channels + units] * bf_below
-        place(count + PAD + i, ahead[:channels], ahead[channels:])
+        line = slice(i * channels, (i + 1) * channels)
+        place(1 + i, f_above_ref[line] * bf_above, above_ref[i] * bf_above)
+        place(count + PAD + i, f_below_ref[line] * bf_below, below_ref[i] * bf_below)
     for r in edge_rows(count, 0, 2):
         place(r, forcing_ref[r - PAD], rows_ref[r - PAD, :units])
 
@@ -427,9 +441,8 @@
         sums[r] = sums_ref[i]
         memory[r] = memory_ref[i]
     group = edge_rows(count, -2, 3)
-    cells = channels + units
-    olds = [above_ref[1, cells:], above_ref[2, cells:], rows_ref[0, units:]]
-    olds += [rows_ref[count - 1, units:], below_ref[0, cells:], below_ref[1, cells:]]
+    olds = [above_ref[3], above_ref[4], rows_ref[0, units:]]
+    olds += [rows_ref[count - 1, units:], below_ref[3], below_ref[4]]
     for r, old in zip(group, olds):
         sums[r] = matmul(in_weight_ref[...], row_taps(f_three, r)) + bias
         first_gates = sums[r] + matmul(weight_ref[...], row_taps(three, r))
@@ -483,7 +496,7 @@
 
 
 def scatter_kernel(
-    target_ref, count_ref, incoming_ref, mark_ref, state_ref, state_strip_ref,
+    target_ref, count_ref, incoming_ref, mark_ref, state_strip_ref,
     rows_ref, strip_ref, up_ref, down_ref, total,
 ):
     cap, sources = target_ref.shape
@@ -504,14 +517,15 @@
     left, right = strips_of(own, others, others)
     strip_ref[:, :STRIP] = left
     strip_ref[:, STRIP:] = right
+    state = state_strip_ref.shape[0] // 2
     for ref, first, tile in ((up_ref, 0, 0), (down_ref, row_count - 3, 2)):
-        ref[:3, :channels] = rows_ref[first : first + 3]
-        ref[:3, channels:] = state_ref[first : first + 3]
-        spot = tile * LANES
-        ref[3, :channels, :LANES] = left[:, spot : spot + LANES]
-        ref[3, :channels, LANES:] = right[:, spot : spot + LANES]
-        ref[3, channels:, :LANES] = state_strip_ref[:, spot : spot + LANES]
-        ref[3, channels:, LANES:] = state_strip_ref[:, STRIP + spot : STRIP + spot + LANES]
+        for i in range(3):
+            ref[i * channels : (i + 1) * channels, :] = rows_ref[first + i]
+        spots = [slice(base + tile * LANES, base + (tile + 1) * LANES) for base in (0, STRIP)]
+        packed = pack_strips(*[state_strip_ref[:, spot] for spot in spots])
+        own_packed = pack_strips(left[:, spots[0]], right[:, spots[0]])
+        ref[3 * channels :, :LANES] = jnp.concatenate([own_packed, packed[:state]], axis=0)
+        ref[3 * channels :, LANES:] = jnp.concatenate([own_packed, packed[state:]], axis=0)
 
 
 def around(count):
@@ -606,7 +620,8 @@
     padded = row_count + 8
     inside = (row_count - 2, gates, column_count)
     parts = inside[0] // PIECE
-    state_gates, strip_gates, bias, strip, marks = call(
+    ends = jax.ShapeDtypeStruct((5, units, column_count), BF)
+    state_gates, strip_gates, bias, strip, marks, up, down = call(
         state_kernel,
         [
             pltpu.HBM(inside, F32),
@@ -614,6 +629,8 @@
             jax.ShapeDtypeStruct((gates, column_count), F32),
             jax.ShapeDtypeStruct((2 * units, 2 * STRIP), BF),
             jax.ShapeDtypeStruct((tiles, LANES), F32),
+            ends,
+            ends,
         ],
         6, 0,
         [
@@ -624,13 +641,14 @@
         ],
         "state_gates", 2 * gates * 9 * units * row_count * column_count,
         (rows, edge, from_left, from_right, state_weight, bias), 16,
-        out_specs=[pl.BlockSpec(memory_space=pl.ANY)] + whole(4),
+        out_specs=[pl.BlockSpec(memory_space=pl.ANY)] + whole(6),
     )
+    above, below = exchange_rows(up, down)
     incoming, state_gates, strip_gates, bias, in_weight = lax.optimization_barrier(
         (incoming, state_gates, strip_gates, bias, in_weight)
     )
 
-    ends = jax.ShapeDtypeStruct((4, channels + 2 * units, column_count), BF)
+    ends = jax.ShapeDtypeStruct((4 * channels + units, column_count), BF)
     forcing, forcing_strip, up, down = call(
         scatter_kernel,
         [
@@ -639,12 +657,12 @@
             ends,
             ends,
         ],
-        4, 2,
+        3, 2,
         [pltpu.VMEM((2 * row_count + 1, channels, block), F32)],
         "scatter_add", slots * channels * block,
-        (slot_target[0].T, tile_counts, incoming, marks, rows, strip),
+        (slot_target[0].T, tile_counts, incoming, marks, strip),
     )
-    above, below = exchange_rows(up, down)
+    f_above, f_below = exchange_rows(up, down)
     inner_rows = jax.ShapeDtypeStruct((row_count - 6, units, column_count), BF)
     threes = jax.ShapeDtypeStruct((4, 3 * units, column_count), BF)
     inner = call(
@@ -677,7 +695,7 @@
     return call(
         edge_kernel,
         [out, out],
-        15, 1,
+        17, 1,
         [
             pltpu.VMEM((padded, 3 * channels, column_count), BF),
             pltpu.VMEM((padded, 3 * units, column_count), BF),
@@ -687,7 +705,8 @@
             pltpu.VMEM((row_count, units, column_count), BF),
         ],
         "edges", 2 * gates * 9 * (channels + 3 * units) * 6 * column_count,
-        (flags, rows, strip, forcing, forcing_strip, above, below, in_weight, state_weight, bias, *inner), 16,
+        (flags, rows, strip, forcing, forcing_strip, above, below, f_above, f_below,
+         in_weight, state_weight, bias, *inner), 16,
     )
 
 

time: 44.7 us -> 44.2 us (0.989)
  waiting for transfers between devices: 8.21 us -> 2.08 us
  starting transfers between devices: 13.9 us -> 18.4 us
  other arithmetic: 0.25 us -> 0.91 us
    all_to_all x1, waiting for transfers between devices: 5.34 us -> 0.79 us  [on_device(): lax.all_to_all(outgoing, ('lat', 'lon'), split_axis=0, concat_axis=0, til...]
    ppermute x1 -> x2, starting transfers between devices: 2.51 us -> 6.33 us  [exchange_rows(): from_below = lax.ppermute(up, 'lat', back(count))]
    ppermute x1 -> x2, waiting for transfers between devices: 0.87 us -> 0.01 us  [exchange_rows(): from_below = lax.ppermute(up, 'lat', back(count))]
    ppermute x1, waiting for transfers between devices: 1.99 us -> 1.27 us  [exchange_columns(): from_left = lax.ppermute(edge, 'lon', around(count))]
    ppermute x1 -> x2, starting transfers between devices: 1.36 us -> 2.08 us  [exchange_rows(): from_above = lax.ppermute(down, 'lat', around(count))]
    broadcast_in_dim x1, other arithmetic: 0.01 us -> 0.66 us  [on_device(): bias = (gate_bias * half)[:, None]]
    unnamed x8 -> x6, local copies, waits for them, and re-layouts: 1.88 us -> 1.87 us
  transfers between devices with their start and end apart: 5 -> 7, of which waited for: 3 -> 2; matrix products, arithmetic and copies ran while one was open for 5% -> 7% of each run, Pallas kernels for 23% -> 28%
where the time goes in v6:
time: 44.2 us; the launch traced here: 43.5 us
  Pallas kernels  19.4 us (44%)
  starting transfers between devices  18.4 us (42%)
  waiting for transfers between devices  2.08 us (5%)
  local copies, waits for them, and re-layouts  1.99 us (5%)
  other arithmetic  0.91 us (2%)
  between operations  0.77 us (2%)
    pallas_call x4, Pallas kernels, call(): pl.pallas_call(kernel, out_shape=tuple(outs), in_specs=in_specs or scalar...  13.9 us
    all_to_all x1, starting transfers between devices, on_device(): lax.all_to_all(outgoing, ('lat', 'lon'), split_axis=0, concat_axis=0, til...  7.3 us
    ppermute x2, starting transfers between devices, exchange_rows(): from_below = lax.ppermute(up, 'lat', back(count))  6.33 us
    pallas_call x1, Pallas kernels, on_device(): pl.pallas_call(functools.partial(gather_kernel, ring), out_shape=pltpu.HB...  3.92 us
    ppermute x1, starting transfers between devices, exchange_columns(): from_right = lax.ppermute(edge, 'lon', back(count))  2.39 us
    ppermute x2, starting transfers between devices, exchange_rows(): from_above = lax.ppermute(down, 'lat', around(count))  2.08 us
    unnamed x6, local copies, waits for them, and re-layouts  1.87 us
    pallas_call x1, Pallas kernels, on_device(): pl.pallas_call(prepare_kernel, out_shape=(jax.ShapeDtypeStruct((row_count...  1.57 us
  transfers between devices with their start and end apart: 7, of which 2 were waited for; matrix products, arithmetic and copies ran while one was open for 7% of the time, Pallas kernels for 28%

profile of v6, /device:TPU:0, one launch (start us, length us, event | category | flops | bytes accessed | tf_op | source)
XLA Modules:
  0.0 43.5 jit_solution(14802689907441386632)
XLA Ops:
  0.6 0.0 copy-start
  0.6 0.0 copy-start.1
  0.7 3.9 %gather_band.1 = bf16[32,72,128]{2,1,0:T(8,128)(2,1)} custom-call(s32[4,32]{1,0:T(4,128)} %bitcast.14, bf16[128,16,128]{2,1,0:T(8,128)(2,1)} %blocks_hbm.1, bf16[128,8,128]{2,1,0:T(8,128)(2,1)} %bitcast.13), custom_call_target="tpu_custom_call" | custom-call | tf_op jit(solution)/shard_map/gather_band/pallas_call | solution.py:581
  4.6 7.3 %all-to-all-start = ((bf16[32,72,128]{2,1,0:T(8,128)(2,1)}), bf16[32,72,128]{2,1,0:T(8,128)(2,1)S(1)}, u32[]{:S(2)}, u32[]{:S(2)}) async-start(bf16[32,72,128]{2,1,0:T(8,128)(2,1)} %gather_band.1), calls=%async_computation | async-start | bytes 1179648 | tf_op jit(solution)/shard_map/all_to_all | solution.py:599
  11.9 1.6 %prepare.1 = (bf16[32,64,256]{2,1,0:T(8,128)(2,1)S(1)}, bf16[96,384]{1,0:T(8,128)(2,1)S(1)}) custom-call(bf16[32,32,256]{2,1,0:T(8,128)(2,1)} %hidden_hbm.1, bf16[32,32,256]{2,1,0:T(8,128)(2,1)} %cell_hbm.1, s32[4,32]{1,0:T(4,128)} %bitcast.11, s32[1,32]{1,0:T(1,128)} %count_ref.1), custom_call_target="tpu_custom_call" | custom-call | tf_op jit(solution)/shard_map/prepare/pallas_call | solution.py:601
  13.5 0.3 collective-permute-start
  13.8 2.4 %collective-permute-start.1 = (bf16[96,384]{1,0:T(8,128)(2,1)S(1)}, bf16[96,384]{1,0:T(8,128)(2,1)S(1)}, u32[]{:S(2)}, u32[]{:S(2)}) collective-permute-start(bf16[96,384]{1,0:T(8,128)(2,1)S(1)} %get-tuple-element.27.edge_ref), channel_id=1, source_target_pairs={{1,0},{2,1},{3,2},{4,3},{5,4},{6,5},{7,6},{0,7},{9,8},{10,9},{11,1... | collective-permute-start | bytes 221192 | tf_op jit(solution)/shard_map/ppermute | solution.py:542
  16.2 1.0 %copy.12 = bf16[128,288]{1,0:T(8,128)(2,1)S(1)} copy(bf16[128,288]{0,1:T(8,128)(2,1)} %param.16) | data formatting | bytes 147456 | tf_op args[6]
  17.2 0.7 %multiply_bitcast_fusion = f32[128,1]{0,1:T(1,128)S(1)} fusion(f32[128]{0:T(128)} %param.17), kind=kLoop, calls=%fused_computation.4 | loop fusion | flops 384 | bytes 1024 | tf_op jit(solution)/shard_map/broadcast_in_dim | solution.py:573
  17.8 0.1 copy.13.bias_ref
  17.9 0.9 %copy.14 = bf16[128,144]{1,0:T(8,128)(2,1)S(1)} copy(bf16[128,144]{0,1:T(8,128)(2,1)} %param.15) | data formatting | bytes 73728 | tf_op args[5]
  18.8 0.1 broadcast_multiply_fusion.1.in_weight_ref
  18.9 0.1 broadcast_multiply_fusion.weight_ref
  19.0 0.1 add_convert_fusion.flag_ref
  19.1 1.3 %collective-permute-done.left_ref = bf16[96,384]{1,0:T(8,128)(2,1)S(1)} collective-permute-done((bf16[96,384]{1,0:T(8,128)(2,1)S(1)}, bf16[96,384]{1,0:T(8,128)(2,1)S(1)}, u32[]{:S(2)}, u32[]{:S(2)}) %collective-permute-start) | collective-permute-done | bytes 73760 | tf_op jit(solution)/shard_map/ppermute | solution.py:541
  20.4 0.0 collective-permute-done.1.right_ref
  20.4 2.9 %state_gates.1 = (f32[30,128,256]{2,1,0:T(8,128)}, f32[128,768]{1,0:T(8,128)S(1)}, f32[128,256]{1,0:T(8,128)S(1)}, bf16[64,768]{1,0:T(8,128)(2,1)S(1)}, f32[32,1...) custom-call(bf16[32,64,256]{2,1,0:T(8,128)(2,1)S(1)} %get-tuple-element.26.rows_ref, ...), custom_call_target="tpu_custom_call" | custom-call | flops 603979776 | bytes 1344000 | tf_op jit(solution)/shard_map/state_gates/pallas_call | solution.py:40
  23.3 0.7 %collective-permute-start.2 = (bf16[5,32,256]{2,1,0:T(8,128)(2,1)S(1)}, bf16[5,32,256]{2,1,0:T(8,128)(2,1)S(1)}, u32[]{:S(2)}, u32[]{:S(2)}) collective-permute-start(bf16[5,32,256]{2,1,0:T(8,128)(2,1)S(1)} %get-tuple-element.36), channel_id=1, source_target_pairs={{0,8},{8,16},{16,24},{24,0},{1,9},{9,17},{17,25},{25,1},{2,10},{10... | collective-permute-start | bytes 245768 | tf_op jit(solution)/shard_map/ppermute | solution.py:548
  24.0 3.9 %collective-permute-start.3 = (bf16[5,32,256]{2,1,0:T(8,128)(2,1)S(1)}, bf16[5,32,256]{2,1,0:T(8,128)(2,1)S(1)}, u32[]{:S(2)}, u32[]{:S(2)}) collective-permute-start(bf16[5,32,256]{2,1,0:T(8,128)(2,1)S(1)} %get-tuple-element.37), channel_id=1, source_target_pairs={{8,0},{16,8},{24,16},{0,24},{9,1},{17,9},{25,17},{1,25},{10,2},{18... | collective-permute-start | bytes 245768 | tf_op jit(solution)/shard_map/ppermute | solution.py:549
  27.8 0.8 %all-to-all-done.incoming_ref = bf16[32,72,128]{2,1,0:T(8,128)(2,1)S(1)} async-done(((bf16[32,72,128]{2,1,0:T(8,128)(2,1)}), bf16[32,72,128]{2,1,0:T(8,128)(2,1)S(1)}, u32[]{:S(2)}, u32[]{:S(2)}) %all-to-all-start) | async-done | bytes 589856 | tf_op jit(solution)/shard_map/all_to_all | solution.py:599
  28.6 0.0 copy-done
  28.6 0.0 copy-done.1
  28.6 1.9 %scatter_add.1 = (bf16[32,16,256]{2,1,0:T(8,128)(2,1)S(1)}, bf16[16,768]{1,0:T(8,128)(2,1)S(1)}, bf16[96,256]{1,0:T(8,128)(2,1)S(1)}, bf16[96,256]{1,0:T(8,128)(2,1)S(1)}) custom-call(s32[4,32]{1,0:T(4,128)S(1)} %bitcast.12, s32[1,32]{1,0:T(1,128)S(1)} %copy-done.1, bf16[32,72,128]{2,1,0:T(8,128)(2,1)S(1)} %all-to-all-done.incoming_ref, ...), custom_call_target="tpu_custom_call" | custom-call | flops 262144 | bytes 705152 | tf_op jit(solution)/shard_map/scatter_add/pallas_call | solution.py:40
  30.5 1.4 %collective-permute-start.4 = (bf16[96,256]{1,0:T(8,128)(2,1)S(1)}, bf16[96,256]{1,0:T(8,128)(2,1)S(1)}, u32[]{:S(2)}, u32[]{:S(2)}) collective-permute-start(bf16[96,256]{1,0:T(8,128)(2,1)S(1)} %get-tuple-element.38), channel_id=1, source_target_pairs={{0,8},{8,16},{16,24},{24,0},{1,9},{9,17},{17,25},{25,1},{2,10},{10... | collective-permute-start | bytes 147464 | tf_op jit(solution)/shard_map/ppermute | solution.py:548
  31.9 2.5 %collective-permute-start.5 = (bf16[96,256]{1,0:T(8,128)(2,1)S(1)}, bf16[96,256]{1,0:T(8,128)(2,1)S(1)}, u32[]{:S(2)}, u32[]{:S(2)}) collective-permute-start(bf16[96,256]{1,0:T(8,128)(2,1)S(1)} %get-tuple-element.39), channel_id=1, source_target_pairs={{8,0},{16,8},{24,16},{0,24},{9,1},{17,9},{25,17},{1,25},{10,2},{18... | collective-permute-start | bytes 147464 | tf_op jit(solution)/shard_map/ppermute | solution.py:549
  34.4 5.6 %inner.1 = (bf16[26,32,256]{2,1,0:T(8,128)(2,1)S(1)}, bf16[26,32,256]{2,1,0:T(8,128)(2,1)S(1)}, f32[4,128,256]{2,1,0:T(8,128)S(1)}, bf16[4,96,256]{2,1,0:T(8,128...) custom-call(f32[30,128,256]{2,1,0:T(8,128)} %get-tuple-element.42.gates_hbm, ...), custom_call_target="tpu_custom_call" | custom-call | flops 1509949440 | bytes 6000640 | tf_op jit(solution)/shard_map/inner/pallas_call | solution.py:40
  40.0 0.0 collective-permute-done.2.above_ref
  40.0 0.0 collective-permute-done.3.below_ref
  40.0 0.0 collective-permute-done.4.f_above_ref
  40.0 0.0 collective-permute-done.5.f_below_ref
  40.1 3.5 %edges.1 = (bf16[32,32,256]{2,1,0:T(8,128)(2,1)}, bf16[32,32,256]{2,1,0:T(8,128)(2,1)}) custom-call(s32[2]{0:T(128)S(1)} %add_convert_fusion.flag_ref, bf16[32,64,256]{2,1,0:T(8,128)(2,1)S(1)} %get-tuple-element.26.rows_ref, bf16[64,768]{1,0:T(8,128)(2,1)S(1)} %get-tuple-element.28.state_strip_ref.strip_ref, ...), custom_call_target="tpu_custom_call" | custom-call | flops 396361728 | bytes 3837960 | tf_op jit(solution)/shard_map/edges/pallas_call | solution.py:40
  (1 shorter events, 0.0 us)
Async XLA Ops:
  0.6 28.0 %copy-start = (s32[1,32,4]{1,2,0:T(4,128)S(1)}, s32[1,32,4]{1,2,0:T(4,128)}, u32[]{:S(2)}) copy-start(s32[1,32,4]{1,2,0:T(4,128)} %param.13) | copy-start | bytes 1540
  0.6 28.0 %copy-start.1 = (s32[1,32]{1,0:T(1,128)S(1)}, s32[1,32]{1,0:T(1,128)}, u32[]{:S(2)}) copy-start(s32[1,32]{1,0:T(1,128)} %count_ref.1) | copy-start | bytes 388
  4.6 24.0 %all-to-all-start = ((bf16[32,72,128]{2,1,0:T(8,128)(2,1)}), bf16[32,72,128]{2,1,0:T(8,128)(2,1)S(1)}, u32[]{:S(2)}, u32[]{:S(2)}) async-start(bf16[32,72,128]{2,1,0:T(8,128)(2,1)} %gather_band.1), calls=%async_computation | async-start | bytes 1179648 | tf_op jit(solution)/shard_map/all_to_all | solution.py:599
  13.5 6.9 %collective-permute-start = (bf16[96,384]{1,0:T(8,128)(2,1)S(1)}, bf16[96,384]{1,0:T(8,128)(2,1)S(1)}, u32[]{:S(2)}, u32[]{:S(2)}) collective-permute-start(bf16[96,384]{1,0:T(8,128)(2,1)S(1)} %get-tuple-element.27.edge_ref), channel_id=1, source_target_pairs={{0,1},{1,2},{2,3},{3,4},{4,5},{5,6},{6,7},{7,0},{8,9},{9,10},{10,1... | collective-permute-start | bytes 221192 | tf_op jit(solution)/shard_map/ppermute | solution.py:541
  13.8 6.6 %collective-permute-start.1 = (bf16[96,384]{1,0:T(8,128)(2,1)S(1)}, bf16[96,384]{1,0:T(8,128)(2,1)S(1)}, u32[]{:S(2)}, u32[]{:S(2)}) collective-permute-start(bf16[96,384]{1,0:T(8,128)(2,1)S(1)} %get-tuple-element.27.edge_ref), channel_id=1, source_target_pairs={{1,0},{2,1},{3,2},{4,3},{5,4},{6,5},{7,6},{0,7},{9,8},{10,9},{11,1... | collective-permute-start | bytes 221192 | tf_op jit(solution)/shard_map/ppermute | solution.py:542
  23.3 16.7 %collective-permute-start.2 = (bf16[5,32,256]{2,1,0:T(8,128)(2,1)S(1)}, bf16[5,32,256]{2,1,0:T(8,128)(2,1)S(1)}, u32[]{:S(2)}, u32[]{:S(2)}) collective-permute-start(bf16[5,32,256]{2,1,0:T(8,128)(2,1)S(1)} %get-tuple-element.36), channel_id=1, source_target_pairs={{0,8},{8,16},{16,24},{24,0},{1,9},{9,17},{17,25},{25,1},{2,10},{10... | collective-permute-start | bytes 245768 | tf_op jit(solution)/shard_map/ppermute | solution.py:548
  24.0 16.1 %collective-permute-start.3 = (bf16[5,32,256]{2,1,0:T(8,128)(2,1)S(1)}, bf16[5,32,256]{2,1,0:T(8,128)(2,1)S(1)}, u32[]{:S(2)}, u32[]{:S(2)}) collective-permute-start(bf16[5,32,256]{2,1,0:T(8,128)(2,1)S(1)} %get-tuple-element.37), channel_id=1, source_target_pairs={{8,0},{16,8},{24,16},{0,24},{9,1},{17,9},{25,17},{1,25},{10,2},{18... | collective-permute-start | bytes 245768 | tf_op jit(solution)/shard_map/ppermute | solution.py:549
  30.5 9.5 %collective-permute-start.4 = (bf16[96,256]{1,0:T(8,128)(2,1)S(1)}, bf16[96,256]{1,0:T(8,128)(2,1)S(1)}, u32[]{:S(2)}, u32[]{:S(2)}) collective-permute-start(bf16[96,256]{1,0:T(8,128)(2,1)S(1)} %get-tuple-element.38), channel_id=1, source_target_pairs={{0,8},{8,16},{16,24},{24,0},{1,9},{9,17},{17,25},{25,1},{2,10},{10... | collective-permute-start | bytes 147464 | tf_op jit(solution)/shard_map/ppermute | solution.py:548
  31.9 8.1 %collective-permute-start.5 = (bf16[96,256]{1,0:T(8,128)(2,1)S(1)}, bf16[96,256]{1,0:T(8,128)(2,1)S(1)}, u32[]{:S(2)}, u32[]{:S(2)}) collective-permute-start(bf16[96,256]{1,0:T(8,128)(2,1)S(1)} %get-tuple-element.39), channel_id=1, source_target_pairs={{8,0},{16,8},{24,16},{0,24},{9,1},{17,9},{25,17},{1,25},{10,2},{18... | collective-permute-start | bytes 147464 | tf_op jit(solution)/shard_map/ppermute | solution.py:549

commit v7 on v6

--- a/solution.py
+++ b/solution.py
@@ -124,7 +124,8 @@
 
 
 def prepare_kernel(
-    hidden_hbm, cell_hbm, target_hbm, count_hbm, rows_ref, edge_ref, hidden, cell, target_ref, count_ref, sems
+    flag_ref, hidden_hbm, cell_hbm, target_hbm, count_hbm, rows_ref, edge_ref, outer_ref, inner_ref,
+    hidden, cell, target_ref, count_ref, sems,
 ):
     fetches = [
         pltpu.make_async_copy(source, target, sems.at[i])
@@ -143,6 +144,10 @@
     rows_ref[:, :units, :] = jnp.swapaxes(hidden[...], 0, 1)
     fetches[3].wait()
     rows_ref[:, units:, :] = jnp.swapaxes(cell[...], 0, 1)
+    hidden_rows = rows_ref[:3, :units], rows_ref[row_count - 3 :, :units]
+    cell_rows = rows_ref[:2, units:], rows_ref[row_count - 2 :, units:]
+    outer_ref[:3], inner_ref[:3] = for_partners(flag_ref[2], *hidden_rows)
+    outer_ref[3:], inner_ref[3:] = for_partners(flag_ref[2], *cell_rows)
     tiles = edge_tiles(lambda y: rows_ref[y], row_count, 2 * units)
     for t, tile in enumerate(tiles):
         edge_ref[: 2 * units, t * LANES : (t + 1) * LANES] = tile
@@ -239,9 +244,14 @@
     return jnp.dot(weights, taps, preferred_element_type=F32)
 
 
+def for_partners(odd, up, down):
+    odd = odd == 1
+    return jnp.where(odd, up, down), jnp.where(odd, down, up)
+
+
 def state_kernel(
     rows_ref, edge_ref, left_ref, right_ref, weight_ref, bias_ref,
-    gates_hbm, strip_gates_ref, wide_bias_ref, strip_ref, mark_ref, up_ref, down_ref,
+    gates_hbm, wide_bias_ref, strip_ref, mark_ref,
     gates, three, patches, sems,
 ):
     units = rows_ref.shape[1] // 2
@@ -251,14 +261,10 @@
     left, right = strips_of(edge_ref[:channels], left_ref[:channels], right_ref[:channels])
     strip_ref[:, :STRIP] = left
     strip_ref[:, STRIP:] = right
-    for ref, hidden_row, cell_row in ((up_ref, 0, 0), (down_ref, count - 3, count - 2)):
-        ref[:3] = rows_ref[hidden_row : hidden_row + 3, :units]
-        ref[3:] = rows_ref[cell_row : cell_row + 2, units:]
     near = lane_of(mark_ref.shape) % 8 < 4
     from_left = left_ref[channels:, :LANES].astype(F32)
     mark_ref[...] = jnp.where(near, from_left, right_ref[channels:, :LANES].astype(F32))
     strip = jnp.concatenate([left[:units], right[:units]], axis=1)
-    strip_gates_ref[...] = matmul(weight_ref[...], strip_taps(strip))
     store_patches(strip, patches, PAD, count + PAD)
     for y in range(count):
         store_three(three, y + PAD, rows_ref[y, :units], patches[y + PAD])
@@ -277,17 +283,6 @@
     return [pltpu.make_async_copy(source.at[s], target.at[s], sems.at[i]) for i, s in enumerate(spots)]
 
 
-def ends_of(strip):
-    return jnp.concatenate([strip[:, t * LANES : (t + 1) * LANES] for t in (0, 2, 3, 5)], axis=1)
-
-
-def edge_patches(strip, first, last, count):
-    found = patches_of(strip, (0, 2), first, last)
-    mirror = count + 2 * PAD - 1
-    found.update(patches_of(strip, (0, 2), mirror - last + 1, mirror - first + 1))
-    return found
-
-
 def update(gates, memory):
     units = memory.shape[0]
     ingate = 0.5 * jnp.tanh(gates[:units]) + 0.5
@@ -297,80 +292,27 @@
     return outgate * jnp.tanh(memory), memory
 
 
-def inner_kernel(
-    gates_hbm, strip_gates_ref, rows_ref, strip_ref, forcing_ref, forcing_strip_ref,
-    in_weight_ref, weight_ref, bias_ref,
-    hidden_ref, cell_ref, sums_ref, first_ref, second_ref, memory_ref,
-    gates, f_three, f_patches, f_gates, first, second, patches, memory, sems,
-):
-    units = rows_ref.shape[1] // 2
+def early_kernel(
+    gates_hbm, rows_ref, forcing_ref, forcing_strip_ref, in_weight_ref, bias_ref,
+    sums_ref, hidden_ref, memory_ref, gates, f_three, f_patches, sems,
+):
+    units = hidden_ref.shape[1]
     count = rows_ref.shape[0]
     bias = bias_ref[...]
     fetches = pieces(gates_hbm, gates, sems)
     for fetch in fetches:
         fetch.start()
-
-    strip = forcing_strip_ref[...]
-    strip_forcing = matmul(in_weight_ref[...], strip_taps(strip)) + jnp.concatenate([bias] * 3, axis=1)
-    store_patches(strip, f_patches, PAD, count + PAD)
+    store_patches(forcing_strip_ref[...], f_patches, PAD, count + PAD)
     for y in range(count):
         store_three(f_three, y + PAD, forcing_ref[y], f_patches[y + PAD])
-
-    strip_memory = strip_ref[units:].astype(F32)
-    strip_hidden, strip_memory = update(strip_gates_ref[...] + strip_forcing, strip_memory)
-    strip_hidden = strip_hidden.astype(BF)
-    store_patches(strip_hidden, patches, PAD + 1, count + PAD - 1)
-
-    def run(margin, body):
-        stop = PAD + count - margin
-        for start in range(PAD + margin, stop, BATCH):
-            body(range(start, min(start + BATCH, stop)))
-
-    def first_rows(group):
-        for r in group:
-            if (r - PAD - 1) % PIECE == 0:
-                fetches[(r - PAD - 1) // PIECE].wait()
-        sums = [matmul(in_weight_ref[...], row_taps(f_three, r)) + bias for r in group]
-        states = [
-            update(gates[r - PAD - 1] + s, rows_ref[r - PAD, units:].astype(F32)) for r, s in zip(group, sums)
-        ]
-        marks = [patches[r] for r in group]
-        for r, s, (hidden, new), mark in zip(group, sums, states, marks):
-            f_gates[r] = s
-            memory[r] = new
-            store_three(first, r, hidden.astype(BF), mark)
-
-    run(1, first_rows)
-
-    strip_gates = matmul(weight_ref[...], strip_taps(strip_hidden)) + strip_forcing
-    strip_hidden, strip_memory = update(strip_gates, strip_memory)
-    store_patches(strip_hidden.astype(BF), patches, PAD + 2, count + PAD - 2)
-
-    def later(source, group):
-        sums = [f_gates[r] + matmul(weight_ref[...], row_taps(source, r)) for r in group]
-        return [update(s, memory[r]) for r, s in zip(group, sums)]
-
-    def second_rows(group):
-        states = later(first, group)
-        marks = [patches[r] for r in group]
-        for r, (hidden, new), mark in zip(group, states, marks):
-            memory[r] = new
-            store_three(second, r, hidden.astype(BF), mark)
-
-    run(2, second_rows)
-
-    def third_rows(group):
-        for r, (hidden, new) in zip(group, later(second, group)):
-            hidden_ref[r - PAD - 3] = hidden.astype(BF)
-            cell_ref[r - PAD - 3] = new.astype(BF)
-
-    run(3, third_rows)
-    for i, r in enumerate(edge_rows(count, 1, 2)):
-        sums_ref[i] = f_gates[r]
-        first_ref[i] = first[r]
-        memory_ref[i] = memory[r]
-    for i, r in enumerate(edge_rows(count, 2, 2)):
-        second_ref[i] = second[r]
+    for i in range(count - 2):
+        if i % PIECE == 0:
+            fetches[i // PIECE].wait()
+        sums = matmul(in_weight_ref[...], row_taps(f_three, i + 1 + PAD)) + bias
+        hidden, memory = update(gates[i] + sums, rows_ref[i + 1, units:].astype(F32))
+        sums_ref[i] = sums
+        hidden_ref[i] = hidden.astype(BF)
+        memory_ref[i] = memory
 
 
 def edge_rows(count, depth, many):
@@ -378,49 +320,50 @@
     return top + [PAD + count - 1 - depth - (many - 1) + i for i in range(many)]
 
 
-def edge_kernel(
+def late_kernel(
     flag_ref, rows_ref, strip_ref, forcing_ref, forcing_strip_ref,
-    above_ref, below_ref, f_above_ref, f_below_ref,
-    in_weight_ref, weight_ref, bias_ref,
-    inner_hidden_ref, inner_cell_ref, sums_ref, first_ref, second_ref, memory_ref,
-    hidden_ref, cell_ref,
-    f_three, three, first, second, h_rows, c_rows,
+    outer_ref, inner_ref, f_outer_ref, f_inner_ref, in_weight_ref, weight_ref, bias_ref,
+    inner_sums_ref, inner_hidden_ref, inner_memory_ref,
+    hidden_hbm, cell_hbm,
+    f_three, three, first, second, sums, memory, patches, h_rows, c_rows, h_out, c_out, sems,
 ):
     units = rows_ref.shape[1] // 2
     count = rows_ref.shape[0]
+    channels = forcing_ref.shape[1]
     has_above = flag_ref[0].astype(F32)
     has_below = flag_ref[1].astype(F32)
     bf_above, bf_below = has_above.astype(BF), has_below.astype(BF)
     bias = bias_ref[...]
 
-    channels = forcing_ref.shape[1]
+    above, below = for_partners(flag_ref[2], outer_ref[...], inner_ref[...])
+    f_above, f_below = for_partners(flag_ref[2], f_outer_ref[...], f_inner_ref[...])
+
+    def strips_in(message, present):
+        packed = message[3 * channels :] * present
+        return jnp.concatenate([packed[:, :LANES], packed[channels:, LANES:]], axis=0)
+
     joined = jnp.concatenate([forcing_strip_ref[...], strip_ref[...]], axis=0)
-
-    def strips_in(ref, present):
-        packed = ref[3 * channels :] * present
-        return jnp.concatenate([packed[:, :LANES], packed[channels:, LANES:]], axis=0)
-
-    joined = full_strip(joined, strips_in(f_above_ref, bf_above), strips_in(f_below_ref, bf_below))
-    joined = ends_of(joined)
-    strip = joined[:channels]
+    joined = full_strip(joined, strips_in(f_above, bf_above), strips_in(f_below, bf_below))
+    strip_forcing = matmul(in_weight_ref[...], strip_taps(joined[:channels]))
+    strip_forcing = strip_forcing + jnp.concatenate([bias] * 3, axis=1)
     state_strip = joined[channels : channels + units]
-    strip_forcing = matmul(in_weight_ref[...], strip_taps(strip)) + jnp.concatenate([bias] * 2, axis=1)
     strip_gates = strip_forcing + matmul(weight_ref[...], strip_taps(state_strip))
-    patches = edge_patches(joined[: channels + units], 1, PAD + 2, count)
+    found = patches_of(joined[: channels + units], range(STRIP // LANES), 1, PAD + 2)
+    found.update(patches_of(joined[: channels + units], range(STRIP // LANES), count + PAD - 2, count + PAD + 3))
 
     def place(r, forcing, hidden):
-        store_three(f_three, r, forcing, patches[r][:channels])
-        store_three(three, r, hidden, patches[r][channels:])
+        store_three(f_three, r, forcing, found[r][:channels])
+        store_three(three, r, hidden, found[r][channels:])
 
     for i in range(3):
         line = slice(i * channels, (i + 1) * channels)
-        place(1 + i, f_above_ref[line] * bf_above, above_ref[i] * bf_above)
-        place(count + PAD + i, f_below_ref[line] * bf_below, below_ref[i] * bf_below)
+        place(1 + i, f_above[line] * bf_above, above[i] * bf_above)
+        place(count + PAD + i, f_below[line] * bf_below, below[i] * bf_below)
     for r in edge_rows(count, 0, 2):
         place(r, forcing_ref[r - PAD], rows_ref[r - PAD, :units])
 
-    lane = lane_of((units, strip.shape[1]))
-    row_of_lane = (lane % LANES) // 8 + 32 * (lane // LANES % 2)
+    lane = lane_of((units, 2 * STRIP))
+    row_of_lane = lane % STRIP // 8
     keep = jnp.where(row_of_lane < PAD, has_above, 1.0)
     keep = jnp.where(row_of_lane >= PAD + count, has_below, keep)
 
@@ -431,44 +374,49 @@
             hidden = hidden * has_below
         return hidden.astype(BF)
 
-    strip_memory = joined[channels + units :].astype(F32)
-    strip_hidden, strip_memory = update(strip_gates, strip_memory)
+    strip_hidden, strip_memory = update(strip_gates, joined[channels + units :].astype(F32))
     strip_hidden = (strip_hidden * keep).astype(BF)
-    marks = edge_patches(strip_hidden, 2, PAD + 1, count)
-
-    sums, memory = {}, {}
-    for i, r in enumerate(edge_rows(count, 1, 2)):
-        sums[r] = sums_ref[i]
-        memory[r] = memory_ref[i]
-    group = edge_rows(count, -2, 3)
-    olds = [above_ref[3], above_ref[4], rows_ref[0, units:]]
-    olds += [rows_ref[count - 1, units:], below_ref[3], below_ref[4]]
-    for r, old in zip(group, olds):
+    store_patches(strip_hidden, patches, 2, count + 6)
+    olds = [above[3], above[4], rows_ref[0, units:]]
+    olds += [rows_ref[count - 1, units:], below[3], below[4]]
+    for r, old in zip(edge_rows(count, -2, 3), olds):
         sums[r] = matmul(in_weight_ref[...], row_taps(f_three, r)) + bias
         first_gates = sums[r] + matmul(weight_ref[...], row_taps(three, r))
         hidden, memory[r] = update(first_gates, old.astype(F32))
-        store_three(first, r, kept(hidden, r), marks[r])
-    for i, r in enumerate(edge_rows(count, 1, 2)):
-        first[r] = first_ref[i]
+        store_three(first, r, kept(hidden, r), patches[r])
+    inner = range(PAD + 1, PAD + count - 1)
+    for i, r in enumerate(inner):
+        store_three(first, r, inner_hidden_ref[i], patches[r])
 
     strip_gates = matmul(weight_ref[...], strip_taps(strip_hidden)) + strip_forcing
     strip_hidden, strip_memory = update(strip_gates, strip_memory)
     strip_hidden = (strip_hidden * keep).astype(BF)
-    marks = edge_patches(strip_hidden, 3, PAD + 2, count)
-    for r in edge_rows(count, -1, 3):
-        hidden, memory[r] = update(sums[r] + matmul(weight_ref[...], row_taps(first, r)), memory[r])
-        store_three(second, r, kept(hidden, r), marks[r])
-    for i, r in enumerate(edge_rows(count, 2, 2)):
-        second[r] = second_ref[i]
-
-    for r in edge_rows(count, 0, 3):
-        hidden, new = update(sums[r] + matmul(weight_ref[...], row_taps(second, r)), memory[r])
-        h_rows[r - PAD] = hidden.astype(BF)
-        c_rows[r - PAD] = new.astype(BF)
-    h_rows[3 : count - 3] = inner_hidden_ref[...]
-    c_rows[3 : count - 3] = inner_cell_ref[...]
-    hidden_ref[...] = jnp.swapaxes(h_rows[...], 0, 1)
-    cell_ref[...] = jnp.swapaxes(c_rows[...], 0, 1)
+    store_patches(strip_hidden, patches, 3, count + 5)
+
+    def later(source, r, old):
+        total = inner_sums_ref[r - PAD - 1] if r in inner else sums[r]
+        return update(total + matmul(weight_ref[...], row_taps(source, r)), old)
+
+    for r in range(PAD - 1, PAD + count + 1):
+        old = inner_memory_ref[r - PAD - 1] if r in inner else memory[r]
+        hidden, memory[r] = later(first, r, old)
+        store_three(second, r, kept(hidden, r), patches[r])
+
+    sends = []
+    part = count // 2
+    for start in (0, part):
+        for y in range(start, start + part):
+            hidden, new = later(second, y + PAD, memory[y + PAD])
+            h_rows[y] = hidden.astype(BF)
+            c_rows[y] = new.astype(BF)
+        spot = pl.ds(start, part)
+        h_out[:, start : start + part, :] = jnp.swapaxes(h_rows[start : start + part], 0, 1)
+        c_out[:, start : start + part, :] = jnp.swapaxes(c_rows[start : start + part], 0, 1)
+        for source, target in ((h_out, hidden_hbm), (c_out, cell_hbm)):
+            sends.append(pltpu.make_async_copy(source.at[:, spot], target.at[:, spot], sems.at[len(sends)]))
+            sends[-1].start()
+    for send in sends:
+        send.wait()
 
 
 def beside(incoming_ref, mark_ref, row_count, channels):
@@ -496,36 +444,40 @@
 
 
 def scatter_kernel(
-    target_ref, count_ref, incoming_ref, mark_ref, state_strip_ref,
-    rows_ref, strip_ref, up_ref, down_ref, total,
+    flag_ref, target_ref, count_ref, incoming_ref, mark_ref, state_strip_ref,
+    rows_ref, strip_ref, outer_ref, inner_ref, *totals,
 ):
     cap, sources = target_ref.shape
     row_count, channels, width = rows_ref.shape
     width = width // 2
     spare = 2 * row_count
-    total[...] = jnp.zeros(total.shape, F32)
+    for total in totals:
+        total[...] = jnp.zeros(total.shape, F32)
     for p in range(sources):
         live = count_ref[0, p]
         for s in range(cap):
             block = jnp.where(s < live, target_ref[s, p], spare)
+            total = totals[s % len(totals)]
             total[block] = total[block] + incoming_ref[p, s * channels : (s + 1) * channels, :].astype(F32)
     for y in range(row_count):
-        rows_ref[y, :, :width] = total[2 * y].astype(BF)
-        rows_ref[y, :, width:] = total[2 * y + 1].astype(BF)
+        for half in range(2):
+            block = sum(total[2 * y + half] for total in totals)
+            rows_ref[y, :, half * width : (half + 1) * width] = block.astype(BF)
     own = jnp.concatenate(edge_tiles(lambda y: rows_ref[y], row_count, channels), axis=1)
     others = beside(incoming_ref, mark_ref, row_count, channels)
     left, right = strips_of(own, others, others)
     strip_ref[:, :STRIP] = left
     strip_ref[:, STRIP:] = right
     state = state_strip_ref.shape[0] // 2
-    for ref, first, tile in ((up_ref, 0, 0), (down_ref, row_count - 3, 2)):
-        for i in range(3):
-            ref[i * channels : (i + 1) * channels, :] = rows_ref[first + i]
+    messages = []
+    for first, tile in ((0, 0), (row_count - 3, 2)):
+        lines = [rows_ref[first + i] for i in range(3)]
         spots = [slice(base + tile * LANES, base + (tile + 1) * LANES) for base in (0, STRIP)]
         packed = pack_strips(*[state_strip_ref[:, spot] for spot in spots])
         own_packed = pack_strips(left[:, spots[0]], right[:, spots[0]])
-        ref[3 * channels :, :LANES] = jnp.concatenate([own_packed, packed[:state]], axis=0)
-        ref[3 * channels :, LANES:] = jnp.concatenate([own_packed, packed[state:]], axis=0)
+        halves = [jnp.concatenate([own_packed, part], axis=0) for part in (packed[:state], packed[state:])]
+        messages.append(jnp.concatenate([*lines, jnp.concatenate(halves, axis=1)], axis=0))
+    outer_ref[...], inner_ref[...] = for_partners(flag_ref[2], *messages)
 
 
 def around(count):
@@ -543,11 +495,18 @@
     return from_left, from_right
 
 
-def exchange_rows(up, down):
+def exchange_rows(outer, inner):
     count = lax.axis_size("lat")
-    from_above = lax.ppermute(down, "lat", around(count))
-    from_below = lax.ppermute(up, "lat", back(count))
-    return from_above, from_below
+
+    def swap(x, first):
+        partner = list(range(count))
+        for i in range(first, count - 1, 2):
+            partner[i], partner[i + 1] = i + 1, i
+        return lax.ppermute(x, "lat", list(enumerate(partner)))
+
+    got_outer = swap(outer, 0)
+    got_inner = swap(inner, 1)
+    return got_outer, got_inner
 
 
 def on_device(
@@ -572,7 +531,7 @@
     state_weight = gate_state_weight * half[:, None].astype(BF)
     bias = (gate_bias * half)[:, None]
     lat = lax.axis_index("lat")
-    flags = jnp.stack([lat > 0, lat < lax.axis_size("lat") - 1]).astype(jnp.int32)
+    flags = jnp.stack([lat > 0, lat < lax.axis_size("lat") - 1, lat % 2 == 1]).astype(jnp.int32)
 
     ring = lax.axis_size("lon")
     height = cap * channels + channels // 2
@@ -598,14 +557,17 @@
     )(in_hbm(slot_source[0].T), in_hbm(satellite_blocks), in_hbm(slot_weight.reshape(slots, band, block)))
     incoming = lax.all_to_all(outgoing, ("lat", "lon"), split_axis=0, concat_axis=0, tiled=True)
 
-    rows, edge = pl.pallas_call(
+    ends = jax.ShapeDtypeStruct((5, units, column_count), BF)
+    rows, edge, outer, inner = pl.pallas_call(
         prepare_kernel,
         out_shape=(
             jax.ShapeDtypeStruct((row_count, 2 * units, column_count), BF),
             jax.ShapeDtypeStruct((2 * units + tiles, STRIP), BF),
+            ends,
+            ends,
         ),
-        in_specs=[pl.BlockSpec(memory_space=pl.ANY)] * 4,
-        out_specs=tuple(whole(2)),
+        in_specs=scalars(1) + [pl.BlockSpec(memory_space=pl.ANY)] * 4,
+        out_specs=tuple(whole(4)),
         scratch_shapes=[
             pltpu.VMEM(hidden_init.shape, BF),
             pltpu.VMEM(cell_init.shape, BF),
@@ -615,22 +577,19 @@
         ],
         compiler_params=pltpu.CompilerParams(vmem_limit_bytes=8 * 2**20),
         name="prepare",
-    )(in_hbm(hidden_init), in_hbm(cell_init), in_hbm(slot_target[0].T), in_hbm(tile_counts))
+    )(flags, in_hbm(hidden_init), in_hbm(cell_init), in_hbm(slot_target[0].T), in_hbm(tile_counts))
     from_left, from_right = exchange_columns(edge)
+    outer, inner = exchange_rows(outer, inner)
     padded = row_count + 8
     inside = (row_count - 2, gates, column_count)
     parts = inside[0] // PIECE
-    ends = jax.ShapeDtypeStruct((5, units, column_count), BF)
-    state_gates, strip_gates, bias, strip, marks, up, down = call(
+    state_gates, bias, strip, marks = call(
         state_kernel,
         [
             pltpu.HBM(inside, F32),
-            jax.ShapeDtypeStruct((gates, 2 * STRIP), F32),
             jax.ShapeDtypeStruct((gates, column_count), F32),
             jax.ShapeDtypeStruct((2 * units, 2 * STRIP), BF),
             jax.ShapeDtypeStruct((tiles, LANES), F32),
-            ends,
-            ends,
         ],
         6, 0,
         [
@@ -641,15 +600,12 @@
         ],
         "state_gates", 2 * gates * 9 * units * row_count * column_count,
         (rows, edge, from_left, from_right, state_weight, bias), 16,
-        out_specs=[pl.BlockSpec(memory_space=pl.ANY)] + whole(6),
+        out_specs=[pl.BlockSpec(memory_space=pl.ANY)] + whole(3),
     )
-    above, below = exchange_rows(up, down)
-    incoming, state_gates, strip_gates, bias, in_weight = lax.optimization_barrier(
-        (incoming, state_gates, strip_gates, bias, in_weight)
-    )
+    incoming, state_gates, bias, in_weight = lax.optimization_barrier((incoming, state_gates, bias, in_weight))
 
     ends = jax.ShapeDtypeStruct((4 * channels + units, column_count), BF)
-    forcing, forcing_strip, up, down = call(
+    forcing, forcing_strip, f_outer, f_inner = call(
         scatter_kernel,
         [
             jax.ShapeDtypeStruct((row_count, channels, column_count), BF),
@@ -657,56 +613,52 @@
             ends,
             ends,
         ],
-        3, 2,
-        [pltpu.VMEM((2 * row_count + 1, channels, block), F32)],
+        3, 3,
+        [pltpu.VMEM((2 * row_count + 1, channels, block), F32)] * 2,
         "scatter_add", slots * channels * block,
-        (slot_target[0].T, tile_counts, incoming, marks, strip),
+        (flags, slot_target[0].T, tile_counts, incoming, marks, strip),
     )
-    f_above, f_below = exchange_rows(up, down)
-    inner_rows = jax.ShapeDtypeStruct((row_count - 6, units, column_count), BF)
-    threes = jax.ShapeDtypeStruct((4, 3 * units, column_count), BF)
-    inner = call(
-        inner_kernel,
+    f_outer, f_inner = exchange_rows(f_outer, f_inner)
+    sums, hidden, memory = call(
+        early_kernel,
         [
-            inner_rows,
-            inner_rows,
-            jax.ShapeDtypeStruct((4, gates, column_count), F32),
-            threes,
-            threes,
-            jax.ShapeDtypeStruct((4, units, column_count), F32),
-        ],
-        9, 0,
+            jax.ShapeDtypeStruct(inside, F32),
+            jax.ShapeDtypeStruct((inside[0], units, column_count), BF),
+            jax.ShapeDtypeStruct((inside[0], units, column_count), F32),
+        ],
+        6, 0,
         [
             pltpu.VMEM(inside, F32),
             pltpu.VMEM((padded, 3 * channels, column_count), BF),
             pltpu.VMEM((padded, channels, LANES), BF),
-            pltpu.VMEM((padded, gates, column_count), F32),
-            pltpu.VMEM((padded, 3 * units, column_count), BF),
-            pltpu.VMEM((padded, 3 * units, column_count), BF),
-            pltpu.VMEM((padded, units, LANES), BF),
-            pltpu.VMEM((padded, units, column_count), F32),
             pltpu.SemaphoreType.DMA((parts,)),
         ],
-        "inner", 2 * gates * 9 * (channels + 2 * units) * row_count * column_count,
-        (in_hbm(state_gates), strip_gates, rows, strip, forcing, forcing_strip, in_weight, state_weight, bias), 24,
-        in_specs=[pl.BlockSpec(memory_space=pl.ANY)] + whole(8),
+        "first_step", 2 * gates * 9 * channels * row_count * column_count,
+        (in_hbm(state_gates), rows, forcing, forcing_strip, in_weight, bias), 16,
+        in_specs=[pl.BlockSpec(memory_space=pl.ANY)] + whole(5),
     )
-    out = jax.ShapeDtypeStruct((units, row_count, column_count), BF)
     return call(
-        edge_kernel,
-        [out, out],
-        17, 1,
+        late_kernel,
+        [pltpu.HBM(hidden_init.shape, BF)] * 2,
+        14, 1,
         [
             pltpu.VMEM((padded, 3 * channels, column_count), BF),
             pltpu.VMEM((padded, 3 * units, column_count), BF),
             pltpu.VMEM((padded, 3 * units, column_count), BF),
             pltpu.VMEM((padded, 3 * units, column_count), BF),
+            pltpu.VMEM((padded, gates, column_count), F32),
+            pltpu.VMEM((padded, units, column_count), F32),
+            pltpu.VMEM((padded, units, LANES), BF),
             pltpu.VMEM((row_count, units, column_count), BF),
             pltpu.VMEM((row_count, units, column_count), BF),
-        ],
-        "edges", 2 * gates * 9 * (channels + 3 * units) * 6 * column_count,
-        (flags, rows, strip, forcing, forcing_strip, above, below, f_above, f_below,
-         in_weight, state_weight, bias, *inner), 16,
+            pltpu.VMEM(hidden_init.shape, BF),
+            pltpu.VMEM(hidden_init.shape, BF),
+            pltpu.SemaphoreType.DMA((4,)),
+        ],
+        "later_steps", 2 * gates * 9 * 2 * units * row_count * column_count,
+        (flags, rows, strip, forcing, forcing_strip, outer, inner, f_outer, f_inner,
+         in_weight, state_weight, bias, sums, hidden, memory), 24,
+        out_specs=[pl.BlockSpec(memory_space=pl.ANY)] * 2,
     )
 
 

time: 44.2 us -> 42 us (0.950)
  starting transfers between devices: 18.4 us -> 13.8 us
  waiting for transfers between devices: 2.08 us -> 5.05 us
  other arithmetic: 0.91 us -> 0.25 us
    ppermute x4, starting transfers between devices: 8.41 us -> 4.04 us  [swap(): return lax.ppermute(x, 'lat', list(enumerate(partner)))]
    all_to_all x1, waiting for transfers between devices: 0.79 us -> 3.59 us  [on_device(): lax.all_to_all(outgoing, ('lat', 'lon'), split_axis=0, concat_axis=0, til...]
    broadcast_in_dim x1, other arithmetic: 0.66 us -> 0.01 us  [on_device(): bias = (gate_bias * half)[:, None]]
    pallas_call x1, Pallas kernels: 1.57 us -> 2.12 us  [on_device(): pl.pallas_call(prepare_kernel, out_shape=(jax.ShapeDtypeStruct((row_count...]
    unnamed x6 -> x8, local copies, waits for them, and re-layouts: 1.87 us -> 1.88 us
  transfers between devices with their start and end apart: 7 -> 7, of which waited for: 2 -> 2; matrix products, arithmetic and copies ran while one was open for 7% -> 5% of each run, Pallas kernels for 28% -> 23%
where the time goes in v7:
time: 42 us; the launch traced here: 41.5 us
  Pallas kernels  19.5 us (46%)
  starting transfers between devices  13.8 us (33%)
  waiting for transfers between devices  5.05 us (12%)
  local copies, waits for them, and re-layouts  2 us (5%)
  between operations  0.81 us (2%)
    pallas_call x4, Pallas kernels, call(): pl.pallas_call(kernel, out_shape=tuple(outs), in_specs=in_specs or scalar...  13.5 us
    all_to_all x1, starting transfers between devices, on_device(): lax.all_to_all(outgoing, ('lat', 'lon'), split_axis=0, concat_axis=0, til...  7.3 us
    ppermute x4, starting transfers between devices, swap(): return lax.ppermute(x, 'lat', list(enumerate(partner)))  4.04 us
    pallas_call x1, Pallas kernels, on_device(): pl.pallas_call(functools.partial(gather_kernel, ring), out_shape=pltpu.HB...  3.93 us
    all_to_all x1, waiting for transfers between devices, on_device(): lax.all_to_all(outgoing, ('lat', 'lon'), split_axis=0, concat_axis=0, til...  3.59 us
    ppermute x1, starting transfers between devices, exchange_columns(): from_right = lax.ppermute(edge, 'lon', back(count))  2.47 us
    pallas_call x1, Pallas kernels, on_device(): pl.pallas_call(prepare_kernel, out_shape=(jax.ShapeDtypeStruct((row_count...  2.12 us
    unnamed x8, local copies, waits for them, and re-layouts  1.88 us
  transfers between devices with their start and end apart: 7, of which 2 were waited for; matrix products, arithmetic and copies ran while one was open for 5% of the time, Pallas kernels for 23%

profile of v7, /device:TPU:0, one launch (start us, length us, event | category | flops | bytes accessed | tf_op | source)
XLA Modules:
  0.0 41.5 jit_solution(8335341869943382305)
XLA Ops:
  0.6 0.0 copy-start.1
  0.6 0.0 copy-start
  0.7 0.0 copy-start.2
  0.7 3.9 %gather_band.1 = bf16[32,72,128]{2,1,0:T(8,128)(2,1)} custom-call(s32[4,32]{1,0:T(4,128)} %bitcast.15, bf16[128,16,128]{2,1,0:T(8,128)(2,1)} %blocks_hbm.1, bf16[128,8,128]{2,1,0:T(8,128)(2,1)} %bitcast.14), custom_call_target="tpu_custom_call" | custom-call | tf_op jit(solution)/shard_map/gather_band/pallas_call | solution.py:540
  4.6 7.3 %all-to-all-start = ((bf16[32,72,128]{2,1,0:T(8,128)(2,1)}), bf16[32,72,128]{2,1,0:T(8,128)(2,1)S(1)}, u32[]{:S(2)}, u32[]{:S(2)}) async-start(bf16[32,72,128]{2,1,0:T(8,128)(2,1)} %gather_band.1), calls=%async_computation | async-start | bytes 1179648 | tf_op jit(solution)/shard_map/all_to_all | solution.py:558
  11.9 0.1 add_convert_fusion.flag_ref
  12.0 2.1 %prepare.1 = (bf16[32,64,256]{2,1,0:T(8,128)(2,1)S(1)}, bf16[96,384]{1,0:T(8,128)(2,1)S(1)}, bf16[5,32,256]{2,1,0:T(8,128)(2,1)S(1)}, bf16[5,32,256]{2,1,0:T(8,128)(2,1)S(1)}) custom-call(s32[3]{0:T(128)S(1)} %add_convert_fusion.flag_ref, bf16[32,32,256]{2,1,0:T(8,128)(2,1)} %hidden_hbm.1, bf16[32,32,256]{2,1,0:T(8,128)(2,1)} %cell_hbm.1, s32[4,32]{1,0:T(4,128)} %bitcast.12, ...), custom_call_target="tpu_custom_call" | custom-call | tf_op jit(solution)/shard_map/prepare/pallas_call | solution.py:561
  14.1 2.5 %collective-permute-start.1 = (bf16[96,384]{1,0:T(8,128)(2,1)S(1)}, bf16[96,384]{1,0:T(8,128)(2,1)S(1)}, u32[]{:S(2)}, u32[]{:S(2)}) collective-permute-start(bf16[96,384]{1,0:T(8,128)(2,1)S(1)} %get-tuple-element.22.edge_ref), channel_id=1, source_target_pairs={{1,0},{2,1},{3,2},{4,3},{5,4},{6,5},{7,6},{0,7},{9,8},{10,9},{11,1... | collective-permute-start | bytes 221192 | tf_op jit(solution)/shard_map/ppermute | solution.py:494
  16.6 0.0 collective-permute-start
  16.6 1.5 %collective-permute-start.2 = (bf16[5,32,256]{2,1,0:T(8,128)(2,1)S(1)}, bf16[5,32,256]{2,1,0:T(8,128)(2,1)S(1)}, u32[]{:S(2)}, u32[]{:S(2)}) collective-permute-start(bf16[5,32,256]{2,1,0:T(8,128)(2,1)S(1)} %get-tuple-element.30), channel_id=1, source_target_pairs={{0,8},{8,0},{16,24},{24,16},{1,9},{9,1},{17,25},{25,17},{2,10},{10... | collective-permute-start | bytes 245768 | tf_op jit(solution)/shard_map/ppermute | solution.py:505
  18.1 0.7 %collective-permute-start.3 = (bf16[5,32,256]{2,1,0:T(8,128)(2,1)S(1)}, bf16[5,32,256]{2,1,0:T(8,128)(2,1)S(1)}, u32[]{:S(2)}, u32[]{:S(2)}) collective-permute-start(bf16[5,32,256]{2,1,0:T(8,128)(2,1)S(1)} %get-tuple-element.31), channel_id=1, source_target_pairs={{0,0},{8,16},{16,8},{24,24},{1,1},{9,17},{17,9},{25,25},{2,2},{10,... | collective-permute-start | bytes 245768 | tf_op jit(solution)/shard_map/ppermute | solution.py:505
  18.7 0.9 %copy.14 = bf16[128,144]{1,0:T(8,128)(2,1)S(1)} copy(bf16[128,144]{0,1:T(8,128)(2,1)} %param.15) | data formatting | bytes 73728 | tf_op args[5]
  19.6 1.0 %copy.12 = bf16[128,288]{1,0:T(8,128)(2,1)S(1)} copy(bf16[128,288]{0,1:T(8,128)(2,1)} %param.16) | data formatting | bytes 147456 | tf_op args[6]
  20.6 0.1 broadcast_multiply_fusion.1.in_weight_ref
  20.7 0.1 broadcast_multiply_fusion.weight_ref
  20.8 0.0 copy-done.2
  20.8 0.1 copy.13.bias_ref
  20.9 0.0 collective-permute-done.1.right_ref
  21.0 1.4 %collective-permute-done.left_ref = bf16[96,384]{1,0:T(8,128)(2,1)S(1)} collective-permute-done((bf16[96,384]{1,0:T(8,128)(2,1)S(1)}, bf16[96,384]{1,0:T(8,128)(2,1)S(1)}, u32[]{:S(2)}, u32[]{:S(2)}) %collective-permute-start) | collective-permute-done | bytes 73760 | tf_op jit(solution)/shard_map/ppermute | solution.py:493
  22.4 2.8 %state_gates.1 = (f32[30,128,256]{2,1,0:T(8,128)}, f32[128,256]{1,0:T(8,128)S(1)}, bf16[64,768]{1,0:T(8,128)(2,1)S(1)}, f32[32,128]{1,0:T(8,128)S(1)}) custom-call(bf16[32,64,256]{2,1,0:T(8,128)(2,1)S(1)} %get-tuple-element.21.rows_ref, bf16[96,384]{1,0:T(8,128)(2,1)S(1)} %get-tuple-element.22.edge_ref, bf16[96,384]{1,0:T(8,128)(2,1)S(1)} %collective-permute-done.left_ref, ...), custom_call_target="tpu_custom_call" | custom-call | flops 603979776 | bytes 1344000 | tf_op jit(solution)/shard_map/state_gates/pallas_call | solution.py:40
  25.2 3.6 %all-to-all-done.incoming_ref = bf16[32,72,128]{2,1,0:T(8,128)(2,1)S(1)} async-done(((bf16[32,72,128]{2,1,0:T(8,128)(2,1)}), bf16[32,72,128]{2,1,0:T(8,128)(2,1)S(1)}, u32[]{:S(2)}, u32[]{:S(2)}) %all-to-all-start) | async-done | bytes 589856 | tf_op jit(solution)/shard_map/all_to_all | solution.py:558
  28.8 0.0 copy-done.1
  28.8 0.0 copy-done
  28.8 1.7 %scatter_add.1 = (bf16[32,16,256]{2,1,0:T(8,128)(2,1)S(1)}, bf16[16,768]{1,0:T(8,128)(2,1)S(1)}, bf16[96,256]{1,0:T(8,128)(2,1)S(1)}, bf16[96,256]{1,0:T(8,128)(2,1)S(1)}) custom-call(s32[3]{0:T(128)S(1)} %add_convert_fusion.flag_ref, s32[4,32]{1,0:T(4,128)S(1)} %bitcast.13, s32[1,32]{1,0:T(1,128)S(1)} %copy-done.1, ...), custom_call_target="tpu_custom_call" | custom-call | flops 262144 | bytes 705164 | tf_op jit(solution)/shard_map/scatter_add/pallas_call | solution.py:40
  30.5 1.3 %collective-permute-start.4 = (bf16[96,256]{1,0:T(8,128)(2,1)S(1)}, bf16[96,256]{1,0:T(8,128)(2,1)S(1)}, u32[]{:S(2)}, u32[]{:S(2)}) collective-permute-start(bf16[96,256]{1,0:T(8,128)(2,1)S(1)} %get-tuple-element.32), channel_id=1, source_target_pairs={{0,8},{8,0},{16,24},{24,16},{1,9},{9,1},{17,25},{25,17},{2,10},{10... | collective-permute-start | bytes 147464 | tf_op jit(solution)/shard_map/ppermute | solution.py:505
  31.7 0.7 %collective-permute-start.5 = (bf16[96,256]{1,0:T(8,128)(2,1)S(1)}, bf16[96,256]{1,0:T(8,128)(2,1)S(1)}, u32[]{:S(2)}, u32[]{:S(2)}) collective-permute-start(bf16[96,256]{1,0:T(8,128)(2,1)S(1)} %get-tuple-element.33), channel_id=1, source_target_pairs={{0,0},{8,16},{16,8},{24,24},{1,1},{9,17},{17,9},{25,25},{2,2},{10,... | collective-permute-start | bytes 147464 | tf_op jit(solution)/shard_map/ppermute | solution.py:505
  32.4 2.9 %first_step.1 = (f32[30,128,256]{2,1,0:T(8,128)S(1)}, bf16[30,32,256]{2,1,0:T(8,128)(2,1)S(1)}, f32[30,32,256]{2,1,0:T(8,128)S(1)}) custom-call(f32[30,128,256]{2,1,0:T(8,128)} %get-tuple-element.36.gates_hbm, bf16[32,64,256]{2,1,0:T(8,128)(2,1)S(1)} %get-tuple-element.21.rows_ref, bf16[32,16,256]{2,1,0:T(8,128)(2,1)S(1)} %get-tuple-element.28.forcing_ref, ...), custom_call_target="tpu_custom_call" | custom-call | flops 301989888 | bytes 5435392 | tf_op jit(solution)/shard_map/first_step/pallas_call | solution.py:40
  35.3 0.0 collective-permute-done.2.outer_ref
  35.3 0.0 collective-permute-done.3.inner_ref
  35.3 0.0 collective-permute-done.4.f_outer_ref
  35.3 0.0 collective-permute-done.5.f_inner_ref
  35.3 6.1 %later_steps.1 = (bf16[32,32,256]{2,1,0:T(8,128)(2,1)}, bf16[32,32,256]{2,1,0:T(8,128)(2,1)}) custom-call(s32[3]{0:T(128)S(1)} %add_convert_fusion.flag_ref, bf16[32,64,256]{2,1,0:T(8,128)(2,1)S(1)} %get-tuple-element.21.rows_ref, bf16[64,768]{1,0:T(8,128)(2,1)S(1)} %get-tuple-element.23.state_strip_ref.strip_ref, ...), custom_call_target="tpu_custom_call" | custom-call | flops 1207959552 | bytes 7344140 | tf_op jit(solution)/shard_map/later_steps/pallas_call | solution.py:40
  (2 shorter events, 0.0 us)
Async XLA Ops:
  0.6 28.2 %copy-start.1 = (s32[1,32]{1,0:T(1,128)S(1)}, s32[1,32]{1,0:T(1,128)}, u32[]{:S(2)}) copy-start(s32[1,32]{1,0:T(1,128)} %count_ref.1) | copy-start | bytes 388
  0.6 28.2 %copy-start = (s32[1,32,4]{1,2,0:T(4,128)S(1)}, s32[1,32,4]{1,2,0:T(4,128)}, u32[]{:S(2)}) copy-start(s32[1,32,4]{1,2,0:T(4,128)} %param.13) | copy-start | bytes 1540
  0.7 20.2 %copy-start.2 = (f32[128]{0:T(128)S(1)}, f32[128]{0:T(128)}, u32[]{:S(2)}) copy-start(f32[128]{0:T(128)} %param.17) | copy-start | bytes 1540
  4.6 24.2 %all-to-all-start = ((bf16[32,72,128]{2,1,0:T(8,128)(2,1)}), bf16[32,72,128]{2,1,0:T(8,128)(2,1)S(1)}, u32[]{:S(2)}, u32[]{:S(2)}) async-start(bf16[32,72,128]{2,1,0:T(8,128)(2,1)} %gather_band.1), calls=%async_computation | async-start | bytes 1179648 | tf_op jit(solution)/shard_map/all_to_all | solution.py:558
  14.1 6.8 %collective-permute-start.1 = (bf16[96,384]{1,0:T(8,128)(2,1)S(1)}, bf16[96,384]{1,0:T(8,128)(2,1)S(1)}, u32[]{:S(2)}, u32[]{:S(2)}) collective-permute-start(bf16[96,384]{1,0:T(8,128)(2,1)S(1)} %get-tuple-element.22.edge_ref), channel_id=1, source_target_pairs={{1,0},{2,1},{3,2},{4,3},{5,4},{6,5},{7,6},{0,7},{9,8},{10,9},{11,1... | collective-permute-start | bytes 221192 | tf_op jit(solution)/shard_map/ppermute | solution.py:494
  16.6 5.8 %collective-permute-start = (bf16[96,384]{1,0:T(8,128)(2,1)S(1)}, bf16[96,384]{1,0:T(8,128)(2,1)S(1)}, u32[]{:S(2)}, u32[]{:S(2)}) collective-permute-start(bf16[96,384]{1,0:T(8,128)(2,1)S(1)} %get-tuple-element.22.edge_ref), channel_id=1, source_target_pairs={{0,1},{1,2},{2,3},{3,4},{4,5},{5,6},{6,7},{7,0},{8,9},{9,10},{10,1... | collective-permute-start | bytes 221192 | tf_op jit(solution)/shard_map/ppermute | solution.py:493
  16.6 18.7 %collective-permute-start.2 = (bf16[5,32,256]{2,1,0:T(8,128)(2,1)S(1)}, bf16[5,32,256]{2,1,0:T(8,128)(2,1)S(1)}, u32[]{:S(2)}, u32[]{:S(2)}) collective-permute-start(bf16[5,32,256]{2,1,0:T(8,128)(2,1)S(1)} %get-tuple-element.30), channel_id=1, source_target_pairs={{0,8},{8,0},{16,24},{24,16},{1,9},{9,1},{17,25},{25,17},{2,10},{10... | collective-permute-start | bytes 245768 | tf_op jit(solution)/shard_map/ppermute | solution.py:505
  18.1 17.2 %collective-permute-start.3 = (bf16[5,32,256]{2,1,0:T(8,128)(2,1)S(1)}, bf16[5,32,256]{2,1,0:T(8,128)(2,1)S(1)}, u32[]{:S(2)}, u32[]{:S(2)}) collective-permute-start(bf16[5,32,256]{2,1,0:T(8,128)(2,1)S(1)} %get-tuple-element.31), channel_id=1, source_target_pairs={{0,0},{8,16},{16,8},{24,24},{1,1},{9,17},{17,9},{25,25},{2,2},{10,... | collective-permute-start | bytes 245768 | tf_op jit(solution)/shard_map/ppermute | solution.py:505
  30.5 4.8 %collective-permute-start.4 = (bf16[96,256]{1,0:T(8,128)(2,1)S(1)}, bf16[96,256]{1,0:T(8,128)(2,1)S(1)}, u32[]{:S(2)}, u32[]{:S(2)}) collective-permute-start(bf16[96,256]{1,0:T(8,128)(2,1)S(1)} %get-tuple-element.32), channel_id=1, source_target_pairs={{0,8},{8,0},{16,24},{24,16},{1,9},{9,1},{17,25},{25,17},{2,10},{10... | collective-permute-start | bytes 147464 | tf_op jit(solution)/shard_map/ppermute | solution.py:505
  31.7 3.6 %collective-permute-start.5 = (bf16[96,256]{1,0:T(8,128)(2,1)S(1)}, bf16[96,256]{1,0:T(8,128)(2,1)S(1)}, u32[]{:S(2)}, u32[]{:S(2)}) collective-permute-start(bf16[96,256]{1,0:T(8,128)(2,1)S(1)} %get-tuple-element.33), channel_id=1, source_target_pairs={{0,0},{8,16},{16,8},{24,24},{1,1},{9,17},{17,9},{25,25},{2,2},{10,... | collective-permute-start | bytes 147464 | tf_op jit(solution)/shard_map/ppermute | solution.py:505

commit v8 on v7

--- a/solution.py
+++ b/solution.py
@@ -208,14 +208,14 @@
 
 def patches_of(strip, tiles, first, last):
     channels = strip.shape[0]
-    near = lane_of((channels, LANES)) % 8 < 4
+    beside_left = lane_of((channels, LANES)) % 8 == 3
     found = {}
     for i, t in enumerate(tiles):
         left = strip[:, i * LANES : (i + 1) * LANES]
         right = strip[:, (len(tiles) + i) * LANES : (len(tiles) + i + 1) * LANES]
-        mixed = jnp.where(near, left, right)
+        mixed = jnp.where(beside_left, left, pltpu.roll(right, LANES - 2, axis=1))
         for r in range(max(first, 16 * t), min(last, 16 * t + 16)):
-            found[r] = pltpu.roll(mixed, -(8 * (r % 16) + 4) % LANES, axis=1)
+            found[r] = pltpu.roll(mixed, -(8 * (r % 16) + 3) % LANES, axis=1)
     return found
 
 
@@ -228,11 +228,14 @@
     channels = row.shape[0]
     lane = lane_of((channels, LANES))
     head, tail = row[:, :LANES], row[:, LANES:]
-    ref[r, :channels, :LANES] = pltpu.roll(jnp.where(lane == LANES - 1, patch, head), 1, axis=1)
-    ref[r, :channels, LANES:] = pltpu.roll(jnp.where(lane == LANES - 1, head, tail), 1, axis=1)
+    first, last = lane == 0, lane == LANES - 1
+    head_up, tail_up = pltpu.roll(head, 1, axis=1), pltpu.roll(tail, 1, axis=1)
+    ref[r, :channels, :LANES] = jnp.where(first, patch, head_up)
+    ref[r, :channels, LANES:] = jnp.where(first, head_up, tail_up)
     ref[r, channels : 2 * channels, :] = row
-    ref[r, 2 * channels :, :LANES] = pltpu.roll(jnp.where(lane == 0, tail, head), LANES - 1, axis=1)
-    ref[r, 2 * channels :, LANES:] = pltpu.roll(jnp.where(lane == 0, patch, tail), LANES - 1, axis=1)
+    head_down, tail_down = pltpu.roll(head, LANES - 1, axis=1), pltpu.roll(tail, LANES - 1, axis=1)
+    ref[r, 2 * channels :, :LANES] = jnp.where(last, tail_down, head_down)
+    ref[r, 2 * channels :, LANES:] = jnp.where(last, patch, tail_down)
 
 
 def row_taps(ref, r):
@@ -614,7 +617,7 @@
             ends,
         ],
         3, 3,
-        [pltpu.VMEM((2 * row_count + 1, channels, block), F32)] * 2,
+        [pltpu.VMEM((2 * row_count + 1, channels, block), F32)] * 4,
         "scatter_add", slots * channels * block,
         (flags, slot_target[0].T, tile_counts, incoming, marks, strip),
     )

time: 42 us -> 41 us (0.976)
  Pallas kernels: 19.5 us -> 18.3 us
    pallas_call x4, Pallas kernels: 13.5 us -> 12.2 us  [call(): pl.pallas_call(kernel, out_shape=tuple(outs), in_specs=in_specs or scalar...]
  transfers between devices with their start and end apart: 7 -> 7, of which waited for: 2 -> 2; matrix products, arithmetic and copies ran while one was open for 5% -> 6% of each run, Pallas kernels for 23% -> 23%
where the time goes in v8:
time: 41 us; the launch traced here: 40.5 us
  Pallas kernels  18.3 us (45%)
  starting transfers between devices  13.8 us (34%)
  waiting for transfers between devices  5.36 us (13%)
  local copies, waits for them, and re-layouts  2 us (5%)
  between operations  0.81 us (2%)
    pallas_call x4, Pallas kernels, call(): pl.pallas_call(kernel, out_shape=tuple(outs), in_specs=in_specs or scalar...  12.2 us
    all_to_all x1, starting transfers between devices, on_device(): lax.all_to_all(outgoing, ('lat', 'lon'), split_axis=0, concat_axis=0, til...  7.3 us
    ppermute x4, starting transfers between devices, swap(): return lax.ppermute(x, 'lat', list(enumerate(partner)))  3.98 us
    pallas_call x1, Pallas kernels, on_device(): pl.pallas_call(functools.partial(gather_kernel, ring), out_shape=pltpu.HB...  3.93 us
    all_to_all x1, waiting for transfers between devices, on_device(): lax.all_to_all(outgoing, ('lat', 'lon'), split_axis=0, concat_axis=0, til...  3.9 us
    ppermute x1, starting transfers between devices, exchange_columns(): from_right = lax.ppermute(edge, 'lon', back(count))  2.47 us
    pallas_call x1, Pallas kernels, on_device(): pl.pallas_call(prepare_kernel, out_shape=(jax.ShapeDtypeStruct((row_count...  2.12 us
    unnamed x8, local copies, waits for them, and re-layouts  1.88 us
  transfers between devices with their start and end apart: 7, of which 2 were waited for; matrix products, arithmetic and copies ran while one was open for 6% of the time, Pallas kernels for 23%

profile of v8, /device:TPU:0, one launch (start us, length us, event | category | flops | bytes accessed | tf_op | source)
XLA Modules:
  0.0 40.5 jit_solution(15407037100090611913)
XLA Ops:
  0.6 0.0 copy-start.1
  0.6 0.0 copy-start
  0.7 0.0 copy-start.2
  0.7 3.9 %gather_band.1 = bf16[32,72,128]{2,1,0:T(8,128)(2,1)} custom-call(s32[4,32]{1,0:T(4,128)} %bitcast.15, bf16[128,16,128]{2,1,0:T(8,128)(2,1)} %blocks_hbm.1, bf16[128,8,128]{2,1,0:T(8,128)(2,1)} %bitcast.14), custom_call_target="tpu_custom_call" | custom-call | tf_op jit(solution)/shard_map/gather_band/pallas_call | solution.py:543
  4.6 7.3 %all-to-all-start = ((bf16[32,72,128]{2,1,0:T(8,128)(2,1)}), bf16[32,72,128]{2,1,0:T(8,128)(2,1)S(1)}, u32[]{:S(2)}, u32[]{:S(2)}) async-start(bf16[32,72,128]{2,1,0:T(8,128)(2,1)} %gather_band.1), calls=%async_computation | async-start | bytes 1179648 | tf_op jit(solution)/shard_map/all_to_all | solution.py:561
  11.9 0.1 add_convert_fusion.flag_ref
  12.0 2.1 %prepare.1 = (bf16[32,64,256]{2,1,0:T(8,128)(2,1)S(1)}, bf16[96,384]{1,0:T(8,128)(2,1)S(1)}, bf16[5,32,256]{2,1,0:T(8,128)(2,1)S(1)}, bf16[5,32,256]{2,1,0:T(8,128)(2,1)S(1)}) custom-call(s32[3]{0:T(128)S(1)} %add_convert_fusion.flag_ref, bf16[32,32,256]{2,1,0:T(8,128)(2,1)} %hidden_hbm.1, bf16[32,32,256]{2,1,0:T(8,128)(2,1)} %cell_hbm.1, s32[4,32]{1,0:T(4,128)} %bitcast.12, ...), custom_call_target="tpu_custom_call" | custom-call | tf_op jit(solution)/shard_map/prepare/pallas_call | solution.py:564
  14.1 2.5 %collective-permute-start.1 = (bf16[96,384]{1,0:T(8,128)(2,1)S(1)}, bf16[96,384]{1,0:T(8,128)(2,1)S(1)}, u32[]{:S(2)}, u32[]{:S(2)}) collective-permute-start(bf16[96,384]{1,0:T(8,128)(2,1)S(1)} %get-tuple-element.22.edge_ref), channel_id=1, source_target_pairs={{1,0},{2,1},{3,2},{4,3},{5,4},{6,5},{7,6},{0,7},{9,8},{10,9},{11,1... | collective-permute-start | bytes 221192 | tf_op jit(solution)/shard_map/ppermute | solution.py:497
  16.6 0.0 collective-permute-start
  16.6 1.5 %collective-permute-start.2 = (bf16[5,32,256]{2,1,0:T(8,128)(2,1)S(1)}, bf16[5,32,256]{2,1,0:T(8,128)(2,1)S(1)}, u32[]{:S(2)}, u32[]{:S(2)}) collective-permute-start(bf16[5,32,256]{2,1,0:T(8,128)(2,1)S(1)} %get-tuple-element.30), channel_id=1, source_target_pairs={{0,8},{8,0},{16,24},{24,16},{1,9},{9,1},{17,25},{25,17},{2,10},{10... | collective-permute-start | bytes 245768 | tf_op jit(solution)/shard_map/ppermute | solution.py:508
  18.1 0.7 %collective-permute-start.3 = (bf16[5,32,256]{2,1,0:T(8,128)(2,1)S(1)}, bf16[5,32,256]{2,1,0:T(8,128)(2,1)S(1)}, u32[]{:S(2)}, u32[]{:S(2)}) collective-permute-start(bf16[5,32,256]{2,1,0:T(8,128)(2,1)S(1)} %get-tuple-element.31), channel_id=1, source_target_pairs={{0,0},{8,16},{16,8},{24,24},{1,1},{9,17},{17,9},{25,25},{2,2},{10,... | collective-permute-start | bytes 245768 | tf_op jit(solution)/shard_map/ppermute | solution.py:508
  18.7 0.9 %copy.14 = bf16[128,144]{1,0:T(8,128)(2,1)S(1)} copy(bf16[128,144]{0,1:T(8,128)(2,1)} %param.15) | data formatting | bytes 73728 | tf_op args[5]
  19.6 1.0 %copy.12 = bf16[128,288]{1,0:T(8,128)(2,1)S(1)} copy(bf16[128,288]{0,1:T(8,128)(2,1)} %param.16) | data formatting | bytes 147456 | tf_op args[6]
  20.6 0.1 broadcast_multiply_fusion.1.in_weight_ref
  20.7 0.1 broadcast_multiply_fusion.weight_ref
  20.8 0.0 copy-done.2
  20.8 0.1 copy.13.bias_ref
  20.9 0.0 collective-permute-done.1.right_ref
  21.0 1.4 %collective-permute-done.left_ref = bf16[96,384]{1,0:T(8,128)(2,1)S(1)} collective-permute-done((bf16[96,384]{1,0:T(8,128)(2,1)S(1)}, bf16[96,384]{1,0:T(8,128)(2,1)S(1)}, u32[]{:S(2)}, u32[]{:S(2)}) %collective-permute-start) | collective-permute-done | bytes 73760 | tf_op jit(solution)/shard_map/ppermute | solution.py:496
  22.4 2.5 %state_gates.1 = (f32[30,128,256]{2,1,0:T(8,128)}, f32[128,256]{1,0:T(8,128)S(1)}, bf16[64,768]{1,0:T(8,128)(2,1)S(1)}, f32[32,128]{1,0:T(8,128)S(1)}) custom-call(bf16[32,64,256]{2,1,0:T(8,128)(2,1)S(1)} %get-tuple-element.21.rows_ref, bf16[96,384]{1,0:T(8,128)(2,1)S(1)} %get-tuple-element.22.edge_ref, bf16[96,384]{1,0:T(8,128)(2,1)S(1)} %collective-permute-done.left_ref, ...), custom_call_target="tpu_custom_call" | custom-call | flops 603979776 | bytes 1344000 | tf_op jit(solution)/shard_map/state_gates/pallas_call | solution.py:40
  24.9 3.9 %all-to-all-done.incoming_ref = bf16[32,72,128]{2,1,0:T(8,128)(2,1)S(1)} async-done(((bf16[32,72,128]{2,1,0:T(8,128)(2,1)}), bf16[32,72,128]{2,1,0:T(8,128)(2,1)S(1)}, u32[]{:S(2)}, u32[]{:S(2)}) %all-to-all-start) | async-done | bytes 589856 | tf_op jit(solution)/shard_map/all_to_all | solution.py:561
  28.8 0.0 copy-done.1
  28.8 0.0 copy-done
  28.8 1.6 %scatter_add.1 = (bf16[32,16,256]{2,1,0:T(8,128)(2,1)S(1)}, bf16[16,768]{1,0:T(8,128)(2,1)S(1)}, bf16[96,256]{1,0:T(8,128)(2,1)S(1)}, bf16[96,256]{1,0:T(8,128)(2,1)S(1)}) custom-call(s32[3]{0:T(128)S(1)} %add_convert_fusion.flag_ref, s32[4,32]{1,0:T(4,128)S(1)} %bitcast.13, s32[1,32]{1,0:T(1,128)S(1)} %copy-done.1, ...), custom_call_target="tpu_custom_call" | custom-call | flops 262144 | bytes 705164 | tf_op jit(solution)/shard_map/scatter_add/pallas_call | solution.py:40
  30.4 1.2 %collective-permute-start.4 = (bf16[96,256]{1,0:T(8,128)(2,1)S(1)}, bf16[96,256]{1,0:T(8,128)(2,1)S(1)}, u32[]{:S(2)}, u32[]{:S(2)}) collective-permute-start(bf16[96,256]{1,0:T(8,128)(2,1)S(1)} %get-tuple-element.32), channel_id=1, source_target_pairs={{0,8},{8,0},{16,24},{24,16},{1,9},{9,1},{17,25},{25,17},{2,10},{10... | collective-permute-start | bytes 147464 | tf_op jit(solution)/shard_map/ppermute | solution.py:508
  31.6 0.7 %collective-permute-start.5 = (bf16[96,256]{1,0:T(8,128)(2,1)S(1)}, bf16[96,256]{1,0:T(8,128)(2,1)S(1)}, u32[]{:S(2)}, u32[]{:S(2)}) collective-permute-start(bf16[96,256]{1,0:T(8,128)(2,1)S(1)} %get-tuple-element.33), channel_id=1, source_target_pairs={{0,0},{8,16},{16,8},{24,24},{1,1},{9,17},{17,9},{25,25},{2,2},{10,... | collective-permute-start | bytes 147464 | tf_op jit(solution)/shard_map/ppermute | solution.py:508
  32.3 2.9 %first_step.1 = (f32[30,128,256]{2,1,0:T(8,128)S(1)}, bf16[30,32,256]{2,1,0:T(8,128)(2,1)S(1)}, f32[30,32,256]{2,1,0:T(8,128)S(1)}) custom-call(f32[30,128,256]{2,1,0:T(8,128)} %get-tuple-element.36.gates_hbm, bf16[32,64,256]{2,1,0:T(8,128)(2,1)S(1)} %get-tuple-element.21.rows_ref, bf16[32,16,256]{2,1,0:T(8,128)(2,1)S(1)} %get-tuple-element.28.forcing_ref, ...), custom_call_target="tpu_custom_call" | custom-call | flops 301989888 | bytes 5435392 | tf_op jit(solution)/shard_map/first_step/pallas_call | solution.py:40
  35.3 0.0 collective-permute-done.2.outer_ref
  35.3 0.0 collective-permute-done.3.inner_ref
  35.3 0.0 collective-permute-done.4.f_outer_ref
  35.3 0.0 collective-permute-done.5.f_inner_ref
  35.3 5.2 %later_steps.1 = (bf16[32,32,256]{2,1,0:T(8,128)(2,1)}, bf16[32,32,256]{2,1,0:T(8,128)(2,1)}) custom-call(s32[3]{0:T(128)S(1)} %add_convert_fusion.flag_ref, bf16[32,64,256]{2,1,0:T(8,128)(2,1)S(1)} %get-tuple-element.21.rows_ref, bf16[64,768]{1,0:T(8,128)(2,1)S(1)} %get-tuple-element.23.state_strip_ref.strip_ref, ...), custom_call_target="tpu_custom_call" | custom-call | flops 1207959552 | bytes 7344140 | tf_op jit(solution)/shard_map/later_steps/pallas_call | solution.py:40
  (2 shorter events, 0.0 us)
Async XLA Ops:
  0.6 28.2 %copy-start.1 = (s32[1,32]{1,0:T(1,128)S(1)}, s32[1,32]{1,0:T(1,128)}, u32[]{:S(2)}) copy-start(s32[1,32]{1,0:T(1,128)} %count_ref.1) | copy-start | bytes 388
  0.6 28.2 %copy-start = (s32[1,32,4]{1,2,0:T(4,128)S(1)}, s32[1,32,4]{1,2,0:T(4,128)}, u32[]{:S(2)}) copy-start(s32[1,32,4]{1,2,0:T(4,128)} %param.13) | copy-start | bytes 1540
  0.7 20.2 %copy-start.2 = (f32[128]{0:T(128)S(1)}, f32[128]{0:T(128)}, u32[]{:S(2)}) copy-start(f32[128]{0:T(128)} %param.17) | copy-start | bytes 1540
  4.6 24.2 %all-to-all-start = ((bf16[32,72,128]{2,1,0:T(8,128)(2,1)}), bf16[32,72,128]{2,1,0:T(8,128)(2,1)S(1)}, u32[]{:S(2)}, u32[]{:S(2)}) async-start(bf16[32,72,128]{2,1,0:T(8,128)(2,1)} %gather_band.1), calls=%async_computation | async-start | bytes 1179648 | tf_op jit(solution)/shard_map/all_to_all | solution.py:561
  14.1 6.8 %collective-permute-start.1 = (bf16[96,384]{1,0:T(8,128)(2,1)S(1)}, bf16[96,384]{1,0:T(8,128)(2,1)S(1)}, u32[]{:S(2)}, u32[]{:S(2)}) collective-permute-start(bf16[96,384]{1,0:T(8,128)(2,1)S(1)} %get-tuple-element.22.edge_ref), channel_id=1, source_target_pairs={{1,0},{2,1},{3,2},{4,3},{5,4},{6,5},{7,6},{0,7},{9,8},{10,9},{11,1... | collective-permute-start | bytes 221192 | tf_op jit(solution)/shard_map/ppermute | solution.py:497
  16.6 5.8 %collective-permute-start = (bf16[96,384]{1,0:T(8,128)(2,1)S(1)}, bf16[96,384]{1,0:T(8,128)(2,1)S(1)}, u32[]{:S(2)}, u32[]{:S(2)}) collective-permute-start(bf16[96,384]{1,0:T(8,128)(2,1)S(1)} %get-tuple-element.22.edge_ref), channel_id=1, source_target_pairs={{0,1},{1,2},{2,3},{3,4},{4,5},{5,6},{6,7},{7,0},{8,9},{9,10},{10,1... | collective-permute-start | bytes 221192 | tf_op jit(solution)/shard_map/ppermute | solution.py:496
  16.6 18.7 %collective-permute-start.2 = (bf16[5,32,256]{2,1,0:T(8,128)(2,1)S(1)}, bf16[5,32,256]{2,1,0:T(8,128)(2,1)S(1)}, u32[]{:S(2)}, u32[]{:S(2)}) collective-permute-start(bf16[5,32,256]{2,1,0:T(8,128)(2,1)S(1)} %get-tuple-element.30), channel_id=1, source_target_pairs={{0,8},{8,0},{16,24},{24,16},{1,9},{9,1},{17,25},{25,17},{2,10},{10... | collective-permute-start | bytes 245768 | tf_op jit(solution)/shard_map/ppermute | solution.py:508
  18.1 17.2 %collective-permute-start.3 = (bf16[5,32,256]{2,1,0:T(8,128)(2,1)S(1)}, bf16[5,32,256]{2,1,0:T(8,128)(2,1)S(1)}, u32[]{:S(2)}, u32[]{:S(2)}) collective-permute-start(bf16[5,32,256]{2,1,0:T(8,128)(2,1)S(1)} %get-tuple-element.31), channel_id=1, source_target_pairs={{0,0},{8,16},{16,8},{24,24},{1,1},{9,17},{17,9},{25,25},{2,2},{10,... | collective-permute-start | bytes 245768 | tf_op jit(solution)/shard_map/ppermute | solution.py:508
  30.4 4.8 %collective-permute-start.4 = (bf16[96,256]{1,0:T(8,128)(2,1)S(1)}, bf16[96,256]{1,0:T(8,128)(2,1)S(1)}, u32[]{:S(2)}, u32[]{:S(2)}) collective-permute-start(bf16[96,256]{1,0:T(8,128)(2,1)S(1)} %get-tuple-element.32), channel_id=1, source_target_pairs={{0,8},{8,0},{16,24},{24,16},{1,9},{9,1},{17,25},{25,17},{2,10},{10... | collective-permute-start | bytes 147464 | tf_op jit(solution)/shard_map/ppermute | solution.py:508
  31.6 3.6 %collective-permute-start.5 = (bf16[96,256]{1,0:T(8,128)(2,1)S(1)}, bf16[96,256]{1,0:T(8,128)(2,1)S(1)}, u32[]{:S(2)}, u32[]{:S(2)}) collective-permute-start(bf16[96,256]{1,0:T(8,128)(2,1)S(1)} %get-tuple-element.33), channel_id=1, source_target_pairs={{0,0},{8,16},{16,8},{24,24},{1,1},{9,17},{17,9},{25,25},{2,2},{10,... | collective-permute-start | bytes 147464 | tf_op jit(solution)/shard_map/ppermute | solution.py:508

commit v9 on v8

--- a/solution.py
+++ b/solution.py
@@ -113,6 +113,7 @@
             folded.append(wide[: channels // 2] + pltpu.roll(wide[channels // 2 :], 8 * cap, axis=1))
         for j in range(ring):
             both = jnp.where(near, folded[j - 1], folded[(j + 1) % ring])
+            both = jnp.concatenate([both, jnp.zeros_like(both)], axis=0)
             out[g * ring + j, cap * channels :, :] = both.astype(BF)
         send = pltpu.make_async_copy(
             out.at[pl.ds(g * ring, ring)], out_hbm.at[pl.ds(g * ring, ring)], out_sem.at[g]
@@ -424,14 +425,14 @@
 
 def beside(incoming_ref, mark_ref, row_count, channels):
     sources = incoming_ref.shape[0]
-    base = incoming_ref.shape[1] - channels // 2
+    base = incoming_ref.shape[1] - channels
     lane = lane_of((channels // 2, LANES))
     group_lanes = 8 * ((base // channels) % 16)
     tiles = [[jnp.zeros((channels // 2, LANES), F32) for _ in range(2)] for _ in range(STRIP // LANES)]
     for start in range(0, row_count, 16):
         sums = [jnp.zeros((channels // 2, LANES), F32) for _ in range(16)]
         for p in range(sources):
-            edges = incoming_ref[p, base:, :].astype(F32)
+            edges = incoming_ref[p, base:, :].astype(F32)[: channels // 2]
             mark = jnp.broadcast_to(mark_ref[p : p + 1, :], edges.shape)
             for i in range(16):
                 sums[i] = sums[i] + jnp.where(mark == float(start + i), edges, 0.0)
@@ -537,7 +538,7 @@
     flags = jnp.stack([lat > 0, lat < lax.axis_size("lat") - 1, lat % 2 == 1]).astype(jnp.int32)
 
     ring = lax.axis_size("lon")
-    height = cap * channels + channels // 2
+    height = (cap + 1) * channels
     message = jax.ShapeDtypeStruct((tiles, height, block), BF)
     groups = tiles // ring
     outgoing = pl.pallas_call(

time: 41 us -> 42.4 us (1.034)
  waiting for transfers between devices: 5.36 us -> 7.63 us
  local copies, waits for them, and re-layouts: 2 us -> 1.12 us
    ppermute x1, waiting for transfers between devices: 1.45 us -> 2.74 us  [exchange_columns(): from_left = lax.ppermute(edge, 'lon', around(count))]
    all_to_all x1, waiting for transfers between devices: 3.9 us -> 4.87 us  [on_device(): lax.all_to_all(outgoing, ('lat', 'lon'), split_axis=0, concat_axis=0, til...]
    unnamed x8 -> x10, local copies, waits for them, and re-layouts: 1.88 us -> 1.01 us
  transfers between devices with their start and end apart: 7 -> 7, of which waited for: 2 -> 2; matrix products, arithmetic and copies ran while one was open for 6% -> 3% of each run, Pallas kernels for 23% -> 22%
where the time goes in v9:
time: 42.4 us; the launch traced here: 41.8 us
  Pallas kernels  18.3 us (43%)
  starting transfers between devices  13.7 us (32%)
  waiting for transfers between devices  7.63 us (18%)
  local copies, waits for them, and re-layouts  1.12 us (3%)
  between operations  0.83 us (2%)
    pallas_call x4, Pallas kernels, call(): pl.pallas_call(kernel, out_shape=tuple(outs), in_specs=in_specs or scalar...  12.2 us
    all_to_all x1, starting transfers between devices, on_device(): lax.all_to_all(outgoing, ('lat', 'lon'), split_axis=0, concat_axis=0, til...  7.3 us
    all_to_all x1, waiting for transfers between devices, on_device(): lax.all_to_all(outgoing, ('lat', 'lon'), split_axis=0, concat_axis=0, til...  4.87 us
    pallas_call x1, Pallas kernels, on_device(): pl.pallas_call(functools.partial(gather_kernel, ring), out_shape=pltpu.HB...  3.93 us
    ppermute x4, starting transfers between devices, swap(): return lax.ppermute(x, 'lat', list(enumerate(partner)))  3.88 us
    ppermute x1, waiting for transfers between devices, exchange_columns(): from_left = lax.ppermute(edge, 'lon', around(count))  2.74 us
    ppermute x1, starting transfers between devices, exchange_columns(): from_right = lax.ppermute(edge, 'lon', back(count))  2.47 us
    pallas_call x1, Pallas kernels, on_device(): pl.pallas_call(prepare_kernel, out_shape=(jax.ShapeDtypeStruct((row_count...  2.12 us
  transfers between devices with their start and end apart: 7, of which 2 were waited for; matrix products, arithmetic and copies ran while one was open for 3% of the time, Pallas kernels for 22%

profile of v9, /device:TPU:0, one launch (start us, length us, event | category | flops | bytes accessed | tf_op | source)
XLA Modules:
  0.0 41.8 jit_solution(7874213849175364489)
XLA Ops:
  0.6 0.0 copy-start.1
  0.6 0.0 copy-start
  0.7 0.0 copy-start.2
  0.7 0.0 copy-start.3
  0.7 3.9 %gather_band.1 = bf16[32,80,128]{2,1,0:T(8,128)(2,1)} custom-call(s32[4,32]{1,0:T(4,128)} %bitcast.15, bf16[128,16,128]{2,1,0:T(8,128)(2,1)} %blocks_hbm.1, bf16[128,8,128]{2,1,0:T(8,128)(2,1)} %bitcast.14), custom_call_target="tpu_custom_call" | custom-call | tf_op jit(solution)/shard_map/gather_band/pallas_call | solution.py:544
  4.6 7.3 %all-to-all-start = ((bf16[32,80,128]{2,1,0:T(8,128)(2,1)}), bf16[32,80,128]{2,1,0:T(8,128)(2,1)S(1)}, u32[]{:S(2)}, u32[]{:S(2)}) async-start(bf16[32,80,128]{2,1,0:T(8,128)(2,1)} %gather_band.1), calls=%async_computation | async-start | bytes 1310720 | tf_op jit(solution)/shard_map/all_to_all | solution.py:562
  11.9 0.1 add_convert_fusion.flag_ref
  12.0 2.1 %prepare.1 = (bf16[32,64,256]{2,1,0:T(8,128)(2,1)S(1)}, bf16[96,384]{1,0:T(8,128)(2,1)S(1)}, bf16[5,32,256]{2,1,0:T(8,128)(2,1)S(1)}, bf16[5,32,256]{2,1,0:T(8,128)(2,1)S(1)}) custom-call(s32[3]{0:T(128)S(1)} %add_convert_fusion.flag_ref, bf16[32,32,256]{2,1,0:T(8,128)(2,1)} %hidden_hbm.1, bf16[32,32,256]{2,1,0:T(8,128)(2,1)} %cell_hbm.1, s32[4,32]{1,0:T(4,128)} %bitcast.12, ...), custom_call_target="tpu_custom_call" | custom-call | tf_op jit(solution)/shard_map/prepare/pallas_call | solution.py:565
  14.1 2.5 %collective-permute-start.1 = (bf16[96,384]{1,0:T(8,128)(2,1)S(1)}, bf16[96,384]{1,0:T(8,128)(2,1)S(1)}, u32[]{:S(2)}, u32[]{:S(2)}) collective-permute-start(bf16[96,384]{1,0:T(8,128)(2,1)S(1)} %get-tuple-element.22.edge_ref), channel_id=1, source_target_pairs={{1,0},{2,1},{3,2},{4,3},{5,4},{6,5},{7,6},{0,7},{9,8},{10,9},{11,1... | collective-permute-start | bytes 221192 | tf_op jit(solution)/shard_map/ppermute | solution.py:498
  16.6 0.0 collective-permute-start
  16.6 1.5 %collective-permute-start.2 = (bf16[5,32,256]{2,1,0:T(8,128)(2,1)S(1)}, bf16[5,32,256]{2,1,0:T(8,128)(2,1)S(1)}, u32[]{:S(2)}, u32[]{:S(2)}) collective-permute-start(bf16[5,32,256]{2,1,0:T(8,128)(2,1)S(1)} %get-tuple-element.30), channel_id=1, source_target_pairs={{0,8},{8,0},{16,24},{24,16},{1,9},{9,1},{17,25},{25,17},{2,10},{10... | collective-permute-start | bytes 245768 | tf_op jit(solution)/shard_map/ppermute | solution.py:509
  18.1 0.7 %collective-permute-start.3 = (bf16[5,32,256]{2,1,0:T(8,128)(2,1)S(1)}, bf16[5,32,256]{2,1,0:T(8,128)(2,1)S(1)}, u32[]{:S(2)}, u32[]{:S(2)}) collective-permute-start(bf16[5,32,256]{2,1,0:T(8,128)(2,1)S(1)} %get-tuple-element.31), channel_id=1, source_target_pairs={{0,0},{8,16},{16,8},{24,24},{1,1},{9,17},{17,9},{25,25},{2,2},{10,... | collective-permute-start | bytes 245768 | tf_op jit(solution)/shard_map/ppermute | solution.py:509
  18.7 0.9 %copy.14 = bf16[128,144]{1,0:T(8,128)(2,1)S(1)} copy(bf16[128,144]{0,1:T(8,128)(2,1)} %param.15) | data formatting | bytes 73728 | tf_op args[5]
  19.6 0.0 copy-done.2
  19.6 0.1 copy.12
  19.8 0.1 broadcast_multiply_fusion.1.in_weight_ref
  19.9 0.1 broadcast_multiply_fusion.weight_ref
  20.0 0.0 copy-done.3
  20.0 0.1 copy.13.bias_ref
  20.1 0.0 collective-permute-done.1.right_ref
  20.1 2.7 %collective-permute-done.left_ref = bf16[96,384]{1,0:T(8,128)(2,1)S(1)} collective-permute-done((bf16[96,384]{1,0:T(8,128)(2,1)S(1)}, bf16[96,384]{1,0:T(8,128)(2,1)S(1)}, u32[]{:S(2)}, u32[]{:S(2)}) %collective-permute-start) | collective-permute-done | bytes 73760 | tf_op jit(solution)/shard_map/ppermute | solution.py:497
  22.8 2.5 %state_gates.1 = (f32[30,128,256]{2,1,0:T(8,128)}, f32[128,256]{1,0:T(8,128)S(1)}, bf16[64,768]{1,0:T(8,128)(2,1)S(1)}, f32[32,128]{1,0:T(8,128)S(1)}) custom-call(bf16[32,64,256]{2,1,0:T(8,128)(2,1)S(1)} %get-tuple-element.21.rows_ref, bf16[96,384]{1,0:T(8,128)(2,1)S(1)} %get-tuple-element.22.edge_ref, bf16[96,384]{1,0:T(8,128)(2,1)S(1)} %collective-permute-done.left_ref, ...), custom_call_target="tpu_custom_call" | custom-call | flops 603979776 | bytes 1344000 | tf_op jit(solution)/shard_map/state_gates/pallas_call | solution.py:40
  25.3 4.9 %all-to-all-done.incoming_ref = bf16[32,80,128]{2,1,0:T(8,128)(2,1)S(1)} async-done(((bf16[32,80,128]{2,1,0:T(8,128)(2,1)}), bf16[32,80,128]{2,1,0:T(8,128)(2,1)S(1)}, u32[]{:S(2)}, u32[]{:S(2)}) %all-to-all-start) | async-done | bytes 655392 | tf_op jit(solution)/shard_map/all_to_all | solution.py:562
  30.2 0.0 copy-done.1
  30.2 0.0 copy-done
  30.2 1.7 %scatter_add.1 = (bf16[32,16,256]{2,1,0:T(8,128)(2,1)S(1)}, bf16[16,768]{1,0:T(8,128)(2,1)S(1)}, bf16[96,256]{1,0:T(8,128)(2,1)S(1)}, bf16[96,256]{1,0:T(8,128)(2,1)S(1)}) custom-call(s32[3]{0:T(128)S(1)} %add_convert_fusion.flag_ref, s32[4,32]{1,0:T(4,128)S(1)} %bitcast.13, s32[1,32]{1,0:T(1,128)S(1)} %copy-done.1, ...), custom_call_target="tpu_custom_call" | custom-call | flops 262144 | bytes 770700 | tf_op jit(solution)/shard_map/scatter_add/pallas_call | solution.py:40
  31.9 1.1 %collective-permute-start.4 = (bf16[96,256]{1,0:T(8,128)(2,1)S(1)}, bf16[96,256]{1,0:T(8,128)(2,1)S(1)}, u32[]{:S(2)}, u32[]{:S(2)}) collective-permute-start(bf16[96,256]{1,0:T(8,128)(2,1)S(1)} %get-tuple-element.32), channel_id=1, source_target_pairs={{0,8},{8,0},{16,24},{24,16},{1,9},{9,1},{17,25},{25,17},{2,10},{10... | collective-permute-start | bytes 147464 | tf_op jit(solution)/shard_map/ppermute | solution.py:509
  33.0 0.7 %collective-permute-start.5 = (bf16[96,256]{1,0:T(8,128)(2,1)S(1)}, bf16[96,256]{1,0:T(8,128)(2,1)S(1)}, u32[]{:S(2)}, u32[]{:S(2)}) collective-permute-start(bf16[96,256]{1,0:T(8,128)(2,1)S(1)} %get-tuple-element.33), channel_id=1, source_target_pairs={{0,0},{8,16},{16,8},{24,24},{1,1},{9,17},{17,9},{25,25},{2,2},{10,... | collective-permute-start | bytes 147464 | tf_op jit(solution)/shard_map/ppermute | solution.py:509
  33.6 2.9 %first_step.1 = (f32[30,128,256]{2,1,0:T(8,128)S(1)}, bf16[30,32,256]{2,1,0:T(8,128)(2,1)S(1)}, f32[30,32,256]{2,1,0:T(8,128)S(1)}) custom-call(f32[30,128,256]{2,1,0:T(8,128)} %get-tuple-element.36.gates_hbm, bf16[32,64,256]{2,1,0:T(8,128)(2,1)S(1)} %get-tuple-element.21.rows_ref, bf16[32,16,256]{2,1,0:T(8,128)(2,1)S(1)} %get-tuple-element.28.forcing_ref, ...), custom_call_target="tpu_custom_call" | custom-call | flops 301989888 | bytes 5435392 | tf_op jit(solution)/shard_map/first_step/pallas_call | solution.py:40
  36.6 0.0 collective-permute-done.2.outer_ref
  36.6 0.0 collective-permute-done.3.inner_ref
  36.6 0.0 collective-permute-done.4.f_outer_ref
  36.6 0.0 collective-permute-done.5.f_inner_ref
  36.6 5.2 %later_steps.1 = (bf16[32,32,256]{2,1,0:T(8,128)(2,1)}, bf16[32,32,256]{2,1,0:T(8,128)(2,1)}) custom-call(s32[3]{0:T(128)S(1)} %add_convert_fusion.flag_ref, bf16[32,64,256]{2,1,0:T(8,128)(2,1)S(1)} %get-tuple-element.21.rows_ref, bf16[64,768]{1,0:T(8,128)(2,1)S(1)} %get-tuple-element.23.state_strip_ref.strip_ref, ...), custom_call_target="tpu_custom_call" | custom-call | flops 1207959552 | bytes 7344140 | tf_op jit(solution)/shard_map/later_steps/pallas_call | solution.py:40
  (2 shorter events, 0.0 us)
Async XLA Ops:
  0.6 29.6 %copy-start.1 = (s32[1,32]{1,0:T(1,128)S(1)}, s32[1,32]{1,0:T(1,128)}, u32[]{:S(2)}) copy-start(s32[1,32]{1,0:T(1,128)} %count_ref.1) | copy-start | bytes 388
  0.6 29.6 %copy-start = (s32[1,32,4]{1,2,0:T(4,128)S(1)}, s32[1,32,4]{1,2,0:T(4,128)}, u32[]{:S(2)}) copy-start(s32[1,32,4]{1,2,0:T(4,128)} %param.13) | copy-start | bytes 1540
  0.7 19.0 %copy-start.2 = (bf16[128,288]{0,1:T(8,128)(2,1)S(1)}, bf16[128,288]{0,1:T(8,128)(2,1)}, u32[]{:S(2)}) copy-start(bf16[128,288]{0,1:T(8,128)(2,1)} %param.16) | copy-start | bytes 221188
  0.7 19.3 %copy-start.3 = (f32[128]{0:T(128)S(1)}, f32[128]{0:T(128)}, u32[]{:S(2)}) copy-start(f32[128]{0:T(128)} %param.17) | copy-start | bytes 1540
  4.6 25.6 %all-to-all-start = ((bf16[32,80,128]{2,1,0:T(8,128)(2,1)}), bf16[32,80,128]{2,1,0:T(8,128)(2,1)S(1)}, u32[]{:S(2)}, u32[]{:S(2)}) async-start(bf16[32,80,128]{2,1,0:T(8,128)(2,1)} %gather_band.1), calls=%async_computation | async-start | bytes 1310720 | tf_op jit(solution)/shard_map/all_to_all | solution.py:562
  14.1 6.0 %collective-permute-start.1 = (bf16[96,384]{1,0:T(8,128)(2,1)S(1)}, bf16[96,384]{1,0:T(8,128)(2,1)S(1)}, u32[]{:S(2)}, u32[]{:S(2)}) collective-permute-start(bf16[96,384]{1,0:T(8,128)(2,1)S(1)} %get-tuple-element.22.edge_ref), channel_id=1, source_target_pairs={{1,0},{2,1},{3,2},{4,3},{5,4},{6,5},{7,6},{0,7},{9,8},{10,9},{11,1... | collective-permute-start | bytes 221192 | tf_op jit(solution)/shard_map/ppermute | solution.py:498
  16.6 6.2 %collective-permute-start = (bf16[96,384]{1,0:T(8,128)(2,1)S(1)}, bf16[96,384]{1,0:T(8,128)(2,1)S(1)}, u32[]{:S(2)}, u32[]{:S(2)}) collective-permute-start(bf16[96,384]{1,0:T(8,128)(2,1)S(1)} %get-tuple-element.22.edge_ref), channel_id=1, source_target_pairs={{0,1},{1,2},{2,3},{3,4},{4,5},{5,6},{6,7},{7,0},{8,9},{9,10},{10,1... | collective-permute-start | bytes 221192 | tf_op jit(solution)/shard_map/ppermute | solution.py:497
  16.6 20.0 %collective-permute-start.2 = (bf16[5,32,256]{2,1,0:T(8,128)(2,1)S(1)}, bf16[5,32,256]{2,1,0:T(8,128)(2,1)S(1)}, u32[]{:S(2)}, u32[]{:S(2)}) collective-permute-start(bf16[5,32,256]{2,1,0:T(8,128)(2,1)S(1)} %get-tuple-element.30), channel_id=1, source_target_pairs={{0,8},{8,0},{16,24},{24,16},{1,9},{9,1},{17,25},{25,17},{2,10},{10... | collective-permute-start | bytes 245768 | tf_op jit(solution)/shard_map/ppermute | solution.py:509
  18.1 18.5 %collective-permute-start.3 = (bf16[5,32,256]{2,1,0:T(8,128)(2,1)S(1)}, bf16[5,32,256]{2,1,0:T(8,128)(2,1)S(1)}, u32[]{:S(2)}, u32[]{:S(2)}) collective-permute-start(bf16[5,32,256]{2,1,0:T(8,128)(2,1)S(1)} %get-tuple-element.31), channel_id=1, source_target_pairs={{0,0},{8,16},{16,8},{24,24},{1,1},{9,17},{17,9},{25,25},{2,2},{10,... | collective-permute-start | bytes 245768 | tf_op jit(solution)/shard_map/ppermute | solution.py:509
  31.9 4.7 %collective-permute-start.4 = (bf16[96,256]{1,0:T(8,128)(2,1)S(1)}, bf16[96,256]{1,0:T(8,128)(2,1)S(1)}, u32[]{:S(2)}, u32[]{:S(2)}) collective-permute-start(bf16[96,256]{1,0:T(8,128)(2,1)S(1)} %get-tuple-element.32), channel_id=1, source_target_pairs={{0,8},{8,0},{16,24},{24,16},{1,9},{9,1},{17,25},{25,17},{2,10},{10... | collective-permute-start | bytes 147464 | tf_op jit(solution)/shard_map/ppermute | solution.py:509
  33.0 3.6 %collective-permute-start.5 = (bf16[96,256]{1,0:T(8,128)(2,1)S(1)}, bf16[96,256]{1,0:T(8,128)(2,1)S(1)}, u32[]{:S(2)}, u32[]{:S(2)}) collective-permute-start(bf16[96,256]{1,0:T(8,128)(2,1)S(1)} %get-tuple-element.33), channel_id=1, source_target_pairs={{0,0},{8,16},{16,8},{24,24},{1,1},{9,17},{17,9},{25,25},{2,2},{10,... | collective-permute-start | bytes 147464 | tf_op jit(solution)/shard_map/ppermute | solution.py:509
